TPU v7x, 32 devices: a whole 2x2x4 slice. The times are simulated.
32 devices in a mesh: fsdp: 2 (over x), context: 16 (over z, y, core).
Axes of the slice: x: 2, y: 2, z: 4, core: 2. Of those that a mesh axis runs over, the one named last changes fastest.
Arguments:
- tokens: bfloat16 [2, 2048, 1600], P('fsdp', 'context'), may hold values from -6 to 6
- cotangent: bfloat16 [2, 2048, 1600], P('fsdp', 'context'), may hold values from -6 to 6
- block_order: int32 [32], replicated, may hold values from 0 to 31, each once
- ln1_gain: bfloat16 [1600], P('fsdp'), may hold values from 0.5 to 1.5
- ln1_bias: bfloat16 [1600], P('fsdp'), may hold values from -3 to 3
- w_qkv: bfloat16 [1600, 4800], P('context', 'fsdp'), may hold values from -5.05 to 5.05
- qv_bias: bfloat16 [1600, 2], P('fsdp'), may hold values from -0.29882812 to 0.29882812
- w_out: bfloat16 [1600, 1600], P('context', 'fsdp'), may hold values from -0.875 to 0.875
- out_bias: bfloat16 [1600], P('fsdp'), may hold values from -3 to 3
- ln2_gain: bfloat16 [1600], P('fsdp'), may hold values from 0.5 to 1.5
- ln2_bias: bfloat16 [1600], P('fsdp'), may hold values from -3 to 3
- w_fc: bfloat16 [1600, 6400], P('context', 'fsdp'), may hold values from -0.15625 to 0.15625
- fc_bias: bfloat16 [6400], P('fsdp'), may hold values from -3 to 3
- w_proj: bfloat16 [6400, 1600], P('context', 'fsdp'), may hold values from -0.078125 to 0.078125
- proj_bias: bfloat16 [1600], P('fsdp'), may hold values from -3 to 3
Outputs:
- out: bfloat16 [2, 2048, 1600], P('fsdp', 'context')
- d_tokens: bfloat16 [2, 2048, 1600], P('fsdp', 'context')
- g_ln1_gain: float32 [1600], P('fsdp')
- g_ln1_bias: float32 [1600], P('fsdp')
- g_w_qkv: float32 [1600, 4800], P('context', 'fsdp')
- g_qv_bias: float32 [1600, 2], P('fsdp')
- g_w_out: float32 [1600, 1600], P('context', 'fsdp')
- g_out_bias: float32 [1600], P('fsdp')
- g_ln2_gain: float32 [1600], P('fsdp')
- g_ln2_bias: float32 [1600], P('fsdp')
- g_w_fc: float32 [1600, 6400], P('context', 'fsdp')
- g_fc_bias: float32 [6400], P('fsdp')
- g_w_proj: float32 [6400, 1600], P('context', 'fsdp')
- g_proj_bias: float32 [1600], P('fsdp')
Inputs may be any that keep to these rules, and one draw needn't show every extreme that they name: block_order names each of the 32 blocks of positions once; rows s * 64 to s * 64 + 63 of a sequence hold positions block_order[s] * 64 onward, in order.
All inputs are finite; a program needn't handle non-finite values.
Results may differ from a plain program's by a relative error of at most 0.025.
Values may be sent and summed in bfloat16 or wider, within the bound.
No kernel may reach another device: no remote copies, remote signals or barrier semaphores. Data moves between devices by JAX's collectives and lax.ppermute only.
A program may use at most 576 MiB of HBM per device.

v0:
```python
import math

import jax
import jax.numpy as jnp
from jax import lax
from jax.sharding import PartitionSpec as P

HEADS = 25
HEAD_DIM = 64


EPSILON = 1e-05
GELU_ROOT = math.sqrt(2.0 / math.pi)
GELU_CUBIC = 0.044715
NEG_LARGE = -1e30


def normalize(values, gain_vec, bias_vec):
    centred = values - jnp.mean(values, axis=-1, keepdims=True)
    inv_std = lax.rsqrt(jnp.mean(centred * centred, axis=-1, keepdims=True) + EPSILON)
    normed = centred * inv_std
    return (normed * gain_vec.astype(jnp.float32) + bias_vec.astype(jnp.float32), normed, inv_std)


def norm_back(upstream, normed, inv_std, gain_vec):
    scaled = upstream * gain_vec.astype(jnp.float32)
    return inv_std * (
        scaled
        - jnp.mean(scaled, axis=-1, keepdims=True)
        - normed * jnp.mean(scaled * normed, axis=-1, keepdims=True)
    )


def gelu_pair(pre_act):
    inner = GELU_ROOT * (pre_act + GELU_CUBIC * pre_act * pre_act * pre_act)
    tangent = jnp.tanh(inner)
    act_value = 0.5 * pre_act * (1.0 + tangent)
    act_slope = 0.5 * (1.0 + tangent) + 0.5 * pre_act * (1.0 - tangent * tangent) * GELU_ROOT * (
        1.0 + 3.0 * GELU_CUBIC * pre_act * pre_act
    )
    return (act_value, act_slope)


def positions_of(block_order, block_len):
    offsets = jnp.arange(block_len, dtype=jnp.int32)
    return (block_order[:, None] * block_len + offsets[None, :]).reshape(-1)


def gather_rows(first, second):
    return (
        lax.all_gather(first, "context", axis=0, tiled=True),
        lax.all_gather(second, "context", axis=0, tiled=True),
    )


def gather_cols(first, second, vec_a, vec_b, vec_c, vec_d):
    return (
        lax.all_gather(first, "fsdp", axis=1, tiled=True),
        lax.all_gather(second, "fsdp", axis=1, tiled=True),
        lax.all_gather(vec_a, "fsdp", axis=0, tiled=True),
        lax.all_gather(vec_b, "fsdp", axis=0, tiled=True),
        lax.all_gather(vec_c, "fsdp", axis=0, tiled=True),
        lax.all_gather(vec_d, "fsdp", axis=0, tiled=True),
    )


def fetch(first, second, vec_a, vec_b, vec_c, vec_d):
    cols = gather_cols(first, second, vec_a, vec_b, vec_c, vec_d)
    rows = gather_rows(cols[0], cols[1])
    return (rows[0], rows[1], cols[2], cols[3], cols[4], cols[5])


def scatter_rows(first, second):
    return (
        lax.psum_scatter(first, "context", scatter_dimension=0, tiled=True),
        lax.psum_scatter(second, "context", scatter_dimension=0, tiled=True),
    )


def scatter_cols(first, second, vec_a, vec_b, vec_c, vec_d):
    return (
        lax.psum_scatter(
            first.astype(jnp.bfloat16), "fsdp", scatter_dimension=1, tiled=True
        ).astype(jnp.float32),
        lax.psum_scatter(
            second.astype(jnp.bfloat16), "fsdp", scatter_dimension=1, tiled=True
        ).astype(jnp.float32),
        lax.psum_scatter(
            vec_a.astype(jnp.bfloat16), "fsdp", scatter_dimension=0, tiled=True
        ).astype(jnp.float32),
        lax.psum_scatter(
            vec_b.astype(jnp.bfloat16), "fsdp", scatter_dimension=0, tiled=True
        ).astype(jnp.float32),
        lax.psum_scatter(
            vec_c.astype(jnp.bfloat16), "fsdp", scatter_dimension=0, tiled=True
        ).astype(jnp.float32),
        lax.psum_scatter(
            vec_d.astype(jnp.bfloat16), "fsdp", scatter_dimension=0, tiled=True
        ).astype(jnp.float32),
    )


def send_grads(first, second, vec_a, vec_b, vec_c, vec_d):
    rows = scatter_rows(first, second)
    return scatter_cols(rows[0], rows[1], vec_a, vec_b, vec_c, vec_d)


def attend_forward(query_heads, keys_all, values_all, query_pos, key_pos):
    length = keys_all.shape[0]
    rows_here = query_heads.shape[0]
    kblock = math.gcd(length, 512)
    nblocks = length // kblock
    score_scale = HEAD_DIM ** (-0.5)
    key_blocks = keys_all.reshape(nblocks, kblock, HEADS, HEAD_DIM)
    value_blocks = values_all.reshape(nblocks, kblock, HEADS, HEAD_DIM)
    pos_blocks = key_pos.reshape(nblocks, kblock)

    def step(carry, inputs):
        maxima, totals, accum = carry
        block_keys, block_values, block_pos = inputs
        scores = (
            jnp.einsum("qhd,khd->hqk", query_heads, block_keys, preferred_element_type=jnp.float32)
            * score_scale
        )
        allowed = (query_pos[:, None] >= block_pos[None, :])[None]
        fresh = jnp.maximum(maxima, jnp.max(jnp.where(allowed, scores, NEG_LARGE), axis=-1))
        exp_terms = jnp.where(allowed, jnp.exp(scores - fresh[..., None]), 0.0)
        decay_factor = jnp.exp(maxima - fresh)
        totals = totals * decay_factor + jnp.sum(exp_terms, axis=-1)
        accum = accum * decay_factor[..., None] + jnp.einsum(
            "hqk,khd->hqd",
            exp_terms.astype(jnp.bfloat16),
            block_values,
            preferred_element_type=jnp.float32,
        )
        return ((fresh, totals, accum), None)

    start_carry = (
        jnp.full((HEADS, rows_here), NEG_LARGE, jnp.float32),
        jnp.zeros((HEADS, rows_here), jnp.float32),
        jnp.zeros((HEADS, rows_here, HEAD_DIM), jnp.float32),
    )
    (maxima, totals, accum), _ = lax.scan(step, start_carry, (key_blocks, value_blocks, pos_blocks))
    attn_out = (accum / totals[..., None]).transpose(1, 0, 2).reshape(rows_here, HEADS * HEAD_DIM)
    return (attn_out.astype(jnp.bfloat16), maxima + jnp.log(totals))


def block_terms(
    query_heads, grad_heads, row_dot, log_norm, query_pos, block_keys, block_values, block_pos
):
    score_scale = HEAD_DIM ** (-0.5)
    scores = (
        jnp.einsum("qhd,khd->hqk", query_heads, block_keys, preferred_element_type=jnp.float32)
        * score_scale
    )
    allowed = (query_pos[:, None] >= block_pos[None, :])[None]
    prob_full = jnp.where(allowed, jnp.exp(scores - log_norm[..., None]), 0.0)
    prob_half = prob_full.astype(jnp.bfloat16)
    value_grad = jnp.einsum(
        "hqk,qhd->khd", prob_half, grad_heads, preferred_element_type=jnp.float32
    )
    dprob = jnp.einsum("qhd,khd->hqk", grad_heads, block_values, preferred_element_type=jnp.float32)
    dscore = (score_scale * prob_full * (dprob - row_dot[..., None])).astype(jnp.bfloat16)
    query_grad = jnp.einsum("hqk,khd->qhd", dscore, block_keys, preferred_element_type=jnp.float32)
    key_grad = jnp.einsum("hqk,qhd->khd", dscore, query_heads, preferred_element_type=jnp.float32)
    return (query_grad, key_grad, value_grad)


def attend_backward(
    query_heads, keys_all, values_all, query_pos, key_pos, log_norm, grad_o16, attn_out
):
    length = keys_all.shape[0]
    rows_here = query_heads.shape[0]
    width = HEADS * HEAD_DIM
    kblock = math.gcd(length, 512)
    nblocks = length // kblock
    grad_heads = grad_o16.reshape(rows_here, HEADS, HEAD_DIM)
    row_dot = jnp.sum(
        grad_o16.astype(jnp.float32).reshape(rows_here, HEADS, HEAD_DIM)
        * attn_out.astype(jnp.float32).reshape(rows_here, HEADS, HEAD_DIM),
        axis=-1,
    ).T
    key_blocks = keys_all.reshape(nblocks, kblock, HEADS, HEAD_DIM)
    value_blocks = values_all.reshape(nblocks, kblock, HEADS, HEAD_DIM)
    pos_blocks = key_pos.reshape(nblocks, kblock)
    start_grad = jnp.zeros((rows_here, HEADS, HEAD_DIM), jnp.float32)

    def step_whole(carry, inputs):
        query_grad, key_grad, value_grad = block_terms(
            query_heads, grad_heads, row_dot, log_norm, query_pos, inputs[0], inputs[1], inputs[2]
        )
        return (carry + query_grad, (key_grad, value_grad))

    query_total, (key_parts, value_parts) = lax.scan(
        step_whole, start_grad, (key_blocks, value_blocks, pos_blocks)
    )
    term = jnp.concatenate(
        [key_parts.reshape(length, width), value_parts.reshape(length, width)], axis=1
    )
    owned = lax.psum_scatter(term, "context", scatter_dimension=0, tiled=True)
    key_owned, value_owned = (owned[:, :width], owned[:, width:])
    return (query_total.reshape(rows_here, width), key_owned, value_owned)


def body(
    tokens,
    cotangent,
    block_order,
    ln1_gain,
    ln1_bias,
    w_qkv,
    qv_bias,
    w_out,
    out_bias,
    ln2_gain,
    ln2_bias,
    w_fc,
    fc_bias,
    w_proj,
    proj_bias,
):
    width = HEADS * HEAD_DIM
    rows_here = tokens.shape[1]
    block_len = rows_here // 2
    grad_scale = 1.0 / math.sqrt(lax.axis_size("fsdp") * lax.axis_size("context") * rows_here)
    key_pos = positions_of(block_order, block_len)
    query_pos = lax.dynamic_slice_in_dim(key_pos, lax.axis_index("context") * rows_here, rows_here)
    w_qkv_all, w_out_all, gain_one, shift_one, qv_all, out_b = fetch(
        w_qkv, w_out, ln1_gain, ln1_bias, qv_bias, out_bias
    )
    w_fc_all, w_proj_all, gain_two, shift_two, fc_b, proj_b = fetch(
        w_fc, w_proj, ln2_gain, ln2_bias, fc_bias, proj_bias
    )
    xs = tokens[0].astype(jnp.float32)
    h_one, normed_one, inv_one = normalize(xs, gain_one, shift_one)
    h_one = h_one.astype(jnp.bfloat16)
    qkv = jnp.dot(h_one, w_qkv_all, preferred_element_type=jnp.float32)
    queries = (qkv[:, :width] + qv_all[:, 0].astype(jnp.float32)).astype(jnp.bfloat16)
    key_rows = qkv[:, width : 2 * width].astype(jnp.bfloat16)
    value_rows = (qkv[:, 2 * width :] + qv_all[:, 1].astype(jnp.float32)).astype(jnp.bfloat16)
    keys_all, values_all = (
        lax.all_gather(key_rows, "context", axis=0, tiled=True),
        lax.all_gather(value_rows, "context", axis=0, tiled=True),
    )
    query_heads = queries.reshape(rows_here, HEADS, HEAD_DIM)
    attn_out, log_norm = attend_forward(query_heads, keys_all, values_all, query_pos, key_pos)
    resid_one = (
        xs
        + jnp.dot(attn_out, w_out_all, preferred_element_type=jnp.float32)
        + out_b.astype(jnp.float32)
    )
    h_two, normed_two, inv_two = normalize(resid_one, gain_two, shift_two)
    h_two = h_two.astype(jnp.bfloat16)
    pre_act = jnp.dot(h_two, w_fc_all, preferred_element_type=jnp.float32) + fc_b.astype(
        jnp.float32
    )
    act_value, act_slope = gelu_pair(pre_act)
    act_half = act_value.astype(jnp.bfloat16)
    result = (
        resid_one
        + jnp.dot(act_half, w_proj_all, preferred_element_type=jnp.float32)
        + proj_b.astype(jnp.float32)
    )
    cot_rows = cotangent[0]
    grad_y = cot_rows.astype(jnp.float32)
    g_w_proj = jnp.dot(act_half.T, cot_rows, preferred_element_type=jnp.float32) * grad_scale
    g_proj_bias = jnp.sum(grad_y, axis=0) * grad_scale
    grad_pre = jnp.dot(cot_rows, w_proj_all.T, preferred_element_type=jnp.float32) * act_slope
    g_fc_bias = jnp.sum(grad_pre, axis=0) * grad_scale
    grad_pre16 = grad_pre.astype(jnp.bfloat16)
    g_w_fc = jnp.dot(h_two.T, grad_pre16, preferred_element_type=jnp.float32) * grad_scale
    grad_h2 = jnp.dot(grad_pre16, w_fc_all.T, preferred_element_type=jnp.float32)
    g_ln2_gain = jnp.sum(grad_h2 * normed_two, axis=0) * grad_scale
    g_ln2_bias = jnp.sum(grad_h2, axis=0) * grad_scale
    mlp_grads = send_grads(g_w_fc, g_w_proj, g_ln2_gain, g_ln2_bias, g_fc_bias, g_proj_bias)
    grad_r1 = grad_y + norm_back(grad_h2, normed_two, inv_two, gain_two)
    g_out_bias = jnp.sum(grad_r1, axis=0) * grad_scale
    grad_r16 = grad_r1.astype(jnp.bfloat16)
    g_w_out = jnp.dot(attn_out.T, grad_r16, preferred_element_type=jnp.float32) * grad_scale
    grad_o16 = jnp.dot(grad_r16, w_out_all.T, preferred_element_type=jnp.float32).astype(
        jnp.bfloat16
    )
    grad_q, grad_k, grad_v = attend_backward(
        query_heads, keys_all, values_all, query_pos, key_pos, log_norm, grad_o16, attn_out
    )
    g_qv_bias = jnp.stack([jnp.sum(grad_q, axis=0), jnp.sum(grad_v, axis=0)], axis=1) * grad_scale
    grad_qkv16 = jnp.concatenate([grad_q, grad_k, grad_v], axis=1).astype(jnp.bfloat16)
    g_w_qkv = jnp.dot(h_one.T, grad_qkv16, preferred_element_type=jnp.float32) * grad_scale
    grad_h1 = jnp.dot(grad_qkv16, w_qkv_all.T, preferred_element_type=jnp.float32)
    g_ln1_gain = jnp.sum(grad_h1 * normed_one, axis=0) * grad_scale
    g_ln1_bias = jnp.sum(grad_h1, axis=0) * grad_scale
    grad_x = (grad_r1 + norm_back(grad_h1, normed_one, inv_one, gain_one)).astype(jnp.bfloat16)
    attn_grads = send_grads(g_w_qkv, g_w_out, g_ln1_gain, g_ln1_bias, g_qv_bias, g_out_bias)
    summed = lax.psum(
        (
            attn_grads[2],
            attn_grads[3],
            attn_grads[4],
            attn_grads[5],
            mlp_grads[2],
            mlp_grads[3],
            mlp_grads[4],
            mlp_grads[5],
        ),
        "context",
    )
    return (
        result.astype(jnp.bfloat16)[None],
        grad_x[None],
        summed[0],
        summed[1],
        attn_grads[0],
        summed[2],
        attn_grads[1],
        summed[3],
        summed[4],
        summed[5],
        mlp_grads[0],
        summed[6],
        mlp_grads[1],
        summed[7],
    )


def solution(mesh):
    placed = (
        P("fsdp", "context", None),
        P("fsdp", "context", None),
        P(),
        P("fsdp"),
        P("fsdp"),
        P("context", "fsdp"),
        P("fsdp", None),
        P("context", "fsdp"),
        P("fsdp"),
        P("fsdp"),
        P("fsdp"),
        P("context", "fsdp"),
        P("fsdp"),
        P("context", "fsdp"),
        P("fsdp"),
    )
    return jax.shard_map(
        body,
        mesh=mesh,
        in_specs=placed,
        out_specs=(
            P("fsdp", "context", None),
            P("fsdp", "context", None),
            P("fsdp"),
            P("fsdp"),
            P("context", "fsdp"),
            P("fsdp", None),
            P("context", "fsdp"),
            P("fsdp"),
            P("fsdp"),
            P("fsdp"),
            P("context", "fsdp"),
            P("fsdp"),
            P("context", "fsdp"),
            P("fsdp"),
        ),
        check_vma=False,
    )
```

profile of v0, /device:TPU:0, one launch (start us, length us, event | category | flops | bytes accessed | tf_op | source)
XLA Modules:
  0.0 2697.7 jit_solution(1883228032706122756)
XLA Ops:
  8.0 18.5 all-gather
  29.9 11.2 all-gather.3
  45.6 8.7 all-reduce.21
  59.3 110.0 %all-gather.25.cloned.1.call-done = bf16[16,100,4800]{2,1,0:T(8,128)(2,1)} async-done(((bf16[1,100,4800]{2,1,0:T(8,128)(2,1)}), bf16[16,100,4800]{2,1,0:T(8,128)(2,1)}) %all-gather.25.cloned.1.call-update) | async-done | bytes 15360016 | tf_op jit(solution)/shard_map/all_gather | solution.py:51
  169.4 16.1 reshape.225
  185.5 12.2 fusion.101
  212.7 42.3 %all-gather.27.cloned.1.call-done = bf16[16,100,1600]{2,1,0:T(8,128)(2,1)} async-done(((bf16[1,100,1600]{2,1,0:T(8,128)(2,1)}), bf16[16,100,1600]{2,1,0:T(8,128)(2,1)}) %all-gather.27.cloned.1.call-update) | async-done | bytes 5120016 | tf_op jit(solution)/shard_map/all_gather | solution.py:52
  255.0 8.2 reshape.231
  263.2 102.2 %all-gather.29.cloned.1.call-done = bf16[16,100,6400]{2,1,0:T(8,128)(2,1)} async-done(((bf16[1,100,6400]{2,1,0:T(8,128)(2,1)}), bf16[16,100,6400]{2,1,0:T(8,128)(2,1)}) %all-gather.29.cloned.1.call-update) | async-done | bytes 20480016 | tf_op jit(solution)/shard_map/all_gather | solution.py:51
  365.4 17.2 reshape.233
  382.7 52.6 %all-gather.19.cloned.1.call-done = bf16[2048,1600]{0,1:T(8,128)(2,1)} async-done(((bf16[128,1600]{0,1:T(8,128)(2,1)}), bf16[2048,1600]{0,1:T(8,128)(2,1)}) %all-gather.19.cloned.1.call-update) | async-done | bytes 6553616 | tf_op jit(solution)/shard_map/all_gather | solution.py:243
  435.2 14.5 reshape.196
  449.7 7.2 copy.59
  456.9 46.5 %all-gather.17.cloned.1.call-done = bf16[2048,1600]{0,1:T(8,128)(2,1)} async-done(((bf16[128,1600]{0,1:T(8,128)(2,1)}), bf16[2048,1600]{0,1:T(8,128)(2,1)}) %all-gather.17.cloned.1.call-update) | async-done | bytes 6553616 | tf_op jit(solution)/shard_map/all_gather | solution.py:242
  503.4 14.5 reshape.194
  517.9 7.2 copy.58
  525.1 31.6 %while.30 = (s32[]{:T(128)}, f32[25,128]{1,0:T(8,128)S(1)}, f32[25,128]{1,0:T(8,128)S(1)}, f32[25,128,64]{1,2,0:T(8,128)S(1)}, s32[128]{0:T(128)S(1)}, /*index=5...) while((s32[]{:T(128)}, f32[25,128]{1,0:T(8,128)S(1)}, ...), condition=%wide.region_5.6_spmd.clone, body=%wide.region_2.5_spmd.clone.sunk | while | flops 438148736 | bytes 25459340 | solution.py:143
  562.1 12.4 convolution_add_fusion
  574.5 39.6 %all-gather.23.cloned.1.call-done = bf16[6400,1600]{1,0:T(8,128)(2,1)} async-done(((bf16[400,1600]{1,0:T(8,128)(2,1)}), bf16[6400,1600]{1,0:T(8,128)(2,1)}) %all-gather.23.cloned.1.call-update) | async-done | bytes 20480016 | tf_op jit(solution)/shard_map/all_gather | solution.py:52
  614.2 11.8 fusion.108
  626.0 12.7 multiply_reduce_fusion
  646.3 598.5 %while.31 = (s32[]{:T(128)}, f32[128,25,64]{0,2,1:T(8,128)}, f32[4,512,25,64]{1,0,3,2:T(4,128)}, f32[4,512,25,64]{1,0,3,2:T(4,128)}, bf16[4,512,25,64]{1,3,2,0:T...) while((s32[]{:T(128)}, f32[128,25,64]{0,2,1:T(8,128)}, ...), condition=%wide.region_12.13_spmd.clone, body=%wide.region_11.12_spmd.clone.sunk | while | flops 1067073536 | bytes 77246696 | solution.py:194
  669.9 63.3 %dynamic_update_slice.11 = f32[4,512,25,64]{1,0,3,2:T(4,128)} dynamic-update-slice(f32[4,512,25,64]{1,0,3,2:T(4,128)} %get-tuple-element.552, f32[1,512,25,64]{1,0,3,2:T(1,128)} %copy.106, s32[]{:T(128)S(6)} %copy.132, s32[]{:T(128)} %constant.28.clone.1..sunk.1, s32[]{:T(128)} %constant.28.clone.1..sunk.1, s32[]{:T(128)} %constant.28.clone.1..sunk.1) | dynamic-update-slice | bytes 6553604 | tf_op jit(solution)/shard_map/while/body/jit(dynamic_update_index_in_dim)/dynamic_update_slice | solution.py:194
  733.2 63.0 %dynamic_update_slice.12 = f32[4,512,25,64]{1,0,3,2:T(4,128)} dynamic-update-slice(f32[4,512,25,64]{1,0,3,2:T(4,128)} %get-tuple-element.553, f32[1,512,25,64]{1,0,3,2:T(1,128)S(1)} %copy.107, s32[]{:T(128)S(6)} %copy.132, s32[]{:T(128)} %constant.28.clone.1..sunk.1, s32[]{:T(128)} %constant.28.clone.1..sunk.1, s32[]{:T(128)} %constant.28.clone.1..sunk.1) | dynamic-update-slice | bytes 6553604 | tf_op jit(solution)/shard_map/while/body/jit(dynamic_update_index_in_dim)/dynamic_update_slice | solution.py:194
  819.4 63.3 %dynamic_update_slice.11 = f32[4,512,25,64]{1,0,3,2:T(4,128)} dynamic-update-slice(f32[4,512,25,64]{1,0,3,2:T(4,128)} %get-tuple-element.552, f32[1,512,25,64]{1,0,3,2:T(1,128)} %copy.106, s32[]{:T(128)S(6)} %copy.132, s32[]{:T(128)} %constant.28.clone.1..sunk.1, s32[]{:T(128)} %constant.28.clone.1..sunk.1, s32[]{:T(128)} %constant.28.clone.1..sunk.1) | dynamic-update-slice | bytes 6553604 | tf_op jit(solution)/shard_map/while/body/jit(dynamic_update_index_in_dim)/dynamic_update_slice | solution.py:194
  882.7 63.0 %dynamic_update_slice.12 = f32[4,512,25,64]{1,0,3,2:T(4,128)} dynamic-update-slice(f32[4,512,25,64]{1,0,3,2:T(4,128)} %get-tuple-element.553, f32[1,512,25,64]{1,0,3,2:T(1,128)S(1)} %copy.107, s32[]{:T(128)S(6)} %copy.132, s32[]{:T(128)} %constant.28.clone.1..sunk.1, s32[]{:T(128)} %constant.28.clone.1..sunk.1, s32[]{:T(128)} %constant.28.clone.1..sunk.1) | dynamic-update-slice | bytes 6553604 | tf_op jit(solution)/shard_map/while/body/jit(dynamic_update_index_in_dim)/dynamic_update_slice | solution.py:194
  968.9 63.3 %dynamic_update_slice.11 = f32[4,512,25,64]{1,0,3,2:T(4,128)} dynamic-update-slice(f32[4,512,25,64]{1,0,3,2:T(4,128)} %get-tuple-element.552, f32[1,512,25,64]{1,0,3,2:T(1,128)} %copy.106, s32[]{:T(128)S(6)} %copy.132, s32[]{:T(128)} %constant.28.clone.1..sunk.1, s32[]{:T(128)} %constant.28.clone.1..sunk.1, s32[]{:T(128)} %constant.28.clone.1..sunk.1) | dynamic-update-slice | bytes 6553604 | tf_op jit(solution)/shard_map/while/body/jit(dynamic_update_index_in_dim)/dynamic_update_slice | solution.py:194
  1032.1 63.0 %dynamic_update_slice.12 = f32[4,512,25,64]{1,0,3,2:T(4,128)} dynamic-update-slice(f32[4,512,25,64]{1,0,3,2:T(4,128)} %get-tuple-element.553, f32[1,512,25,64]{1,0,3,2:T(1,128)S(1)} %copy.107, s32[]{:T(128)S(6)} %copy.132, s32[]{:T(128)} %constant.28.clone.1..sunk.1, s32[]{:T(128)} %constant.28.clone.1..sunk.1, s32[]{:T(128)} %constant.28.clone.1..sunk.1) | dynamic-update-slice | bytes 6553604 | tf_op jit(solution)/shard_map/while/body/jit(dynamic_update_index_in_dim)/dynamic_update_slice | solution.py:194
  1118.3 63.3 %dynamic_update_slice.11 = f32[4,512,25,64]{1,0,3,2:T(4,128)} dynamic-update-slice(f32[4,512,25,64]{1,0,3,2:T(4,128)} %get-tuple-element.552, f32[1,512,25,64]{1,0,3,2:T(1,128)} %copy.106, s32[]{:T(128)S(6)} %copy.132, s32[]{:T(128)} %constant.28.clone.1..sunk.1, s32[]{:T(128)} %constant.28.clone.1..sunk.1, s32[]{:T(128)} %constant.28.clone.1..sunk.1) | dynamic-update-slice | bytes 6553604 | tf_op jit(solution)/shard_map/while/body/jit(dynamic_update_index_in_dim)/dynamic_update_slice | solution.py:194
  1181.6 63.0 %dynamic_update_slice.12 = f32[4,512,25,64]{1,0,3,2:T(4,128)} dynamic-update-slice(f32[4,512,25,64]{1,0,3,2:T(4,128)} %get-tuple-element.553, f32[1,512,25,64]{1,0,3,2:T(1,128)S(1)} %copy.107, s32[]{:T(128)S(6)} %copy.132, s32[]{:T(128)} %constant.28.clone.1..sunk.1, s32[]{:T(128)} %constant.28.clone.1..sunk.1, s32[]{:T(128)} %constant.28.clone.1..sunk.1) | dynamic-update-slice | bytes 6553604 | tf_op jit(solution)/shard_map/while/body/jit(dynamic_update_index_in_dim)/dynamic_update_slice | solution.py:194
  1244.8 15.9 copy.103
  1260.7 16.2 copy.102
  1276.9 19.0 pad_maximum_fusion
  1297.6 26.2 convolution_multiply_fusion
  1323.8 507.8 %fusion.2 = f32[104,6400]{1,0:T(8,128)S(1)} fusion(f32[1600,6400]{1,0:T(8,128)} %convolution_multiply_fusion), kind=kCustom, calls=%all-reduce-scatter.2 | all-reduce-scatter fusion | flops 10649601 | bytes 43622912
  1832.6 29.2 %collective-permute-start.3 = (bf16[60,6400]{1,0:T(8,128)(2,1)}, bf16[60,6400]{1,0:T(8,128)(2,1)}, u32[]{:S(2)}, u32[]{:S(2)}) collective-permute-start(bf16[60,6400]{1,0:T(8,128)(2,1)} %slice.35), channel_id=1, source_target_pairs={{0,1},{1,2},{2,3},{3,4},{4,5},{5,6},{6,7},{7,8},{8,9},{9,10},{10,1... | collective-permute-start | bytes 2304008
  1863.3 12.3 concatenate.12
  1879.1 18.5 convolution_multiply_fusion.1
  1901.0 5.5 convolution_multiply_fusion.3
  1909.0 12.7 convolution_multiply_fusion.2
  1921.7 591.9 %fusion.103 = (f32[104,4800]{1,0:T(8,128)}, f32[112,1600]{1,0:T(8,128)S(1)}) fusion(f32[1600,4800]{1,0:T(8,128)} %convolution_multiply_fusion.2, f32[1600,1600]{1,0:T(8,128)} %convolution_multiply_fusion.3), kind=kCustom, calls=%all-reduce-scatter.3 | all-reduce-scatter fusion | flops 10854402 | bytes 43674112
  2514.4 28.0 %collective-permute-start.1 = (bf16[112,1600]{1,0:T(8,128)(2,1)}, bf16[112,1600]{1,0:T(8,128)(2,1)S(1)}, u32[]{:S(2)}, u32[]{:S(2)}) collective-permute-start(bf16[112,1600]{1,0:T(8,128)(2,1)} %convert.26), channel_id=1, source_target_pairs={{0,1},{1,2},{2,3},{3,4},{4,5},{5,6},{6,7},{7,8},{8,9},{9,10},{10,1... | collective-permute-start | bytes 1075208
  2554.4 7.2 concatenate.11
  2566.5 11.6 concatenate.10
  2581.2 9.3 fusion.82
  2590.6 9.6 all-reduce.20
  2608.5 14.7 fusion.67
  2624.2 59.8 %all-reduce.19 = (f32[800]{0:T(1024)}, f32[800]{0:T(1024)}, f32[800,2]{0,1:T(2,128)}, f32[800]{0:T(1024)}, f32[800]{0:T(1024)}, /*index=5*/f32[800]{0:T(1024)}, f32[3200]{0:T(1024)}, f32[800]{0:T(1024)}) all-reduce(f32[800]{0:T(1024)S(1)} %dynamic-slice_convert_fusion.9, ...), channel_id=1, replica_groups=mesh['fsdp'=2,'context'=16] {'context'}, use_global_device_ids=true, to_apply=%region_18.19 | all-reduce | flops 9600 | bytes 73600 | tf_op jit(solution)/shard_map/psum | solution.py:294
  (325 shorter events, 211.6 us)
Async XLA Ops:
  7.2 35.4 %all-gather.21.cloned.1.call-start = ((), (), s32[]{:S(2)}) async-start(), calls=%async_computation.9 | async-start | bytes 1996800 | tf_op jit(solution)/shard_map/all_gather | solution.py:58
  7.9 161.5 %all-gather.25.cloned.1.call-start = ((), (), s32[]{:S(2)}) async-start(), calls=%async_computation.13 | async-start | bytes 17199104 | tf_op jit(solution)/shard_map/all_gather | solution.py:51
  8.0 21.9 copy-start.24
  27.2 15.9 copy-start.36
  27.2 17.2 copy-start.37
  27.2 17.4 copy-start.38
  27.2 17.6 copy-start.39
  27.3 17.9 copy-start.40
  27.3 18.1 copy-start.41
  27.3 27.1 %copy-start.35 = (bf16[800,2]{0,1:T(2,128)(2,1)S(1)}, bf16[800,2]{0,1:T(2,128)(2,1)}, u32[]{:S(2)}) copy-start(bf16[800,2]{0,1:T(2,128)(2,1)} %param.25) | copy-start | bytes 9604
  29.1 29.8 %copy-start.5 = (bf16[1,128,1600]{1,2,0:T(8,128)(2,1)S(1)}, bf16[1,128,1600]{1,2,0:T(8,128)(2,1)}, u32[]{:S(2)}) copy-start(bf16[1,128,1600]{1,2,0:T(8,128)(2,1)} %param.19) | copy-start | bytes 1228804
  29.1 173.6 %all-gather.31.cloned.1.call-start = ((), (), s32[]{:S(2)}) async-start(), calls=%async_computation.16 | async-start | bytes 2150400 | tf_op jit(solution)/shard_map/all_gather | solution.py:59
  29.8 225.1 %all-gather.27.cloned.1.call-start = ((), (), s32[]{:S(2)}) async-start(), calls=%async_computation.14 | async-start | bytes 5883904 | tf_op jit(solution)/shard_map/all_gather | solution.py:52
  42.5 323.0 %all-gather.29.cloned.1.call-start = ((), (), s32[]{:S(2)}) async-start(), calls=%async_computation.15 | async-start | bytes 22630400 | tf_op jit(solution)/shard_map/all_gather | solution.py:51
  43.1 392.2 %all-gather.19.cloned.1.call-start = ((), (), s32[]{:S(2)}) async-start(), calls=%async_computation.8 | async-start | bytes 6963200 | tf_op jit(solution)/shard_map/all_gather | solution.py:243
  54.3 131.2 %copy-start.20 = (f32[1600]{0:T(1024)}, f32[1600]{0:T(1024)S(1)}, u32[]{:S(2)}) copy-start(f32[1600]{0:T(1024)S(1)} %convert_element_type.185) | copy-start | bytes 19204
  58.8 126.7 %copy-start.18 = (f32[1600]{0:T(1024)}, f32[1600]{0:T(1024)S(1)}, u32[]{:S(2)}) copy-start(f32[1600]{0:T(1024)S(1)} %convert_element_type.184) | copy-start | bytes 19204
  59.1 126.4 %copy-start.30 = (f32[128]{0:T(128)}, f32[128]{0:T(128)S(1)}, u32[]{:S(2)}) copy-start(f32[128]{0:T(128)S(1)} %broadcast_multiply_fusion.5) | copy-start | bytes 1540
  59.3 126.2 %copy-start.32 = (f32[128]{0:T(128)}, f32[128]{0:T(128)S(1)}, u32[]{:S(2)}) copy-start(f32[128]{0:T(128)S(1)} %add_rsqrt_fusion.1) | copy-start | bytes 1540
  200.6 302.8 %all-gather.17.cloned.1.call-start = ((), (), s32[]{:S(2)}) async-start(), calls=%async_computation.7 | async-start | bytes 6963200 | tf_op jit(solution)/shard_map/all_gather | solution.py:242
  202.6 4.5 copy-start.44
  202.6 4.7 copy-start.34
  202.6 411.6 %all-gather.23.cloned.1.call-start = ((), (), s32[]{:S(2)}) async-start(), calls=%async_computation.10 | async-start | bytes 22630400 | tf_op jit(solution)/shard_map/all_gather | solution.py:52
  207.0 1699.5 %reduce-scatter.24.cloned.1.call-start = ((), (), s32[]{:S(2)}) async-start(), calls=%async_computation.11 | async-start | bytes 27852800 | tf_op jit(solution)/shard_map/reduce_scatter | solution.py:200
  207.3 354.8 %copy-start.22 = (f32[1600]{0:T(1024)}, f32[1600]{0:T(1024)S(1)}, u32[]{:S(2)}) copy-start(f32[1600]{0:T(1024)S(1)} %convert_element_type.198) | copy-start | bytes 19204
  556.8 5.0 copy-start.11
  561.8 76.9 %copy-start = (f32[128,1600]{0,1:T(8,128)}, f32[128,1600]{0,1:T(8,128)S(1)}, u32[]{:S(2)}) copy-start(f32[128,1600]{0,1:T(8,128)S(1)} %get-tuple-element.356) | copy-start | bytes 2457604
  562.1 52.1 %copy-start.14 = (bf16[1,128,1600]{1,2,0:T(8,128)(2,1)S(1)}, bf16[1,128,1600]{1,2,0:T(8,128)(2,1)}, u32[]{:S(2)}) copy-start(bf16[1,128,1600]{1,2,0:T(8,128)(2,1)} %param.20) | copy-start | bytes 1228804
  626.0 12.7 copy-start.9
  640.0 5.1 copy-start.7
  1295.9 1267.8 %reduce-scatter.34.cloned.1.call-start = ((), (), s32[]{:S(2)}) async-start(), calls=%async_computation.20 | async-start | bytes 2457600
  1323.8 538.1 %copy-start.43 = (u32[32]{0:T(128)S(1)}, u32[32]{0:T(128)}, u32[]{:S(2)}) copy-start(u32[32]{0:T(128)} %constant.134) | copy-start | bytes 388
  1832.6 30.6 %collective-permute-start.3 = (bf16[60,6400]{1,0:T(8,128)(2,1)}, bf16[60,6400]{1,0:T(8,128)(2,1)}, u32[]{:S(2)}, u32[]{:S(2)}) collective-permute-start(bf16[60,6400]{1,0:T(8,128)(2,1)} %slice.35), channel_id=1, source_target_pairs={{0,1},{1,2},{2,3},{3,4},{4,5},{5,6},{6,7},{7,8},{8,9},{9,10},{10,1... | collective-permute-start | bytes 2304008
  1879.0 721.6 %reduce-scatter.26.cloned.1.call-start = ((), (), s32[]{:S(2)}) async-start(), calls=%async_computation.12 | async-start | bytes 45260800 | tf_op jit(solution)/shard_map/reduce_scatter | solution.py:76
  1897.7 725.5 %reduce-scatter.30.cloned.1.call-start = ((), (), s32[]{:S(2)}) async-start(), calls=%async_computation.18 | async-start | bytes 614400
  1900.8 7.2 copy-start.16
  1901.0 7.9 copy-start.6
  1901.0 7.9 copy-start.19
  1901.0 7.9 copy-start.21
  1901.0 7.9 copy-start.31
  1901.0 7.9 copy-start.33
  2514.4 40.0 %collective-permute-start.1 = (bf16[112,1600]{1,0:T(8,128)(2,1)}, bf16[112,1600]{1,0:T(8,128)(2,1)S(1)}, u32[]{:S(2)}, u32[]{:S(2)}) collective-permute-start(bf16[112,1600]{1,0:T(8,128)(2,1)} %convert.26), channel_id=1, source_target_pairs={{0,1},{1,2},{2,3},{3,4},{4,5},{5,6},{6,7},{7,8},{8,9},{9,10},{10,1... | collective-permute-start | bytes 1075208
  2543.8 19.9 copy-start.25
  2543.9 10.5 collective-permute-start.2
  2551.0 15.4 collective-permute-start
  2554.3 129.7 %reduce-scatter.32.cloned.1.call-start = ((), (), s32[]{:S(2)}) async-start(), calls=%async_computation.19 | async-start | bytes 614400
  2563.7 122.2 %reduce-scatter.28.cloned.1.call-start = ((), (), s32[]{:S(2)}) async-start(), calls=%async_computation.17 | async-start | bytes 1843200
  2581.1 107.2 %reduce-scatter.36.cloned.1.call-start = ((), (), s32[]{:S(2)}) async-start(), calls=%async_computation.21 | async-start | bytes 2457600
  (22 other events, 60.9 us)
Sparse Core Ops, SparseCore 0:
  9.6 32.3 all-gather.20
  44.8 124.5 all-gather.24
  170.9 23.8 all-gather.30
  197.4 57.5 all-gather.26
  256.4 108.9 all-gather.28
  368.0 67.2 all-gather.18
  438.0 65.3 all-gather.16
  505.6 108.5 all-gather.22
  1296.0 427.5 reduce-scatter.23
  1879.2 37.8 reduce-scatter.33
  1921.9 617.4 reduce-scatter.25
  2554.4 11.3 reduce-scatter.29
  2568.7 13.3 reduce-scatter.31
  2584.2 23.3 reduce-scatter.27
  2609.7 26.7 reduce-scatter.35
where the time goes:
time: 2720 us; the launch traced here: 2700 us
  blocking collectives  1220 us (45%)
  local copies, waits for them, and re-layouts  727 us (27%)
  waiting for transfers between devices  396 us (15%)
  matrix products  229 us (8%)
  starting transfers between devices  65 us (2%)
  other arithmetic  44.6 us (2%)
    unnamed x4, blocking collectives  1120 us
    dynamic_update_slice x16, local copies, waits for them, and re-layouts, attend_backward(): lax.scan(step_whole, start_grad, (key_blocks, value_blocks, pos_blocks))  539 us
    all_gather x2, waiting for transfers between devices, gather_rows(): lax.all_gather(first, 'context', axis=0, tiled=True)  212 us
    unnamed x128, local copies, waits for them, and re-layouts  148 us
    all_gather x2, waiting for transfers between devices, gather_rows(): lax.all_gather(second, 'context', axis=0, tiled=True)  81.9 us
    unnamed x9, starting transfers between devices  64.6 us
    psum x1, blocking collectives, body(): lax.psum((attn_grads[2], attn_grads[3], attn_grads[4], attn_grads[5], mlp...  59.8 us
  transfers between devices with their start and end apart: 19, of which 7 were waited for; matrix products, arithmetic and copies ran while one was open for 52% of the time, Pallas kernels for 0%

commit v1 on v0

v1 whole, which is shorter than its diff:
```python
import functools
import math

import jax
import jax.numpy as jnp
from jax import lax
from jax.experimental import pallas as pl
from jax.experimental.pallas import tpu as pltpu
from jax.sharding import PartitionSpec as P

HEADS = 25
HEAD_DIM = 64
SLOT = 2 * HEAD_DIM

EPSILON = 1e-05
GELU_ROOT = math.sqrt(2.0 / math.pi)
GELU_CUBIC = 0.044715
NEG_LARGE = -1e30
SCALE = HEAD_DIM ** (-0.5)
VMEM_LIMIT = 56 * 1024 * 1024
F32 = jnp.float32
BF16 = jnp.bfloat16


def norm_stats(values):
    centred = values - jnp.mean(values, axis=-1, keepdims=True)
    inv_std = lax.rsqrt(jnp.mean(centred * centred, axis=-1, keepdims=True) + EPSILON)
    return centred * inv_std, inv_std


def norm_back(upstream, normed, inv_std, gain_vec):
    scaled = upstream * gain_vec
    return inv_std * (
        scaled
        - jnp.mean(scaled, axis=-1, keepdims=True)
        - normed * jnp.mean(scaled * normed, axis=-1, keepdims=True)
    )


def gelu_pair(pre_act):
    inner = GELU_ROOT * (pre_act + GELU_CUBIC * pre_act * pre_act * pre_act)
    tangent = jnp.tanh(inner)
    act_value = 0.5 * pre_act * (1.0 + tangent)
    act_slope = 0.5 * (1.0 + tangent) + 0.5 * pre_act * (1.0 - tangent * tangent) * GELU_ROOT * (
        1.0 + 3.0 * GELU_CUBIC * pre_act * pre_act
    )
    return (act_value, act_slope)


class Ring:
    def __init__(self, count):
        chips = count // 2
        self.count, self.size = count, chips
        self.mine = lax.axis_index("context")
        self.core = self.mine % 2
        chip = self.mine // 2
        if chips == 8:
            order = [0, 2, 4, 6, 7, 5, 3, 1]
            self.place = jnp.where(chip % 2 == 0, chip // 2, (15 - chip) // 2)
        else:
            order = list(range(chips))
            self.place = chip
        self.right = []
        self.left = []
        for i in range(chips):
            for core in range(2):
                here = 2 * order[i] + core
                self.right.append((here, 2 * order[(i + 1) % chips] + core))
                self.left.append((here, 2 * order[(i - 1) % chips] + core))
        self.swap = [(i, i ^ 1) for i in range(count)]

    def device(self, offset, other=0):
        at = (self.place + (offset % self.size)) % self.size
        chip = jnp.where(at < 4, 2 * at, 15 - 2 * at) if self.size == 8 else at
        return 2 * chip + (self.core ^ other)

    def send(self, value, links):
        return lax.ppermute(value, "context", links)

    def gather(self, block, place):
        far = self.size // 2
        to_right = to_left = block
        place(self.device(0), block, 0)
        place(self.device(0, 1), self.send(block, self.swap), 0)
        for step in range(1, far + 1):
            at_left = 0
            if step == far:
                to_right, to_left, at_left = to_right[:1], to_left[1:], 1
            to_right = self.send(to_right, self.right)
            to_left = self.send(to_left, self.left)
            place(self.device(-step), to_right, 0)
            place(self.device(step), to_left, at_left)
            place(self.device(-step, 1), self.send(to_right, self.swap), 0)
            place(self.device(step, 1), self.send(to_left, self.swap), at_left)

    def scatter(self, take):
        far = self.size // 2

        def term(offset):
            return add_half(take(self.device(offset)), self.send(take(self.device(offset, 1)), self.swap))

        last = term(far)
        to_right = self.send(last[:1], self.right)
        to_left = self.send(last[1:], self.left)
        for step in range(far - 1, 0, -1):
            right_term, left_term = term(step), term(-step)
            if step == far - 1:
                right_term = jnp.concatenate([add_half(right_term[:1], to_right), right_term[1:]], 0)
                left_term = jnp.concatenate([left_term[:1], add_half(left_term[1:], to_left)], 0)
            else:
                right_term, left_term = add_half(right_term, to_right), add_half(left_term, to_left)
            to_right = self.send(right_term, self.right)
            to_left = self.send(left_term, self.left)
        return term(0).astype(F32) + to_right.astype(F32) + to_left.astype(F32)


def add_half(first, second):
    return (first.astype(F32) + second.astype(F32)).astype(first.dtype)


def cross(value):
    return lax.ppermute(value, "fsdp", [(0, 1), (1, 0)])


def pair_halves(own, side):
    got = cross(own)
    return jnp.where(side == 0, own, got), jnp.where(side == 0, got, own)


def pair_sum(left, right, side):
    got = cross(jnp.where(side == 0, right, left).astype(BF16))
    return jnp.where(side == 0, left, right).astype(F32) + got.astype(F32)


def sum_everywhere(value, count):
    step = 1
    while step < count:
        value = value + lax.ppermute(value, "context", [(i, i ^ step) for i in range(count)])
        step *= 2
    return value + cross(value)


def dot_nt(first, second):
    return lax.dot_general(first, second, (((1,), (1,)), ((), ())), preferred_element_type=F32)


def dot_nn(first, second):
    return lax.dot_general(first, second, (((1,), (0,)), ((), ())), preferred_element_type=F32)


def head_masks(scale):
    lane = lax.broadcasted_iota(jnp.int32, (1, SLOT), 1)
    return [jnp.where(lane < HEAD_DIM, scale, 0.0), jnp.where(lane < HEAD_DIM, 0.0, scale)]


def flipped(value):
    return value.astype(F32).T


def causal(tile):
    keys = lax.broadcasted_iota(jnp.int32, (tile, tile), 0)
    queries = lax.broadcasted_iota(jnp.int32, (tile, tile), 1)
    return keys <= queries


def forward_kernel(order, q_ref, k_ref, v_ref, o_ref, lse_ref, qs, ks, vs, vt, os, *, blk, tile):
    seq = q_ref.shape[0]
    tiles = seq // tile
    masks = head_masks(SCALE)

    def span(index, size):
        return pl.ds(pl.multiple_of(index * size, size), size)

    def sort_in(s, carry):
        here, there = span(s, blk), span(order[s], blk)
        block = q_ref[here, :].astype(F32)
        for head in range(2):
            qs[head, there, :] = (block * masks[head]).astype(BF16)
        ks[there, :] = k_ref[here, :]
        vs[there, :] = v_ref[here, :]
        return carry

    lax.fori_loop(0, seq // blk, sort_in, 0)

    def turn(t, carry):
        vt[t] = flipped(vs[span(t, tile), :]).astype(BF16)
        return carry

    lax.fori_loop(0, tiles, turn, 0)
    visible = causal(tile)

    def query_tile(i, carry):
        def key_tile(j, state, diagonal):
            fresh = []
            for head in range(2):
                top, total, accum = state[3 * head : 3 * head + 3]
                scores = dot_nt(ks[span(j, tile), :], qs[head, span(i, tile), :])
                if diagonal:
                    scores = jnp.where(visible, scores, NEG_LARGE)
                new_top = jnp.maximum(top, jnp.max(scores, axis=0, keepdims=True))
                terms = jnp.exp(scores - new_top)
                decay = jnp.exp(top - new_top)
                total = total * decay + jnp.sum(terms, axis=0, keepdims=True)
                values = vt[j, head * HEAD_DIM : (head + 1) * HEAD_DIM, :]
                accum = accum * decay + dot_nn(values, terms.astype(BF16))
                fresh += [new_top, total, accum]
            return tuple(fresh)

        start = (
            jnp.full((1, tile), NEG_LARGE, F32),
            jnp.zeros((1, tile), F32),
            jnp.zeros((HEAD_DIM, tile), F32),
        )
        state = lax.fori_loop(0, i, lambda j, state: key_tile(j, state, False), start + start)
        state = key_tile(i, state, True)
        mixed = jnp.concatenate([state[2] / state[1], state[5] / state[4]], axis=0)
        os[span(i, tile), :] = mixed.T.astype(BF16)
        for head in range(2):
            lse_ref[i, head : head + 1, :] = state[3 * head] + jnp.log(state[3 * head + 1])
        return carry

    lax.fori_loop(0, tiles, query_tile, 0)

    def sort_out(s, carry):
        o_ref[span(s, blk), :] = os[span(order[s], blk), :]
        return carry

    lax.fori_loop(0, seq // blk, sort_out, 0)


def backward_kernel(
    order, q_ref, k_ref, v_ref, g_ref, o_ref, lse_ref, d_ref, sum_ref, qs, ks, vs, gs, ps, kt, dqt, drow, dk, dv, dsort, *, blk, tile
):
    seq = q_ref.shape[0]
    tiles = seq // tile
    q_masks, g_masks = head_masks(SCALE), head_masks(1.0)

    def span(index, size):
        return pl.ds(pl.multiple_of(index * size, size), size)

    def sort_in(s, carry):
        here, there = span(s, blk), span(order[s], blk)
        q_block, g_block = q_ref[here, :].astype(F32), g_ref[here, :].astype(F32)
        for head in range(2):
            qs[head, there, :] = (q_block * q_masks[head]).astype(BF16)
            gs[head, there, :] = (g_block * g_masks[head]).astype(BF16)
        ks[there, :] = k_ref[here, :]
        vs[there, :] = v_ref[here, :]
        ps[there, :] = g_block * o_ref[here, :].astype(F32)
        return carry

    lax.fori_loop(0, seq // blk, sort_in, 0)

    def turn(t, carry):
        kt[t] = flipped(ks[span(t, tile), :]).astype(BF16)
        products = ps[span(t, tile), :].T
        for head in range(2):
            drow[t, head : head + 1, :] = jnp.sum(
                products[head * HEAD_DIM : (head + 1) * HEAD_DIM], axis=0, keepdims=True
            )
        dqt[t] = jnp.zeros((SLOT, tile), F32)
        return carry

    lax.fori_loop(0, tiles, turn, 0)
    visible = causal(tile)
    sum_ref[...] = jnp.zeros(sum_ref.shape, F32)

    def key_tile(j, carry):
        dk[...] = jnp.zeros(dk.shape, F32)
        dv[...] = jnp.zeros(dv.shape, F32)

        def query_tile(i, diagonal):
            key_add, value_add = [], []
            for head in range(2):
                scores = dot_nt(ks[span(j, tile), :], qs[head, span(i, tile), :])
                terms = jnp.exp(scores - lse_ref[i, head : head + 1, :])
                if diagonal:
                    terms = jnp.where(visible, terms, 0.0)
                slopes = dot_nt(vs[span(j, tile), :], gs[head, span(i, tile), :])
                slopes = (terms * (slopes - drow[i, head : head + 1, :])).astype(BF16)
                value_add.append(dot_nn(terms.astype(BF16), gs[head, span(i, tile), :]))
                key_add.append(dot_nn(slopes, qs[head, span(i, tile), :]))
                rows = slice(head * HEAD_DIM, (head + 1) * HEAD_DIM)
                dqt[i, rows, :] += dot_nn(kt[j, rows, :], slopes)
            dk[...] += key_add[0] + key_add[1]
            dv[...] += value_add[0] + value_add[1]

        query_tile(j, True)

        def later(i, carry):
            query_tile(i, False)
            return carry

        lax.fori_loop(j + 1, tiles, later, 0)
        dsort[1, span(j, tile), :] = dk[...].astype(BF16)
        dsort[2, span(j, tile), :] = dv[...].astype(BF16)
        sum_ref[1:2, :] += jnp.sum(dv[...], axis=0, keepdims=True)
        return carry

    lax.fori_loop(0, tiles, key_tile, 0)

    def finish(t, carry):
        query_grad = dqt[t].T * SCALE
        dsort[0, span(t, tile), :] = query_grad.astype(BF16)
        sum_ref[0:1, :] += jnp.sum(query_grad, axis=0, keepdims=True)
        return carry

    lax.fori_loop(0, tiles, finish, 0)

    def sort_out(s, carry):
        for part in range(3):
            d_ref[span(s, blk), part * SLOT : (part + 1) * SLOT] = dsort[part, span(order[s], blk), :]
        return carry

    lax.fori_loop(0, seq // blk, sort_out, 0)


def tile_of(seq):
    return math.gcd(seq, 512)


VMEM_SPEC = pl.BlockSpec(memory_space=pltpu.VMEM)
SMEM_SPEC = pl.BlockSpec(memory_space=pltpu.SMEM)


def attend_forward(order, queries, keys, values, blk):
    seq = queries.shape[0]
    tile = tile_of(seq)
    return pl.pallas_call(
        functools.partial(forward_kernel, blk=blk, tile=tile),
        out_shape=(
            jax.ShapeDtypeStruct((seq, SLOT), BF16),
            jax.ShapeDtypeStruct((seq // tile, 8, tile), F32),
        ),
        in_specs=[SMEM_SPEC] + [VMEM_SPEC] * 3,
        out_specs=(VMEM_SPEC, VMEM_SPEC),
        scratch_shapes=[
            pltpu.VMEM((2, seq, SLOT), BF16),
            pltpu.VMEM((seq, SLOT), BF16),
            pltpu.VMEM((seq, SLOT), BF16),
            pltpu.VMEM((seq // tile, SLOT, tile), BF16),
            pltpu.VMEM((seq, SLOT), BF16),
        ],
        compiler_params=pltpu.CompilerParams(vmem_limit_bytes=VMEM_LIMIT),
        cost_estimate=pl.CostEstimate(
            flops=4 * seq * seq * SLOT, bytes_accessed=8 * seq * SLOT, transcendentals=seq * seq
        ),
        name="attend_forward",
    )(order, queries, keys, values)


def attend_backward(order, queries, keys, values, grads, mixed, lse, blk):
    seq = queries.shape[0]
    tile = tile_of(seq)
    tiles = seq // tile
    return pl.pallas_call(
        functools.partial(backward_kernel, blk=blk, tile=tile),
        out_shape=(
            jax.ShapeDtypeStruct((seq, 3 * SLOT), BF16),
            jax.ShapeDtypeStruct((8, SLOT), F32),
        ),
        in_specs=[SMEM_SPEC] + [VMEM_SPEC] * 6,
        out_specs=(VMEM_SPEC, VMEM_SPEC),
        scratch_shapes=[
            pltpu.VMEM((2, seq, SLOT), BF16),
            pltpu.VMEM((seq, SLOT), BF16),
            pltpu.VMEM((seq, SLOT), BF16),
            pltpu.VMEM((2, seq, SLOT), BF16),
            pltpu.VMEM((seq, SLOT), F32),
            pltpu.VMEM((tiles, SLOT, tile), BF16),
            pltpu.VMEM((tiles, SLOT, tile), F32),
            pltpu.VMEM((tiles, 8, tile), F32),
            pltpu.VMEM((tile, SLOT), F32),
            pltpu.VMEM((tile, SLOT), F32),
            pltpu.VMEM((3, seq, SLOT), BF16),
        ],
        compiler_params=pltpu.CompilerParams(vmem_limit_bytes=VMEM_LIMIT),
        cost_estimate=pl.CostEstimate(
            flops=10 * seq * seq * SLOT, bytes_accessed=20 * seq * SLOT, transcendentals=seq * seq
        ),
        name="attend_backward",
    )(order, queries, keys, values, grads, mixed, lse)


def body(
    tokens,
    cotangent,
    block_order,
    ln1_gain,
    ln1_bias,
    w_qkv,
    qv_bias,
    w_out,
    out_bias,
    ln2_gain,
    ln2_bias,
    w_fc,
    fc_bias,
    w_proj,
    proj_bias,
):
    width = HEADS * HEAD_DIM
    half = width // 2
    count = lax.axis_size("context")
    rows = tokens.shape[1]
    seq = count * rows
    blk = rows // 2
    hidden = fc_bias.shape[0] * 2
    share = hidden // count
    own_rows = w_qkv.shape[0]
    padded = count * SLOT
    grad_scale = 1.0 / math.sqrt(lax.axis_size("fsdp") * seq)
    side = lax.axis_index("fsdp")
    ring = Ring(count)
    mine = ring.mine
    order = block_order.astype(jnp.int32)

    vectors = jnp.concatenate(
        [
            jnp.stack(
                [ln1_gain, ln1_bias, qv_bias[:, 0], qv_bias[:, 1], out_bias, ln2_gain, ln2_bias, proj_bias]
            ),
            fc_bias.reshape(-1, half),
        ],
        axis=0,
    )
    low, high = pair_halves(vectors, side)
    wide = jnp.concatenate([low[:8], high[:8]], axis=1).astype(F32)
    gain_one, shift_one, q_bias, v_bias, out_b, gain_two, shift_two, proj_b = [wide[i] for i in range(8)]
    fc_b = jnp.concatenate([low[8:].reshape(-1), high[8:].reshape(-1)])
    fc_b = lax.dynamic_slice(fc_b, (mine * share,), (share,)).astype(F32)
    slot_bias = jnp.stack([q_bias, jnp.zeros_like(q_bias), v_bias])
    slot_bias = jnp.pad(slot_bias, ((0, 0), (0, padded - width))).reshape(3, count, SLOT)
    slot_bias = lax.dynamic_index_in_dim(slot_bias, mine, axis=1, keepdims=False).reshape(3 * SLOT)

    xs16 = tokens[0]
    xs = xs16.astype(F32)
    buffers = {}

    def put(name):
        def place(device, piece, first):
            value = piece
            if name == "h_one":
                normed, _ = norm_stats(piece.astype(F32))
                value = (normed * gain_one + shift_one).astype(BF16)
            if name not in buffers:
                buffers[name] = jnp.zeros((count, 2, blk, width), BF16)
            buffers[name] = lax.dynamic_update_slice(
                buffers[name], value[None], (device, jnp.int32(first), jnp.int32(0), jnp.int32(0))
            )

        return place

    ring.gather(xs16.reshape(2, blk, width), put("h_one"))
    h_one_all = buffers["h_one"].reshape(seq, width)
    normed_one, inv_one = norm_stats(xs)

    low, high = pair_halves(w_qkv, side)
    parts = jnp.concatenate([low, high], axis=1).reshape(own_rows, 3, width)
    parts = jnp.pad(parts, ((0, 0), (0, 0), (0, padded - width))).reshape(own_rows, 3, count, SLOT)
    parts = parts.transpose(2, 0, 1, 3).reshape(count, own_rows, 3 * SLOT)
    w_heads = lax.all_to_all(parts, "context", 0, 0, tiled=True).reshape(width, 3 * SLOT)

    qkv = jnp.dot(h_one_all, w_heads, preferred_element_type=F32) + slot_bias
    qkv = qkv.astype(BF16)
    queries, keys, values = qkv[:, :SLOT], qkv[:, SLOT : 2 * SLOT], qkv[:, 2 * SLOT :]

    w_out_b, cot_b, h_one_b = lax.optimization_barrier((w_out, cotangent, h_one_all))
    low, high = pair_halves(w_out_b, side)
    w_out_all = lax.all_gather(jnp.concatenate([low, high], axis=1), "context", axis=0, tiled=True)
    cot16 = cot_b[0]
    cot_all = lax.all_gather(cot16, "context", axis=0, tiled=True)

    low, high = pair_halves(w_fc, side)
    parts = jnp.concatenate([low, high], axis=1).reshape(own_rows, count, share).transpose(1, 0, 2)
    w_fc_part = lax.all_to_all(parts, "context", 0, 0, tiled=True).reshape(width, share)
    low, high = pair_halves(w_proj, side)
    w_proj_part = jnp.concatenate([low, high], axis=1)

    mixed, lse = attend_forward(order, queries, keys, values, blk)
    attn_out = lax.all_to_all(mixed, "context", 0, 1, tiled=True)[:, :width]

    resid_one = xs + jnp.dot(attn_out, w_out_all, preferred_element_type=F32) + out_b
    normed_two, inv_two = norm_stats(resid_one)
    h_two = (normed_two * gain_two + shift_two).astype(BF16)
    ring.gather(h_two.reshape(2, blk, width), put("h_two"))
    h_two_all = buffers["h_two"].reshape(seq, width)

    grad_act = dot_nt(cot_all, w_proj_part)
    pre_act = jnp.dot(h_two_all, w_fc_part, preferred_element_type=F32) + fc_b
    act_value, act_slope = gelu_pair(pre_act)
    act_half = act_value.astype(BF16)
    grad_pre = grad_act * act_slope
    g_fc_bias = jnp.sum(grad_pre, axis=0)
    grad_pre16 = grad_pre.astype(BF16)
    h2_terms = dot_nt(grad_pre16, w_fc_part).astype(BF16).reshape(count, 2, blk, width)

    def taker(terms):
        return lambda device: lax.dynamic_index_in_dim(terms, device, axis=0, keepdims=False)

    grad_h2 = ring.scatter(taker(h2_terms)).reshape(rows, width)

    grad_y = cotangent[0].astype(F32)
    grad_r1 = grad_y + norm_back(grad_h2, normed_two, inv_two, gain_two)
    grad_r16 = grad_r1.astype(BF16)
    grad_o16 = dot_nt(grad_r16, w_out_all).astype(BF16)
    grad_heads = lax.all_to_all(
        jnp.pad(grad_o16, ((0, 0), (0, padded - width))), "context", 1, 0, tiled=True
    )

    act_b, grad_heads_b = lax.optimization_barrier((act_half, grad_heads))
    out_terms = jnp.dot(act_b, w_proj_part, preferred_element_type=F32).astype(BF16)
    out_sum = ring.scatter(taker(out_terms.reshape(count, 2, blk, width))).reshape(rows, width)
    result = (resid_one + out_sum + proj_b).astype(BF16)

    g_proj = lax.dot_general(act_b, cot_all, (((0,), (0,)), ((), ())), preferred_element_type=F32) * grad_scale
    g_w_proj = pair_sum(g_proj[:, :half], g_proj[:, half:], side)

    g_fc = lax.dot_general(h_two_all, grad_pre16, (((0,), (0,)), ((), ())), preferred_element_type=F32)
    g_fc = (g_fc * grad_scale).astype(BF16).reshape(count, own_rows, share)
    g_fc = lax.all_to_all(g_fc, "context", 0, 0, tiled=True)
    g_fc = g_fc.transpose(1, 0, 2).reshape(own_rows, hidden)
    g_w_fc = pair_sum(g_fc[:, : hidden // 2], g_fc[:, hidden // 2 :], side)

    g_out = lax.dot_general(attn_out, grad_r16, (((0,), (0,)), ((), ())), preferred_element_type=F32) * grad_scale
    g_out = pair_sum(g_out[:, :half], g_out[:, half:], side).astype(BF16).reshape(count, own_rows, half)
    even = own_rows + own_rows % 2
    g_out = jnp.pad(g_out, ((0, 0), (0, even - own_rows), (0, 0))).reshape(count, 2, even // 2, half)
    g_w_out = ring.scatter(taker(g_out)).reshape(even, half)[:own_rows]

    grad_qkv16, head_sums = attend_backward(order, queries, keys, values, grad_heads, mixed, lse, blk)
    h1_terms = dot_nt(grad_qkv16, w_heads).astype(BF16).reshape(count, 2, blk, width)
    grad_h1 = ring.scatter(taker(h1_terms)).reshape(rows, width)
    grad_x = (grad_r1 + norm_back(grad_h1, normed_one, inv_one, gain_one)).astype(BF16)

    g_qkv = lax.dot_general(h_one_all, grad_qkv16, (((0,), (0,)), ((), ())), preferred_element_type=F32)
    g_qkv = (g_qkv * grad_scale).astype(BF16).reshape(count, own_rows, 3 * SLOT)
    g_qkv = lax.all_to_all(g_qkv, "context", 0, 0, tiled=True)
    g_qkv = g_qkv.reshape(count, own_rows, 3, SLOT).transpose(1, 2, 0, 3)
    g_qkv = g_qkv.reshape(own_rows, 3, padded)[:, :, :width].reshape(own_rows, 3 * width)
    g_w_qkv = pair_sum(g_qkv[:, : 3 * half], g_qkv[:, 3 * half :], side)

    fc_place = lax.dynamic_update_slice(jnp.zeros((hidden,), F32), g_fc_bias, (mine * share,))
    early = jnp.concatenate(
        [
            jnp.sum(grad_h2 * normed_two, axis=0),
            jnp.sum(grad_h2, axis=0),
            jnp.sum(grad_r1, axis=0),
            jnp.sum(grad_y, axis=0),
            fc_place,
        ]
    )
    early = sum_everywhere(early.reshape(-1, SLOT) * grad_scale, count).reshape(-1)
    head_place = lax.dynamic_update_slice(
        jnp.zeros((2, padded), F32), head_sums[:2], (jnp.int32(0), mine * SLOT)
    )[:, :width]
    late = jnp.concatenate(
        [jnp.sum(grad_h1 * normed_one, axis=0), jnp.sum(grad_h1, axis=0), head_place[0], head_place[1]]
    )
    late = sum_everywhere(late.reshape(-1, SLOT) * grad_scale, count).reshape(-1)

    def own_half(vector):
        return lax.dynamic_slice(vector, (side * (vector.shape[0] // 2),), (vector.shape[0] // 2,))

    g_ln2_gain, g_ln2_bias, g_out_bias, g_proj_bias = [
        own_half(early[i * width : (i + 1) * width]) for i in range(4)
    ]
    g_fc_bias = own_half(early[4 * width :])
    g_ln1_gain, g_ln1_bias, g_q, g_v = [own_half(late[i * width : (i + 1) * width]) for i in range(4)]
    return (
        result[None],
        grad_x[None],
        g_ln1_gain,
        g_ln1_bias,
        g_w_qkv,
        jnp.stack([g_q, g_v], axis=1),
        g_w_out,
        g_out_bias,
        g_ln2_gain,
        g_ln2_bias,
        g_w_fc,
        g_fc_bias,
        g_w_proj,
        g_proj_bias,
    )


def solution(mesh):
    rows = P("fsdp", "context", None)
    weight = P("context", "fsdp")
    vector = P("fsdp")
    pair = P("fsdp", None)
    return jax.shard_map(
        body,
        mesh=mesh,
        in_specs=(
            rows, rows, P(), vector, vector, weight, pair, weight,
            vector, vector, vector, weight, vector, weight, vector,
        ),
        out_specs=(
            rows, rows, vector, vector, weight, pair, weight,
            vector, vector, vector, weight, vector, weight, vector,
        ),
        check_vma=False,
    )
```

time: 2720 us -> 835 us (0.31)
  blocking collectives: 1220 us -> 0 us
  local copies, waits for them, and re-layouts: 727 us -> 149 us
  matrix products: 229 us -> 71.6 us
  waiting for transfers between devices: 396 us -> 303 us
  starting transfers between devices: 65 us -> 150 us
  other arithmetic: 44.6 us -> 99.7 us
  Pallas kernels: 0 us -> 36.2 us
    unnamed x4 -> x0, blocking collectives: 1120 us -> none
    dynamic_update_slice x16 -> x20, local copies, waits for them, and re-layouts: 539 us -> 3.71 us  [the longest x18 2.74 us: place(): lax.dynamic_update_slice(buffers[name], value[None], (device, jnp.int32(f...]
    all_gather x8 -> x2, waiting for transfers between devices: 393 us -> 0.01 us  [the longest x1 0.01 us: body(): lax.all_gather(jnp.concatenate([low, high], axis=1), 'context', axis=0, t...]
    ppermute x0 -> x117, waiting for transfers between devices: none -> 221 us  [the longest x98 197 us: send(): return lax.ppermute(value, 'context', links)]
    dot_general x40 -> x12, matrix products: 229 us -> 71.6 us  [the longest x4 20.8 us: dot_nt(): lax.dot_general(first, second, (((1,), (1,)), ((), ())), preferred_elemen...]
    unnamed x128 -> x102, local copies, waits for them, and re-layouts: 148 us -> 21.2 us
    ppermute x0 -> x117, starting transfers between devices: none -> 109 us  [the longest x98 83.8 us: send(): return lax.ppermute(value, 'context', links)]
    all_to_all x0 -> x6, waiting for transfers between devices: none -> 81.5 us  [the longest x1 42.6 us: body(): lax.all_to_all(parts, 'context', 0, 0, tiled=True).reshape(width, 3 * SLOT)]
  transfers between devices with their start and end apart: 19 -> 125, of which waited for: 7 -> 50; matrix products, arithmetic and copies ran while one was open for 52% -> 33% of each run, Pallas kernels for 0% -> 4%
where the time goes in v1:
time: 835 us; the launch traced here: 825 us
  waiting for transfers between devices  303 us (36%)
  starting transfers between devices  150 us (18%)
  local copies, waits for them, and re-layouts  149 us (18%)
  other arithmetic  99.7 us (12%)
  matrix products  71.6 us (9%)
  Pallas kernels  36.2 us (4%)
  between operations  16.1 us (2%)
    ppermute x98, waiting for transfers between devices, send(): return lax.ppermute(value, 'context', links)  197 us
    ppermute x98, starting transfers between devices, send(): return lax.ppermute(value, 'context', links)  83.8 us
    all_to_all x1, waiting for transfers between devices, body(): lax.all_to_all(parts, 'context', 0, 0, tiled=True).reshape(width, 3 * SLOT)  42.6 us
    convert_element_type x28, other arithmetic, add_half(): return (first.astype(F32) + second.astype(F32)).astype(first.dtype)  31 us
    all_to_all x1, waiting for transfers between devices, body(): lax.all_to_all(parts, 'context', 0, 0, tiled=True).reshape(width, share)  27.2 us
    pallas_call x1, Pallas kernels, attend_backward(): pl.pallas_call(functools.partial(backward_kernel, blk=blk, tile=tile), ou...  21.2 us
    unnamed x102, local copies, waits for them, and re-layouts  21.2 us
    dot_general x4, matrix products, dot_nt(): lax.dot_general(first, second, (((1,), (1,)), ((), ())), preferred_elemen...  20.8 us
  transfers between devices with their start and end apart: 125, of which 50 were waited for; matrix products, arithmetic and copies ran while one was open for 33% of the time, Pallas kernels for 4%

profile of v1, /device:TPU:0, one launch (start us, length us, event | category | flops | bytes accessed | tf_op | source)
XLA Modules:
  0.0 825.0 jit_solution(14422733323936377095)
XLA Ops:
  36.4 6.3 collective-permute-done.7
  76.6 6.4 collective-permute-done.19
  84.8 12.0 %collective-permute-done.18 = bf16[100,2400]{1,0:T(8,128)(2,1)S(1)} collective-permute-done((bf16[100,2400]{1,0:T(8,128)(2,1)S(1)}, bf16[100,2400]{1,0:T(8,128)(2,1)S(1)}, u32[]{:S(2)}, u32[]{:S(2)}) %collective-permute-start.18) | collective-permute-done | bytes 480032 | tf_op jit(solution)/shard_map/ppermute | solution.py:122
  101.5 5.1 all-to-all-start
  107.4 42.6 %all-to-all-done = bf16[16,100,384]{2,1,0:T(8,128)(2,1)S(1)} async-done(((bf16[16,100,384]{2,1,0:T(8,128)(2,1)}), bf16[16,100,384]{2,1,0:T(8,128)(2,1)S(1)}, u32[]{:S(2)}, u32[]{:S(2)}) %all-to-all-start) | async-done | bytes 1228832 | tf_op jit(solution)/shard_map/all_to_all | solution.py:462
  150.3 7.2 add_convert_fusion.1
  158.8 15.0 %attend_forward.1 = (bf16[2048,128]{1,0:T(8,128)(2,1)}, f32[4,8,512]{2,1,0:T(8,128)}) custom-call(s32[32]{0:T(128)} %order.3, bf16[2048,128]{1,0:T(8,128)(2,1)} %get-tuple-element.128.q_ref, bf16[2048,128]{1,0:T(8,128)(2,1)} %get-tuple-element.127.k_ref, bf16[2048,128]{1,0:T(8,128)(2,1)} %get-tuple-element.126.v_ref), custom_call_target="tpu_custom_call" | custom-call | flops 2147483648 | bytes 2097152 | tf_op jit(solution)/shard_map/attend_forward/pallas_call | solution.py:329
  175.8 13.0 %all-to-all-start.1 = ((bf16[16,128,128]{1,2,0:T(8,128)(2,1)}), bf16[16,128,128]{1,2,0:T(8,128)(2,1)S(1)}, u32[]{:S(2)}, u32[]{:S(2)}) async-start(bf16[16,128,128]{1,2,0:T(8,128)(2,1)} %copy.107), calls=%async_computation.1 | async-start | bytes 1048576 | tf_op jit(solution)/shard_map/all_to_all | solution.py:481
  191.9 11.3 %all-to-all-done.1 = bf16[16,128,128]{1,2,0:T(8,128)(2,1)S(1)} async-done(((bf16[16,128,128]{1,2,0:T(8,128)(2,1)}), bf16[16,128,128]{1,2,0:T(8,128)(2,1)S(1)}, u32[]{:S(2)}, u32[]{:S(2)}) %all-to-all-start.1) | async-done | bytes 524320 | tf_op jit(solution)/shard_map/all_to_all | solution.py:481
  203.3 6.6 all-to-all-start.2
  211.6 8.0 reshape.673
  219.7 4.8 fusion.214
  230.8 27.2 %all-to-all-done.2 = bf16[16,100,400]{1,2,0:T(8,128)(2,1)} async-done(((bf16[16,100,400]{1,2,0:T(8,128)(2,1)}), bf16[16,100,400]{1,2,0:T(8,128)(2,1)}, u32[]{:S(2)}, u32[]{:S(2)}) %all-to-all-start.2) | async-done | bytes 1280032 | tf_op jit(solution)/shard_map/all_to_all | solution.py:476
  269.3 21.9 %collective-permute-start.25 = (bf16[2,64,1600]{2,1,0:T(8,128)(2,1)}, bf16[2,64,1600]{2,1,0:T(8,128)(2,1)S(1)}, u32[]{:S(2)}, u32[]{:S(2)}) collective-permute-start(bf16[2,64,1600]{2,1,0:T(8,128)(2,1)} %collective-permute-done.21), channel_id=1, source_target_pairs={{0,4},{1,5},{4,8},{5,9},{8,12},{9,13},{12,14},{13,15},{14,10},{15,... | collective-permute-start | bytes 1228808 | tf_op jit(solution)/shard_map/ppermute | solution.py:78
  293.6 7.6 collective-permute-done.26
  303.9 8.6 %collective-permute-done.30 = bf16[2,64,1600]{2,1,0:T(8,128)(2,1)S(1)} collective-permute-done((bf16[2,64,1600]{2,1,0:T(8,128)(2,1)S(1)}, bf16[2,64,1600]{2,1,0:T(8,128)(2,1)S(1)}, u32[]{:S(2)}, u32[]{:S(2)}) %collective-permute-start.30) | collective-permute-done | bytes 409632 | tf_op jit(solution)/shard_map/ppermute | solution.py:78
  324.7 5.5 multiply_convert_fusion
  330.2 8.1 fusion.215
  339.6 5.6 convolution_convert_fusion.2
  345.2 9.6 %copy.112 = bf16[2048,1600]{1,0:T(8,128)(2,1)} copy(bf16[2048,1600]{0,1:T(8,128)(2,1)} %convolution_convert_fusion.2) | data formatting | bytes 13107200 | tf_op jit(solution)/shard_map/convert_element_type | solution.py:496
  362.7 5.7 collective-permute-done.44
  370.7 8.9 %collective-permute-done.45 = bf16[2,64,1600]{2,1,0:T(8,128)(2,1)S(1)} collective-permute-done((bf16[2,64,1600]{2,1,0:T(8,128)(2,1)S(1)}, bf16[2,64,1600]{2,1,0:T(8,128)(2,1)S(1)}, u32[]{:S(2)}, u32[]{:S(2)}) %collective-permute-start.45) | collective-permute-done | bytes 409632 | tf_op jit(solution)/shard_map/ppermute | solution.py:78
  382.9 8.1 collective-permute-done.46
  393.0 8.8 %collective-permute-done.52 = bf16[2,64,1600]{2,1,0:T(8,128)(2,1)S(1)} collective-permute-done((bf16[2,64,1600]{2,1,0:T(8,128)(2,1)S(1)}, bf16[2,64,1600]{2,1,0:T(8,128)(2,1)S(1)}, u32[]{:S(2)}, u32[]{:S(2)}) %collective-permute-start.52) | collective-permute-done | bytes 409632 | tf_op jit(solution)/shard_map/ppermute | solution.py:78
  408.5 5.4 reshape.636
  417.0 5.1 all-to-all-start.5
  426.9 31.9 %collective-permute-done.47 = bf16[2,64,1600]{2,1,0:T(8,128)(2,1)} collective-permute-done((bf16[2,64,1600]{2,1,0:T(8,128)(2,1)S(1)}, bf16[2,64,1600]{2,1,0:T(8,128)(2,1)}, u32[]{:S(2)}, u32[]{:S(2)}) %collective-permute-start.47) | collective-permute-done | bytes 409632 | tf_op jit(solution)/shard_map/ppermute | solution.py:78
  475.7 10.4 %collective-permute-start.112 = (f32[100,128]{1,0:T(8,128)S(1)}, f32[100,128]{1,0:T(8,128)S(1)}, u32[]{:S(2)}, u32[]{:S(2)}) collective-permute-start(f32[100,128]{1,0:T(8,128)S(1)} %fusion.232), channel_id=1, source_target_pairs={{0,4},{1,5},{2,6},{3,7},{4,0},{5,1},{6,2},{7,3},{8,12},{9,13},{10,... | collective-permute-start | bytes 153608 | tf_op jit(solution)/shard_map/ppermute | solution.py:138
  486.1 6.7 convolution_multiply_fusion
  495.6 5.3 all-to-all-start.3
  501.9 6.1 select_convert_fusion
  516.2 21.2 %attend_backward.1 = (bf16[2048,384]{1,0:T(8,128)(2,1)}, f32[8,128]{1,0:T(8,128)}) custom-call(s32[32]{0:T(128)} %order.3, bf16[2048,128]{1,0:T(8,128)(2,1)} %get-tuple-element.128.q_ref, bf16[2048,128]{1,0:T(8,128)(2,1)} %get-tuple-element.127.k_ref, bf16[2048,128]{1,0:T(8,128)(2,1)} %get-tuple-element.126.v_ref, bf16[2048,128]{1,0:T(8,128)(2,1)} %bitcast.432, ...), custom_call_target="tpu_custom_call" | custom-call | flops 5368709120 | bytes 5242880 | tf_op jit(solution)/shard_map/attend_backward/pallas_call | solution.py:356
  537.4 8.1 fusion.16
  545.6 5.5 convolution_convert_fusion
  553.4 6.2 all-to-all-start.4
  559.6 8.2 convolution_convert_fusion.1
  567.8 6.0 fusion.10
  576.5 9.6 %copy.115 = bf16[2048,1600]{1,0:T(8,128)(2,1)} copy(bf16[2048,1600]{0,1:T(8,128)(2,1)} %convolution_convert_fusion.1) | data formatting | bytes 13107200 | tf_op jit(solution)/shard_map/convert_element_type | solution.py:512
  590.5 9.7 %copy.117 = bf16[2048,1600]{1,0:T(8,128)(2,1)} copy(bf16[2048,1600]{0,1:T(8,128)(2,1)} %convolution_convert_fusion) | data formatting | bytes 13107200 | tf_op jit(solution)/shard_map/convert_element_type | solution.py:532
  616.2 4.9 collective-permute-done.76
  626.0 5.6 collective-permute-done.61
  633.9 7.6 collective-permute-done.77
  644.4 7.1 collective-permute-done.62
  668.5 4.8 collective-permute-done.83
  677.6 5.2 copy.124
  722.4 8.6 %collective-permute-done.69 = bf16[2,64,1600]{2,1,0:T(8,128)(2,1)S(1)} collective-permute-done((bf16[2,64,1600]{2,1,0:T(8,128)(2,1)S(1)}, bf16[2,64,1600]{2,1,0:T(8,128)(2,1)S(1)}, u32[]{:S(2)}, u32[]{:S(2)}) %collective-permute-start.69) | collective-permute-done | bytes 409632 | tf_op jit(solution)/shard_map/ppermute | solution.py:78
  735.1 7.6 collective-permute-done.107
  769.4 10.3 %collective-permute-done.109 = bf16[2,50,800]{2,1,0:T(8,128)(2,1)S(1)} collective-permute-done((bf16[2,50,800]{2,1,0:T(8,128)(2,1)S(1)}, bf16[2,50,800]{2,1,0:T(8,128)(2,1)S(1)}, u32[]{:S(2)}, u32[]{:S(2)}) %collective-permute-start.109) | collective-permute-done | bytes 160032 | tf_op jit(solution)/shard_map/ppermute | solution.py:78
  (619 shorter events, 337.6 us)
Async XLA Ops:
  7.2 204.5 %all-gather.7.cloned.1.call-start = ((), (), s32[]{:S(2)}) async-start(), calls=%async_computation.7 | async-start | bytes 5883904 | tf_op jit(solution)/shard_map/all_gather | solution.py:470
  8.5 21.0 %collective-permute-start.3 = (bf16[2,64,1600]{2,1,0:T(8,128)(2,1)S(1)}, bf16[2,64,1600]{2,1,0:T(8,128)(2,1)S(1)}, u32[]{:S(2)}, u32[]{:S(2)}) collective-permute-start(bf16[2,64,1600]{2,1,0:T(8,128)(2,1)S(1)} %bitcast.423), channel_id=1, source_target_pairs={{0,2},{1,3},{4,0},{5,1},{8,4},{9,5},{12,8},{13,9},{14,12},{15,13},... | collective-permute-start | bytes 1228808 | tf_op jit(solution)/shard_map/ppermute | solution.py:78
  11.5 18.1 %collective-permute-start.2 = (bf16[2,64,1600]{2,1,0:T(8,128)(2,1)S(1)}, bf16[2,64,1600]{2,1,0:T(8,128)(2,1)S(1)}, u32[]{:S(2)}, u32[]{:S(2)}) collective-permute-start(bf16[2,64,1600]{2,1,0:T(8,128)(2,1)S(1)} %bitcast.424), channel_id=1, source_target_pairs={{0,4},{1,5},{4,8},{5,9},{8,12},{9,13},{12,14},{13,15},{14,10},{15,... | collective-permute-start | bytes 1228808 | tf_op jit(solution)/shard_map/ppermute | solution.py:78
  11.6 18.7 %collective-permute-start.1 = (bf16[2,64,1600]{2,1,0:T(8,128)(2,1)S(1)}, bf16[2,64,1600]{2,1,0:T(8,128)(2,1)S(1)}, u32[]{:S(2)}, u32[]{:S(2)}) collective-permute-start(bf16[2,64,1600]{2,1,0:T(8,128)(2,1)S(1)} %bitcast.425), channel_id=1, source_target_pairs={{0,1},{1,0},{2,3},{3,2},{4,5},{5,4},{6,7},{7,6},{8,9},{9,8},{10,11... | collective-permute-start | bytes 1228808 | tf_op jit(solution)/shard_map/ppermute | solution.py:78
  47.7 13.5 %collective-permute-start.8 = (bf16[2,64,1600]{2,1,0:T(8,128)(2,1)S(1)}, bf16[2,64,1600]{2,1,0:T(8,128)(2,1)S(1)}, u32[]{:S(2)}, u32[]{:S(2)}) collective-permute-start(bf16[2,64,1600]{2,1,0:T(8,128)(2,1)S(1)} %collective-permute-done.6), channel_id=1, source_target_pairs={{0,1},{1,0},{2,3},{3,2},{4,5},{5,4},{6,7},{7,6},{8,9},{9,8},{10,11... | collective-permute-start | bytes 1228808 | tf_op jit(solution)/shard_map/ppermute | solution.py:78
  101.5 48.5 %all-to-all-start = ((bf16[16,100,384]{2,1,0:T(8,128)(2,1)}), bf16[16,100,384]{2,1,0:T(8,128)(2,1)S(1)}, u32[]{:S(2)}, u32[]{:S(2)}) async-start(bf16[16,100,384]{2,1,0:T(8,128)(2,1)} %reshape.674), calls=%async_computation | async-start | bytes 2555904 | tf_op jit(solution)/shard_map/all_to_all | solution.py:462
  106.6 82.2 %collective-permute-start.37 = (bf16[100,3200]{1,0:T(8,128)(2,1)S(1)}, bf16[100,3200]{1,0:T(8,128)(2,1)}, u32[]{:S(2)}, u32[]{:S(2)}) collective-permute-start(bf16[100,3200]{1,0:T(8,128)(2,1)S(1)} %copy-done.18), channel_id=1, source_target_pairs={{0,16},{16,0},{1,17},{17,1},{2,18},{18,2},{3,19},{19,3},{4,20},{20... | collective-permute-start | bytes 1920008 | tf_op jit(solution)/shard_map/ppermute | solution.py:122
  175.8 27.5 %all-to-all-start.1 = ((bf16[16,128,128]{1,2,0:T(8,128)(2,1)}), bf16[16,128,128]{1,2,0:T(8,128)(2,1)S(1)}, u32[]{:S(2)}, u32[]{:S(2)}) async-start(bf16[16,128,128]{1,2,0:T(8,128)(2,1)} %copy.107), calls=%async_computation.1 | async-start | bytes 1048576 | tf_op jit(solution)/shard_map/all_to_all | solution.py:481
  188.8 141.4 %all-gather.5.cloned.1.call-start = ((), (), s32[]{:S(2)}) async-start(), calls=%async_computation.6 | async-start | bytes 6963200 | tf_op jit(solution)/shard_map/all_gather | solution.py:472
  203.3 54.7 %all-to-all-start.2 = ((bf16[16,100,400]{1,2,0:T(8,128)(2,1)}), bf16[16,100,400]{1,2,0:T(8,128)(2,1)}, u32[]{:S(2)}, u32[]{:S(2)}) async-start(bf16[16,100,400]{1,2,0:T(8,128)(2,1)} %bitcast.52), calls=%async_computation.2 | async-start | bytes 3276800 | tf_op jit(solution)/shard_map/all_to_all | solution.py:476
  209.8 18.6 %collective-permute-start.38 = (bf16[400,800]{1,0:T(8,128)(2,1)}, bf16[400,800]{1,0:T(8,128)(2,1)}, u32[]{:S(2)}, u32[]{:S(2)}) collective-permute-start(bf16[400,800]{1,0:T(8,128)(2,1)} %param.28), channel_id=1, source_target_pairs={{0,16},{16,0},{1,17},{17,1},{2,18},{18,2},{3,19},{19,3},{4,20},{20... | collective-permute-start | bytes 1920008 | tf_op jit(solution)/shard_map/ppermute | solution.py:122
  225.5 43.6 %collective-permute-start.22 = (bf16[2,64,1600]{2,1,0:T(8,128)(2,1)S(1)}, bf16[2,64,1600]{2,1,0:T(8,128)(2,1)S(1)}, u32[]{:S(2)}, u32[]{:S(2)}) collective-permute-start(bf16[2,64,1600]{2,1,0:T(8,128)(2,1)S(1)} %bitcast.427), channel_id=1, source_target_pairs={{0,2},{1,3},{4,0},{5,1},{8,4},{9,5},{12,8},{13,9},{14,12},{15,13},... | collective-permute-start | bytes 1228808 | tf_op jit(solution)/shard_map/ppermute | solution.py:78
  227.3 42.0 %collective-permute-start.21 = (bf16[2,64,1600]{2,1,0:T(8,128)(2,1)S(1)}, bf16[2,64,1600]{2,1,0:T(8,128)(2,1)}, u32[]{:S(2)}, u32[]{:S(2)}) collective-permute-start(bf16[2,64,1600]{2,1,0:T(8,128)(2,1)S(1)} %bitcast.428), channel_id=1, source_target_pairs={{0,4},{1,5},{4,8},{5,9},{8,12},{9,13},{12,14},{13,15},{14,10},{15,... | collective-permute-start | bytes 1228808 | tf_op jit(solution)/shard_map/ppermute | solution.py:78
  227.9 63.5 %collective-permute-start.20 = (bf16[2,64,1600]{2,1,0:T(8,128)(2,1)S(1)}, bf16[2,64,1600]{2,1,0:T(8,128)(2,1)}, u32[]{:S(2)}, u32[]{:S(2)}) collective-permute-start(bf16[2,64,1600]{2,1,0:T(8,128)(2,1)S(1)} %bitcast.429), channel_id=1, source_target_pairs={{0,1},{1,0},{2,3},{3,2},{4,5},{5,4},{6,7},{7,6},{8,9},{9,8},{10,11... | collective-permute-start | bytes 1228808 | tf_op jit(solution)/shard_map/ppermute | solution.py:78
  269.1 32.1 %collective-permute-start.26 = (bf16[2,64,1600]{2,1,0:T(8,128)(2,1)S(1)}, bf16[2,64,1600]{2,1,0:T(8,128)(2,1)S(1)}, u32[]{:S(2)}, u32[]{:S(2)}) collective-permute-start(bf16[2,64,1600]{2,1,0:T(8,128)(2,1)S(1)} %collective-permute-done.22), channel_id=1, source_target_pairs={{0,2},{1,3},{4,0},{5,1},{8,4},{9,5},{12,8},{13,9},{14,12},{15,13},... | collective-permute-start | bytes 1228808 | tf_op jit(solution)/shard_map/ppermute | solution.py:78
  269.3 34.4 %collective-permute-start.24 = (bf16[2,64,1600]{2,1,0:T(8,128)(2,1)S(1)}, bf16[2,64,1600]{2,1,0:T(8,128)(2,1)S(1)}, u32[]{:S(2)}, u32[]{:S(2)}) collective-permute-start(bf16[2,64,1600]{2,1,0:T(8,128)(2,1)S(1)} %collective-permute-done.22), channel_id=1, source_target_pairs={{0,1},{1,0},{2,3},{3,2},{4,5},{5,4},{6,7},{7,6},{8,9},{9,8},{10,11... | collective-permute-start | bytes 1228808 | tf_op jit(solution)/shard_map/ppermute | solution.py:78
  269.3 31.9 %collective-permute-start.25 = (bf16[2,64,1600]{2,1,0:T(8,128)(2,1)}, bf16[2,64,1600]{2,1,0:T(8,128)(2,1)S(1)}, u32[]{:S(2)}, u32[]{:S(2)}) collective-permute-start(bf16[2,64,1600]{2,1,0:T(8,128)(2,1)} %collective-permute-done.21), channel_id=1, source_target_pairs={{0,4},{1,5},{4,8},{5,9},{8,12},{9,13},{12,14},{13,15},{14,10},{15,... | collective-permute-start | bytes 1228808 | tf_op jit(solution)/shard_map/ppermute | solution.py:78
  301.2 14.9 %collective-permute-start.28 = (bf16[2,64,1600]{2,1,0:T(8,128)(2,1)S(1)}, bf16[2,64,1600]{2,1,0:T(8,128)(2,1)S(1)}, u32[]{:S(2)}, u32[]{:S(2)}) collective-permute-start(bf16[2,64,1600]{2,1,0:T(8,128)(2,1)S(1)} %collective-permute-done.26), channel_id=1, source_target_pairs={{0,1},{1,0},{2,3},{3,2},{4,5},{5,4},{6,7},{7,6},{8,9},{9,8},{10,11... | collective-permute-start | bytes 1228808 | tf_op jit(solution)/shard_map/ppermute | solution.py:78
  393.0 31.3 %collective-permute-start.48 = (bf16[2,64,1600]{2,1,0:T(8,128)(2,1)S(1)}, bf16[2,64,1600]{2,1,0:T(8,128)(2,1)}, u32[]{:S(2)}, u32[]{:S(2)}) collective-permute-start(bf16[2,64,1600]{2,1,0:T(8,128)(2,1)S(1)} %get-tuple-element.103), channel_id=1, source_target_pairs={{0,1},{1,0},{2,3},{3,2},{4,5},{5,4},{6,7},{7,6},{8,9},{9,8},{10,11... | collective-permute-start | bytes 1228808 | tf_op jit(solution)/shard_map/ppermute | solution.py:78
  403.7 20.5 %collective-permute-start.53 = (bf16[2,64,1600]{2,1,0:T(8,128)(2,1)}, bf16[2,64,1600]{2,1,0:T(8,128)(2,1)}, u32[]{:S(2)}, u32[]{:S(2)}) collective-permute-start(bf16[2,64,1600]{2,1,0:T(8,128)(2,1)} %add_convert_fusion.11), channel_id=1, source_target_pairs={{0,2},{1,3},{4,0},{5,1},{8,4},{9,5},{12,8},{13,9},{14,12},{15,13},... | collective-permute-start | bytes 1228808 | tf_op jit(solution)/shard_map/ppermute | solution.py:78
  417.0 48.2 %all-to-all-start.5 = ((bf16[16,100,400]{1,2,0:T(8,128)(2,1)}), bf16[16,100,400]{1,2,0:T(8,128)(2,1)}, u32[]{:S(2)}, u32[]{:S(2)}) async-start(bf16[16,100,400]{1,2,0:T(8,128)(2,1)} %copy.126), calls=%async_computation.5 | async-start | bytes 3276800 | tf_op jit(solution)/shard_map/all_to_all | solution.py:521
  422.5 36.3 %collective-permute-start.47 = (bf16[2,64,1600]{2,1,0:T(8,128)(2,1)S(1)}, bf16[2,64,1600]{2,1,0:T(8,128)(2,1)}, u32[]{:S(2)}, u32[]{:S(2)}) collective-permute-start(bf16[2,64,1600]{2,1,0:T(8,128)(2,1)S(1)} %get-tuple-element.108), channel_id=1, source_target_pairs={{0,4},{1,5},{4,8},{5,9},{8,12},{9,13},{12,14},{13,15},{14,10},{15,... | collective-permute-start | bytes 1228808 | tf_op jit(solution)/shard_map/ppermute | solution.py:78
  425.6 35.2 %collective-permute-start.54 = (bf16[2,64,1600]{2,1,0:T(8,128)(2,1)S(1)}, bf16[2,64,1600]{2,1,0:T(8,128)(2,1)}, u32[]{:S(2)}, u32[]{:S(2)}) collective-permute-start(bf16[2,64,1600]{2,1,0:T(8,128)(2,1)S(1)} %add_convert_fusion.10), channel_id=1, source_target_pairs={{0,2},{1,3},{4,0},{5,1},{8,4},{9,5},{12,8},{13,9},{14,12},{15,13},... | collective-permute-start | bytes 1228808 | tf_op jit(solution)/shard_map/ppermute | solution.py:78
  474.9 37.8 %collective-permute-start.115 = (bf16[100,3200]{1,0:T(8,128)(2,1)}, bf16[100,3200]{1,0:T(8,128)(2,1)}, u32[]{:S(2)}, u32[]{:S(2)}) collective-permute-start(bf16[100,3200]{1,0:T(8,128)(2,1)} %broadcast_select_fusion.2), channel_id=1, source_target_pairs={{0,16},{16,0},{1,17},{17,1},{2,18},{18,2},{3,19},{19,3},{4,20},{20... | collective-permute-start | bytes 1920008 | tf_op jit(solution)/shard_map/ppermute | solution.py:122
  475.7 17.2 %collective-permute-start.112 = (f32[100,128]{1,0:T(8,128)S(1)}, f32[100,128]{1,0:T(8,128)S(1)}, u32[]{:S(2)}, u32[]{:S(2)}) collective-permute-start(f32[100,128]{1,0:T(8,128)S(1)} %fusion.232), channel_id=1, source_target_pairs={{0,4},{1,5},{2,6},{3,7},{4,0},{5,1},{6,2},{7,3},{8,12},{9,13},{10,... | collective-permute-start | bytes 153608 | tf_op jit(solution)/shard_map/ppermute | solution.py:138
  495.6 19.8 %all-to-all-start.3 = ((bf16[128,16,128]{2,0,1:T(8,128)(2,1)}), bf16[128,16,128]{2,0,1:T(8,128)(2,1)S(1)}, u32[]{:S(2)}, u32[]{:S(2)}) async-start(bf16[128,16,128]{2,0,1:T(8,128)(2,1)} %copy.114), calls=%async_computation.3 | async-start | bytes 1048576 | tf_op jit(solution)/shard_map/all_to_all | solution.py:507
  507.9 165.5 %collective-permute-start.93 = (bf16[1600,800]{0,1:T(8,128)(2,1)}, bf16[1600,800]{0,1:T(8,128)(2,1)}, u32[]{:S(2)}, u32[]{:S(2)}) collective-permute-start(bf16[1600,800]{0,1:T(8,128)(2,1)} %select_convert_fusion), channel_id=1, source_target_pairs={{0,16},{16,0},{1,17},{17,1},{2,18},{18,2},{3,19},{19,3},{4,20},{20... | collective-permute-start | bytes 7680008 | tf_op jit(solution)/shard_map/ppermute | solution.py:122
  553.4 194.1 %all-to-all-start.4 = ((bf16[16,100,384]{2,1,0:T(8,128)(2,1)}), bf16[16,100,384]{2,1,0:T(8,128)(2,1)}, u32[]{:S(2)}, u32[]{:S(2)}) async-start(bf16[16,100,384]{2,1,0:T(8,128)(2,1)} %reshape.629), calls=%async_computation.4 | async-start | bytes 2555904 | tf_op jit(solution)/shard_map/all_to_all | solution.py:538
  575.7 47.0 %collective-permute-start.116 = (bf16[400,800]{1,0:T(8,128)(2,1)S(1)}, bf16[400,800]{1,0:T(8,128)(2,1)}, u32[]{:S(2)}, u32[]{:S(2)}) collective-permute-start(bf16[400,800]{1,0:T(8,128)(2,1)S(1)} %select_convert_fusion.1), channel_id=1, source_target_pairs={{0,16},{16,0},{1,17},{17,1},{2,18},{18,2},{3,19},{19,3},{4,20},{20... | collective-permute-start | bytes 1920008 | tf_op jit(solution)/shard_map/ppermute | solution.py:122
  589.8 54.0 %collective-permute-start.66 = (bf16[2,64,1600]{2,1,0:T(8,128)(2,1)}, bf16[2,64,1600]{2,1,0:T(8,128)(2,1)}, u32[]{:S(2)}, u32[]{:S(2)}) collective-permute-start(bf16[2,64,1600]{2,1,0:T(8,128)(2,1)} %get-tuple-element.89), channel_id=1, source_target_pairs={{0,1},{1,0},{2,3},{3,2},{4,5},{5,4},{6,7},{7,6},{8,9},{9,8},{10,11... | collective-permute-start | bytes 1228808 | tf_op jit(solution)/shard_map/ppermute | solution.py:78
  590.0 14.2 %collective-permute-start.59 = (bf16[2,64,1600]{2,1,0:T(8,128)(2,1)}, bf16[2,64,1600]{2,1,0:T(8,128)(2,1)}, u32[]{:S(2)}, u32[]{:S(2)}) collective-permute-start(bf16[2,64,1600]{2,1,0:T(8,128)(2,1)} %get-tuple-element.92), channel_id=1, source_target_pairs={{0,1},{1,0},{2,3},{3,2},{4,5},{5,4},{6,7},{7,6},{8,9},{9,8},{10,11... | collective-permute-start | bytes 1228808 | tf_op jit(solution)/shard_map/ppermute | solution.py:78
  590.3 14.2 %collective-permute-start.58 = (bf16[2,64,1600]{2,1,0:T(8,128)(2,1)}, bf16[2,64,1600]{2,1,0:T(8,128)(2,1)}, u32[]{:S(2)}, u32[]{:S(2)}) collective-permute-start(bf16[2,64,1600]{2,1,0:T(8,128)(2,1)} %get-tuple-element.93), channel_id=1, source_target_pairs={{0,1},{1,0},{2,3},{3,2},{4,5},{5,4},{6,7},{7,6},{8,9},{9,8},{10,11... | collective-permute-start | bytes 1228808 | tf_op jit(solution)/shard_map/ppermute | solution.py:78
  606.4 19.2 %collective-permute-start.57 = (bf16[2,64,1600]{2,1,0:T(8,128)(2,1)S(1)}, bf16[2,64,1600]{2,1,0:T(8,128)(2,1)S(1)}, u32[]{:S(2)}, u32[]{:S(2)}) collective-permute-start(bf16[2,64,1600]{2,1,0:T(8,128)(2,1)S(1)} %copy-done.24), channel_id=1, source_target_pairs={{0,1},{1,0},{2,3},{3,2},{4,5},{5,4},{6,7},{7,6},{8,9},{9,8},{10,11... | collective-permute-start | bytes 1228808 | tf_op jit(solution)/shard_map/ppermute | solution.py:78
  622.7 76.4 %collective-permute-start.65 = (bf16[2,64,1600]{2,1,0:T(8,128)(2,1)}, bf16[2,64,1600]{2,1,0:T(8,128)(2,1)}, u32[]{:S(2)}, u32[]{:S(2)}) collective-permute-start(bf16[2,64,1600]{2,1,0:T(8,128)(2,1)} %get-tuple-element.90), channel_id=1, source_target_pairs={{0,1},{1,0},{2,3},{3,2},{4,5},{5,4},{6,7},{7,6},{8,9},{9,8},{10,11... | collective-permute-start | bytes 1228808 | tf_op jit(solution)/shard_map/ppermute | solution.py:78
  654.9 66.3 %collective-permute-start.64 = (bf16[2,64,1600]{2,1,0:T(8,128)(2,1)}, bf16[2,64,1600]{2,1,0:T(8,128)(2,1)}, u32[]{:S(2)}, u32[]{:S(2)}) collective-permute-start(bf16[2,64,1600]{2,1,0:T(8,128)(2,1)} %get-tuple-element.91), channel_id=1, source_target_pairs={{0,1},{1,0},{2,3},{3,2},{4,5},{5,4},{6,7},{7,6},{8,9},{9,8},{10,11... | collective-permute-start | bytes 1228808 | tf_op jit(solution)/shard_map/ppermute | solution.py:78
  654.9 55.6 %collective-permute-start.81 = (bf16[2,64,1600]{2,1,0:T(8,128)(2,1)}, bf16[2,64,1600]{2,1,0:T(8,128)(2,1)}, u32[]{:S(2)}, u32[]{:S(2)}) collective-permute-start(bf16[2,64,1600]{2,1,0:T(8,128)(2,1)} %get-tuple-element.78), channel_id=1, source_target_pairs={{0,1},{1,0},{2,3},{3,2},{4,5},{5,4},{6,7},{7,6},{8,9},{9,8},{10,11... | collective-permute-start | bytes 1228808 | tf_op jit(solution)/shard_map/ppermute | solution.py:78
  697.9 14.2 %collective-permute-start.84 = (bf16[2,64,1600]{2,1,0:T(8,128)(2,1)S(1)}, bf16[2,64,1600]{2,1,0:T(8,128)(2,1)S(1)}, u32[]{:S(2)}, u32[]{:S(2)}) collective-permute-start(bf16[2,64,1600]{2,1,0:T(8,128)(2,1)S(1)} %pad_maximum_fusion.10), channel_id=1, source_target_pairs={{0,2},{1,3},{4,0},{5,1},{8,4},{9,5},{12,8},{13,9},{14,12},{15,13},... | collective-permute-start | bytes 1228808 | tf_op jit(solution)/shard_map/ppermute | solution.py:78
  706.5 76.6 %collective-permute-start.71 = (bf16[2,64,1600]{2,1,0:T(8,128)(2,1)}, bf16[2,64,1600]{2,1,0:T(8,128)(2,1)}, u32[]{:S(2)}, u32[]{:S(2)}) collective-permute-start(bf16[2,64,1600]{2,1,0:T(8,128)(2,1)} %get-tuple-element.76), channel_id=1, source_target_pairs={{0,1},{1,0},{2,3},{3,2},{4,5},{5,4},{6,7},{7,6},{8,9},{9,8},{10,11... | collective-permute-start | bytes 1228808 | tf_op jit(solution)/shard_map/ppermute | solution.py:78
  714.9 29.6 %collective-permute-start.80 = (bf16[2,64,1600]{2,1,0:T(8,128)(2,1)S(1)}, bf16[2,64,1600]{2,1,0:T(8,128)(2,1)S(1)}, u32[]{:S(2)}, u32[]{:S(2)}) collective-permute-start(bf16[2,64,1600]{2,1,0:T(8,128)(2,1)S(1)} %copy-done.22), channel_id=1, source_target_pairs={{0,1},{1,0},{2,3},{3,2},{4,5},{5,4},{6,7},{7,6},{8,9},{9,8},{10,11... | collective-permute-start | bytes 1228808 | tf_op jit(solution)/shard_map/ppermute | solution.py:78
  721.2 23.7 %collective-permute-start.85 = (bf16[2,64,1600]{2,1,0:T(8,128)(2,1)S(1)}, bf16[2,64,1600]{2,1,0:T(8,128)(2,1)S(1)}, u32[]{:S(2)}, u32[]{:S(2)}) collective-permute-start(bf16[2,64,1600]{2,1,0:T(8,128)(2,1)S(1)} %add_convert_fusion.3), channel_id=1, source_target_pairs={{0,2},{1,3},{4,0},{5,1},{8,4},{9,5},{12,8},{13,9},{14,12},{15,13},... | collective-permute-start | bytes 1228808 | tf_op jit(solution)/shard_map/ppermute | solution.py:78
  734.0 49.6 %collective-permute-start.79 = (bf16[2,64,1600]{2,1,0:T(8,128)(2,1)}, bf16[2,64,1600]{2,1,0:T(8,128)(2,1)}, u32[]{:S(2)}, u32[]{:S(2)}) collective-permute-start(bf16[2,64,1600]{2,1,0:T(8,128)(2,1)} %get-tuple-element.84), channel_id=1, source_target_pairs={{0,4},{1,5},{4,8},{5,9},{8,12},{9,13},{12,14},{13,15},{14,10},{15,... | collective-permute-start | bytes 1228808 | tf_op jit(solution)/shard_map/ppermute | solution.py:78
  742.7 23.0 %collective-permute-start.94 = (bf16[2,50,800]{2,1,0:T(8,128)(2,1)S(1)}, bf16[2,50,800]{2,1,0:T(8,128)(2,1)}, u32[]{:S(2)}, u32[]{:S(2)}) collective-permute-start(bf16[2,50,800]{2,1,0:T(8,128)(2,1)S(1)} %get-tuple-element.112), channel_id=1, source_target_pairs={{0,1},{1,0},{2,3},{3,2},{4,5},{5,4},{6,7},{7,6},{8,9},{9,8},{10,11... | collective-permute-start | bytes 480008 | tf_op jit(solution)/shard_map/ppermute | solution.py:78
  744.4 18.1 %collective-permute-start.103 = (bf16[2,50,800]{2,1,0:T(8,128)(2,1)}, bf16[2,50,800]{2,1,0:T(8,128)(2,1)}, u32[]{:S(2)}, u32[]{:S(2)}) collective-permute-start(bf16[2,50,800]{2,1,0:T(8,128)(2,1)} %get-tuple-element.115), channel_id=1, source_target_pairs={{0,1},{1,0},{2,3},{3,2},{4,5},{5,4},{6,7},{7,6},{8,9},{9,8},{10,11... | collective-permute-start | bytes 480008 | tf_op jit(solution)/shard_map/ppermute | solution.py:78
  744.9 19.1 %collective-permute-start.108 = (bf16[2,50,800]{2,1,0:T(8,128)(2,1)}, bf16[2,50,800]{2,1,0:T(8,128)(2,1)}, u32[]{:S(2)}, u32[]{:S(2)}) collective-permute-start(bf16[2,50,800]{2,1,0:T(8,128)(2,1)} %add_convert_fusion.25), channel_id=1, source_target_pairs={{0,2},{1,3},{4,0},{5,1},{8,4},{9,5},{12,8},{13,9},{14,12},{15,13},... | collective-permute-start | bytes 480008 | tf_op jit(solution)/shard_map/ppermute | solution.py:78
  764.0 20.9 %collective-permute-start.86 = (bf16[2,64,1600]{2,1,0:T(8,128)(2,1)}, bf16[2,64,1600]{2,1,0:T(8,128)(2,1)}, u32[]{:S(2)}, u32[]{:S(2)}) collective-permute-start(bf16[2,64,1600]{2,1,0:T(8,128)(2,1)} %add_convert_fusion.2), channel_id=1, source_target_pairs={{0,2},{1,3},{4,0},{5,1},{8,4},{9,5},{12,8},{13,9},{14,12},{15,13},... | collective-permute-start | bytes 1228808 | tf_op jit(solution)/shard_map/ppermute | solution.py:78
  765.8 14.0 %collective-permute-start.109 = (bf16[2,50,800]{2,1,0:T(8,128)(2,1)S(1)}, bf16[2,50,800]{2,1,0:T(8,128)(2,1)S(1)}, u32[]{:S(2)}, u32[]{:S(2)}) collective-permute-start(bf16[2,50,800]{2,1,0:T(8,128)(2,1)S(1)} %add_convert_fusion.24), channel_id=1, source_target_pairs={{0,2},{1,3},{4,0},{5,1},{8,4},{9,5},{12,8},{13,9},{14,12},{15,13},... | collective-permute-start | bytes 480008 | tf_op jit(solution)/shard_map/ppermute | solution.py:78
  769.4 17.8 %collective-permute-start.55 = (bf16[2,64,1600]{2,1,0:T(8,128)(2,1)}, bf16[2,64,1600]{2,1,0:T(8,128)(2,1)}, u32[]{:S(2)}, u32[]{:S(2)}) collective-permute-start(bf16[2,64,1600]{2,1,0:T(8,128)(2,1)} %get-tuple-element.88), channel_id=1, source_target_pairs={{0,1},{1,0},{2,3},{3,2},{4,5},{5,4},{6,7},{7,6},{8,9},{9,8},{10,11... | collective-permute-start | bytes 1228808 | tf_op jit(solution)/shard_map/ppermute | solution.py:78
  783.7 27.8 %collective-permute-start.92 = (bf16[100,2400]{1,0:T(8,128)(2,1)}, bf16[100,2400]{1,0:T(8,128)(2,1)}, u32[]{:S(2)}, u32[]{:S(2)}) collective-permute-start(bf16[100,2400]{1,0:T(8,128)(2,1)} %copy.122), channel_id=1, source_target_pairs={{0,16},{16,0},{1,17},{17,1},{2,18},{18,2},{3,19},{19,3},{4,20},{20... | collective-permute-start | bytes 1440008 | tf_op jit(solution)/shard_map/ppermute | solution.py:122
  (124 other events, 1402.1 us)
Sparse Core Ops, SparseCore 0:
  84.0 76.4 all-gather.6
  191.8 99.9 all-gather.4

commit v2 on v1

v2 whole, which is shorter than its diff:
```python
import functools
import math

import jax
import jax.numpy as jnp
from jax import lax
from jax.experimental import pallas as pl
from jax.experimental.pallas import tpu as pltpu
from jax.sharding import PartitionSpec as P

HEADS = 25
HEAD_DIM = 64
SLOT = 2 * HEAD_DIM

EPSILON = 1e-05
GELU_ROOT = math.sqrt(2.0 / math.pi)
GELU_CUBIC = 0.044715
NEG_LARGE = -1e30
SCALE = HEAD_DIM ** (-0.5)
VMEM_LIMIT = 56 * 1024 * 1024
F32 = jnp.float32
BF16 = jnp.bfloat16


def norm_stats(values):
    centred = values - jnp.mean(values, axis=-1, keepdims=True)
    inv_std = lax.rsqrt(jnp.mean(centred * centred, axis=-1, keepdims=True) + EPSILON)
    return centred * inv_std, inv_std


def norm_back(upstream, normed, inv_std, gain_vec):
    scaled = upstream * gain_vec
    return inv_std * (
        scaled
        - jnp.mean(scaled, axis=-1, keepdims=True)
        - normed * jnp.mean(scaled * normed, axis=-1, keepdims=True)
    )


def gelu_pair(pre_act):
    inner = GELU_ROOT * (pre_act + GELU_CUBIC * pre_act * pre_act * pre_act)
    tangent = jnp.tanh(inner)
    act_value = 0.5 * pre_act * (1.0 + tangent)
    act_slope = 0.5 * (1.0 + tangent) + 0.5 * pre_act * (1.0 - tangent * tangent) * GELU_ROOT * (
        1.0 + 3.0 * GELU_CUBIC * pre_act * pre_act
    )
    return (act_value, act_slope)


class Ring:
    def __init__(self, count):
        chips = count // 2
        self.count, self.size, self.far = count, chips, chips // 2
        self.mine = lax.axis_index("context")
        self.core = self.mine % 2
        chip = self.mine // 2
        if chips == 8:
            order = [0, 2, 4, 6, 7, 5, 3, 1]
            self.place = jnp.where(chip % 2 == 0, chip // 2, (15 - chip) // 2)
        else:
            order = list(range(chips))
            self.place = chip
        self.spot = jnp.stack([self.place, self.core]).astype(jnp.int32)
        self.links = []
        for i in range(chips):
            self.links.append((2 * order[i], 2 * order[(i + 1) % chips]))
            self.links.append((2 * order[i] + 1, 2 * order[(i - 1) % chips] + 1))
        self.swaps = [(i, i ^ 1) for i in range(count)]

    def layout(self):
        steps = [[(0, None)]] + [[(step, None), (-step, None)] for step in range(1, self.far)]
        return steps + [[(self.far, 0), (self.far, 1)]]

    def swap(self, value):
        return lax.ppermute(value, "context", self.swaps)

    def send(self, value):
        return lax.ppermute(value, "context", self.links)

    def own(self, value, other=0):
        rows = value.shape[0] // 2
        return lax.dynamic_slice_in_dim(value, (self.core ^ other) * rows, rows)

    def gather(self, block, visit, hold=None):
        other = self.swap(block)
        current = jnp.concatenate(
            [jnp.where(self.core == 0, block, other), jnp.where(self.core == 0, other, block)], axis=0
        )
        events = [visit(0, [current])]
        for step in range(1, self.far + 1):
            if step == self.far:
                current = self.own(current)
            if step >= 2:
                current = after(current, events[step - 2])
            if hold is not None:
                current = hold(step, current)
            current = self.send(current)
            events.append(visit(step, [current, self.swap(current)]))

    def pick(self, array):
        cut = array.shape[1] // 2
        steps = []
        for entries in self.layout():
            blocks = []
            for offset, other in entries:
                first, size = (0, 2 * cut) if other is None else ((self.core ^ other) * cut, cut)
                chip = device_at(self.size, self.spot, offset, None) // 2
                blocks.append(lax.dynamic_slice(array, (chip, first, 0), (1, size, array.shape[2]))[0])
            steps.append(blocks)
        return steps

    def scatter(self, give, hold=None):
        sent = None
        for step in range(self.far, 0, -1):
            first, second = give(step, sent)
            if step == self.far:
                value = total([first, self.swap(second)])
            else:
                value = total([second, self.swap(first)])
            if step == self.far - 1:
                got = got.astype(F32)
                blank = jnp.zeros_like(got)
                value = value + jnp.concatenate(
                    [jnp.where(self.core == 0, got, blank), jnp.where(self.core == 0, blank, got)], axis=0
                )
            elif step < self.far - 1:
                value = value + got.astype(F32)
            sent = value.astype(BF16)
            if hold is not None:
                sent = hold(step, sent)
            got = self.send(sent)
        value = total([give(0, sent)[0], got])
        return self.own(value) + self.swap(self.own(value, 1).astype(BF16)).astype(F32)


def device_at(size, spot, offset, other):
    place, core = spot[0], spot[1]
    at = lax.rem(place + offset * (2 * core - 1) + size, size)
    chip = jnp.where(at < 4, 2 * at, 15 - 2 * at) if size == 8 else at
    return 2 * chip if other is None else 2 * chip + (core ^ other)


def wide(value, axis=-1):
    axis %= value.ndim
    more = -value.shape[axis] % 128
    return jnp.pad(value, [(0, more if i == axis else 0) for i in range(value.ndim)])


def total(values):
    result = values[0].astype(F32)
    for value in values[1:]:
        result = result + value.astype(F32)
    return result


def after(value, *events):
    return lax.optimization_barrier((value,) + events)[0]


def cross(value):
    return lax.ppermute(value, "fsdp", [(0, 1), (1, 0)])


def pair_halves(own, side):
    got = cross(own)
    return jnp.where(side == 0, own, got), jnp.where(side == 0, got, own)


def pair_sum(left, right, side):
    got = cross(jnp.where(side == 0, right, left).astype(BF16))
    return jnp.where(side == 0, left, right).astype(F32) + got.astype(F32)


def sum_everywhere(value, count):
    step = 1
    while step < count:
        value = value + lax.ppermute(value, "context", [(i, i ^ step) for i in range(count)])
        step *= 2
    return value + cross(value)


def even_rows(value, axis=0):
    odd = value.shape[axis] % 2
    if not odd:
        return value
    return jnp.pad(value, [(0, odd if i == axis else 0) for i in range(value.ndim)])


def spread(value):
    return lax.all_to_all(value, "context", 0, 0, tiled=True)


def start_fc(w_fc, side, count, share):
    w_fc = even_rows(w_fc)
    cut = w_fc.shape[0] // 2
    mine, got = w_fc[:cut], cross(w_fc[cut:])
    blocks = jnp.concatenate([jnp.where(side == 0, mine, got), jnp.where(side == 0, got, mine)], axis=1)
    return blocks.reshape(cut, count, share).transpose(1, 0, 2)


def finish_fc(landed, side, upper, rows):
    other = cross(landed)
    is_first = upper == side
    both = jnp.concatenate(
        [jnp.where(is_first, landed, other), jnp.where(is_first, other, landed)], axis=1
    )
    return both[:, :rows].reshape(landed.shape[0] * rows, landed.shape[2])


def return_fc(grad, side, upper, count, share, rows):
    grad = even_rows(grad.reshape(count, rows, share), 1)
    cut = grad.shape[1] // 2
    first, second = grad[:, :cut], grad[:, cut:]
    is_first = upper == side
    got = cross(jnp.where(is_first, second, first))
    landed = spread(total([jnp.where(is_first, first, second), got]).astype(BF16))
    low, high = landed[: count // 2], landed[count // 2 :]
    mine, got = jnp.where(side == 0, low, high), cross(jnp.where(side == 0, high, low))
    both = jnp.concatenate([mine, got], axis=1).astype(F32).transpose(1, 0, 2)
    return both.reshape(2 * cut, count // 2 * share)[:rows]


def start_heads(w_qkv, side, count):
    rows, width = w_qkv.shape[0], w_qkv.shape[1] * 2 // 3
    half = width // 2
    main = jnp.where(side == 0, w_qkv[:, :width], w_qkv[:, half:])
    keys = even_rows(jnp.where(side == 0, w_qkv[:, width:], w_qkv[:, :half]))
    cut = keys.shape[0] // 2
    first, second = keys[:cut], keys[cut:]
    got = cross(jnp.where(side == 0, second, first))
    keys = jnp.concatenate([jnp.where(side == 0, first, got), jnp.where(side == 0, got, second)], axis=1)
    blocks = jnp.pad(jnp.concatenate([main, keys], axis=0), ((0, 0), (0, count * SLOT - width)))
    return blocks.reshape(rows + cut, count, SLOT).transpose(1, 0, 2)


def finish_heads(landed, side, rows, width):
    other = cross(landed)
    one, two = jnp.where(side == 0, landed, other), jnp.where(side == 0, other, landed)
    keys = jnp.concatenate([one[:, rows:], two[:, rows:]], axis=1)[:, :rows]
    heads = jnp.concatenate([one[:, :rows], keys, two[:, :rows]], axis=2)
    return heads.reshape(width, 3 * SLOT)


def return_heads(grad, side, count, rows, width):
    half = width // 2
    grad = grad.reshape(count, rows, 3 * SLOT)
    keys = even_rows(grad[:, :, SLOT : 2 * SLOT], 1)
    cut = keys.shape[1] // 2
    one = jnp.concatenate([grad[:, :, :SLOT], keys[:, :cut]], axis=1)
    two = jnp.concatenate([grad[:, :, 2 * SLOT :], keys[:, cut:]], axis=1)
    got = cross(jnp.where(side == 0, two, one))
    landed = spread(total([jnp.where(side == 0, one, two), got]).astype(BF16))
    landed = landed.transpose(1, 0, 2).reshape(rows + cut, count * SLOT)[:, :width]
    main, keys = landed[:rows], landed[rows:]
    low, high = keys[:, :half], keys[:, half:]
    got, own = cross(jnp.where(side == 0, high, low)), jnp.where(side == 0, low, high)
    keys = jnp.concatenate([jnp.where(side == 0, own, got), jnp.where(side == 0, got, own)], axis=0)[:rows]
    return jnp.where(
        side == 0, jnp.concatenate([main, keys], axis=1), jnp.concatenate([keys, main], axis=1)
    ).astype(F32)


def dot_nt(first, second):
    return lax.dot_general(first, second, (((1,), (1,)), ((), ())), preferred_element_type=F32)


def dot_nn(first, second):
    return lax.dot_general(first, second, (((1,), (0,)), ((), ())), preferred_element_type=F32)


def dot_tn(first, second):
    return lax.dot_general(first, second, (((0,), (0,)), ((), ())), preferred_element_type=F32)


VMEM_SPEC = pl.BlockSpec(memory_space=pltpu.VMEM)
SMEM_SPEC = pl.BlockSpec(memory_space=pltpu.SMEM)
ANY_SPEC = pl.BlockSpec(memory_space=pl.ANY)


def local_call(kernel, name, outs, ins, args, flops, scratch=(), exps=0):
    moved = sum(math.prod(x.shape) * x.dtype.itemsize for x in list(args) + list(outs))
    return pl.pallas_call(
        kernel,
        out_shape=tuple(outs),
        in_specs=list(ins),
        out_specs=tuple(VMEM_SPEC for _ in outs),
        scratch_shapes=list(scratch),
        compiler_params=pltpu.CompilerParams(vmem_limit_bytes=VMEM_LIMIT),
        cost_estimate=pl.CostEstimate(flops=flops, bytes_accessed=moved, transcendentals=exps),
        name=name,
    )(*args)


def shape_of(rows, cols, kind):
    return jax.ShapeDtypeStruct((rows, cols), kind)


def norm_blocks(blocks, gain, shift, width):
    count = len(blocks)

    def kernel(*refs):
        ins, gain_ref, shift_ref, outs = refs[:count], refs[count], refs[count + 1], refs[count + 2 :]
        for i in range(count):
            values = ins[i][...].astype(F32)
            lane = lax.broadcasted_iota(jnp.int32, (1, values.shape[1]), 1)
            centred = values - jnp.sum(values, axis=-1, keepdims=True) * (1.0 / width)
            centred = jnp.where(lane < width, centred, 0.0)
            spread_of = jnp.sum(centred * centred, axis=-1, keepdims=True) * (1.0 / width)
            normed = centred * lax.rsqrt(spread_of + EPSILON)
            outs[i][...] = (normed * gain_ref[...] + shift_ref[...]).astype(BF16)
            outs[count + i][...] = normed.astype(BF16)

    outs = [jax.ShapeDtypeStruct(x.shape, BF16) for x in blocks] * 2
    args = list(blocks) + [gain, shift]
    size = sum(x.size for x in blocks)
    result = local_call(kernel, "norm_blocks", outs, [VMEM_SPEC] * len(args), args, 10 * size)
    return list(result[:count]), list(result[count:])


def feed_blocks(spot, blocks, cot_all, w_fc, w_proj, bias, size, entries):
    count, (width, share) = len(blocks), w_fc.shape
    sizes = [x.shape[0] for x in blocks]
    rows = sum(sizes)
    unit = sizes[0] // 2 if entries[0][1] is None else sizes[0]

    def kernel(*refs):
        spot_ref, cot_ref, h_refs = refs[0], refs[1], refs[2 : 2 + count]
        fc_ref, proj_ref, bias_ref, act_ref, du_ref, sum_ref = refs[2 + count : 8 + count]
        outs, cots, sems = refs[8 + count : -2], refs[-2], refs[-1]
        copies, at = [], 0
        for i, (offset, other) in enumerate(entries):
            device = device_at(size, spot_ref, offset, other)
            rows_there = pl.ds(pl.multiple_of(device * unit, unit), sizes[i])
            copy = pltpu.make_async_copy(cot_ref.at[rows_there, :], cots.at[pl.ds(at, sizes[i]), :], sems.at[i])
            copy.start()
            copies.append(copy)
            at += sizes[i]
        rows_in = jnp.concatenate([h_refs[i][...] for i in range(count)], axis=0)
        act, slope = gelu_pair(dot_nn(rows_in, fc_ref[...]) + bias_ref[...])
        act_ref[...] = act.astype(BF16)
        for copy in copies:
            copy.wait()
        grad = dot_nt(cots[...], proj_ref[...]) * slope
        sum_ref[...] = jnp.sum(grad, axis=0, keepdims=True)
        grad = grad.astype(BF16)
        du_ref[...] = grad
        terms = dot_nt(grad, fc_ref[...]).astype(BF16)
        at = 0
        for i in range(count):
            outs[i][...] = terms[at : at + sizes[i]]
            at += sizes[i]

    outs = [shape_of(rows, share, BF16), shape_of(rows, share, BF16), shape_of(1, share, F32)]
    outs += [shape_of(size, width, BF16) for size in sizes]
    args = [spot, cot_all] + list(blocks) + [w_fc, w_proj, bias]
    ins = [SMEM_SPEC, ANY_SPEC] + [VMEM_SPEC] * (count + 3)
    scratch = [pltpu.VMEM((rows, width), BF16), pltpu.SemaphoreType.DMA((count,))]
    result = local_call(
        kernel, "feed_blocks", outs, ins, args, 6 * rows * width * share, scratch, rows * share
    )
    return result[0], result[1], result[2], list(result[3:])


def project_blocks(act, w_proj, sizes):
    width = w_proj.shape[1]

    def kernel(act_ref, proj_ref, *outs):
        terms = dot_nn(act_ref[...], proj_ref[...]).astype(BF16)
        at = 0
        for i, size in enumerate(sizes):
            outs[i][...] = terms[at : at + size]
            at += size

    outs = [shape_of(size, width, BF16) for size in sizes]
    result = local_call(
        kernel, "project_blocks", outs, [VMEM_SPEC] * 2, [act, w_proj], 2 * act.size * width
    )
    return list(result)


def input_blocks(grad, w_heads, normed):
    count, width = len(normed), w_heads.shape[0]
    sizes = [x.shape[0] for x in normed]

    def kernel(*refs):
        grad_ref, w_ref, n_refs, sum_ref, outs = refs[0], refs[1], refs[2 : 2 + count], refs[2 + count], refs[3 + count :]
        terms = dot_nt(grad_ref[...], w_ref[...])
        gains = jnp.zeros((1, width), F32)
        at = 0
        for i, size in enumerate(sizes):
            term = terms[at : at + size]
            at += size
            outs[i][...] = term.astype(BF16)
            gains += jnp.sum(term * n_refs[i][...].astype(F32), axis=0, keepdims=True)
        sum_ref[0:1, :] = gains
        sum_ref[1:2, :] = jnp.sum(terms, axis=0, keepdims=True)

    outs = [shape_of(2, width, F32)] + [shape_of(size, width, BF16) for size in sizes]
    args = [grad, w_heads] + list(normed)
    result = local_call(
        kernel, "input_blocks", outs, [VMEM_SPEC] * len(args), args, 2 * grad.size * width
    )
    return result[0], list(result[1:])


def pack(spot, groups, layout, size, seq):
    flat, plan = [], []
    for index, steps in enumerate(groups):
        for blocks, entries in zip(steps, layout):
            blocks = blocks if isinstance(blocks, list) else [blocks]
            at = 0
            for i, (offset, other) in enumerate(entries):
                rows = 2 * seq // (2 * size) if other is None else seq // (2 * size)
                if len(blocks) == len(entries):
                    plan.append((index, len(flat) + i, 0, rows, offset, other))
                else:
                    plan.append((index, len(flat), at, rows, offset, other))
                at += rows
            flat += blocks
    unit = seq // (2 * size)

    def kernel(*refs):
        spot_ref, ins = refs[0], refs[1 : 1 + len(flat)]
        outs, sems = refs[1 + len(flat) : -1], refs[-1]
        copies = []
        for i, (index, source, first, rows, offset, other) in enumerate(plan):
            device = device_at(size, spot_ref, offset, other)
            there = pl.ds(pl.multiple_of(device * unit, unit), rows)
            copy = pltpu.make_async_copy(
                ins[source].at[pl.ds(first, rows), :], outs[index].at[there, :], sems.at[i]
            )
            copy.start()
            copies.append(copy)
        for copy in copies:
            copy.wait()

    outs = []
    for steps in groups:
        sample = steps[0][0] if isinstance(steps[0], list) else steps[0]
        outs.append(shape_of(seq, sample.shape[1], sample.dtype))
    moved = sum(2 * math.prod(x.shape) * x.dtype.itemsize for x in outs)
    return pl.pallas_call(
        kernel,
        out_shape=tuple(outs),
        in_specs=[SMEM_SPEC] + [ANY_SPEC] * len(flat),
        out_specs=tuple(VMEM_SPEC for _ in outs),
        scratch_shapes=[pltpu.SemaphoreType.DMA((len(plan),))],
        compiler_params=pltpu.CompilerParams(vmem_limit_bytes=VMEM_LIMIT),
        cost_estimate=pl.CostEstimate(flops=0, bytes_accessed=moved, transcendentals=0),
        name="pack",
    )(spot, *flat)


def head_masks(scale):
    lane = lax.broadcasted_iota(jnp.int32, (1, SLOT), 1)
    return [jnp.where(lane < HEAD_DIM, scale, 0.0), jnp.where(lane < HEAD_DIM, 0.0, scale)]


def flipped(value):
    return value.astype(F32).T


def causal(tile):
    keys = lax.broadcasted_iota(jnp.int32, (tile, tile), 0)
    queries = lax.broadcasted_iota(jnp.int32, (tile, tile), 1)
    return keys <= queries


def span(index, size):
    return pl.ds(pl.multiple_of(index * size, size), size)


def tile_of(seq):
    return math.gcd(seq, 512)


def attend_forward(order, spot, blocks, w_heads, bias, layout, blk):
    size = len(layout) - 1
    chips = 2 * size
    seq = 4 * chips * blk
    width = w_heads.shape[0]
    tile = tile_of(seq)
    tiles = seq // tile
    flat = [(step, entry) for step, entries in enumerate(layout) for entry in entries]
    pieces = len(flat)

    def kernel(*refs):
        order_ref, spot_ref = refs[:2]
        h_refs = refs[2 : 2 + pieces]
        w_ref, bias_ref, o_ref, lse_ref, qs, ks, vs, held, vt, os, sems = refs[2 + pieces :]
        masks = head_masks(SCALE)
        copies, starts, at = [], [], 0
        for i in range(pieces):
            rows = h_refs[i].shape[0]
            copy = pltpu.make_async_copy(h_refs[i], held.at[pl.ds(at, rows), :], sems.at[i])
            copy.start()
            copies.append(copy)
            starts.append(at)
            at += rows

        index = 0
        for step, entries in enumerate(layout):
            first = starts[index]
            for i in range(len(entries)):
                copies[index + i].wait()
            rows = sum(h_refs[index + i].shape[0] for i in range(len(entries)))
            mixed = dot_nn(held[first : first + rows, :], w_ref[...]) + bias_ref[...]
            for i, (offset, other) in enumerate(entries):
                base = starts[index + i] - first
                device = device_at(chips, spot_ref, offset, other)
                for part in range(4 if other is None else 2):
                    there = span(order_ref[2 * device + part], blk)
                    block = mixed[base : base + blk].astype(BF16)
                    base += blk
                    query = block[:, :SLOT].astype(F32)
                    for head in range(2):
                        qs[head, there, :] = (query * masks[head]).astype(BF16)
                    ks[there, :] = block[:, SLOT : 2 * SLOT]
                    vs[there, :] = block[:, 2 * SLOT :]
            index += len(entries)

        def turn(t, carry):
            vt[t] = flipped(vs[span(t, tile), :]).astype(BF16)
            return carry

        lax.fori_loop(0, tiles, turn, 0)
        visible = causal(tile)

        def query_tile(i, carry):
            def key_tile(j, state, diagonal):
                fresh = []
                for head in range(2):
                    top, sums, accum = state[3 * head : 3 * head + 3]
                    scores = dot_nt(ks[span(j, tile), :], qs[head, span(i, tile), :])
                    if diagonal:
                        scores = jnp.where(visible, scores, NEG_LARGE)
                    new_top = jnp.maximum(top, jnp.max(scores, axis=0, keepdims=True))
                    terms = jnp.exp(scores - new_top)
                    decay = jnp.exp(top - new_top)
                    sums = sums * decay + jnp.sum(terms, axis=0, keepdims=True)
                    values = vt[j, head * HEAD_DIM : (head + 1) * HEAD_DIM, :]
                    accum = accum * decay + dot_nn(values, terms.astype(BF16))
                    fresh += [new_top, sums, accum]
                return tuple(fresh)

            start = (
                jnp.full((1, tile), NEG_LARGE, F32),
                jnp.zeros((1, tile), F32),
                jnp.zeros((HEAD_DIM, tile), F32),
            )
            state = lax.fori_loop(0, i, lambda j, state: key_tile(j, state, False), start + start)
            state = key_tile(i, state, True)
            mixed = jnp.concatenate([state[2] / state[1], state[5] / state[4]], axis=0)
            os[span(i, tile), :] = mixed.T.astype(BF16)
            for head in range(2):
                lse_ref[i, head : head + 1, :] = state[3 * head] + jnp.log(state[3 * head + 1])
            return carry

        lax.fori_loop(0, tiles, query_tile, 0)

        def sort_out(s, carry):
            o_ref[span(s, blk), :] = os[span(order_ref[s], blk), :]
            return carry

        lax.fori_loop(0, seq // blk, sort_out, 0)

    outs = [
        shape_of(seq, SLOT, BF16),
        jax.ShapeDtypeStruct((tiles, 8, tile), F32),
        jax.ShapeDtypeStruct((2, seq, SLOT), BF16),
        shape_of(seq, SLOT, BF16),
        shape_of(seq, SLOT, BF16),
    ]
    scratch = [
        pltpu.VMEM((seq, width), BF16),
        pltpu.VMEM((tiles, SLOT, tile), BF16),
        pltpu.VMEM((seq, SLOT), BF16),
        pltpu.SemaphoreType.DMA((pieces,)),
    ]
    args = [order, spot] + [block for step in blocks for block in step] + [w_heads, bias]
    ins = [SMEM_SPEC] * 2 + [ANY_SPEC] * pieces + [VMEM_SPEC] * 2
    flops = 4 * seq * seq * SLOT + 6 * seq * width * SLOT
    return local_call(kernel, "attend_forward", outs, ins, args, flops, scratch, seq * seq)


def attend_backward(order, spot, saved, grads, mixed, lse, layout, blk):
    queries, keys, values = saved
    seq = keys.shape[0]
    chips = 2 * (len(layout) - 1)
    tile = tile_of(seq)
    tiles = seq // tile
    steps = len(layout)

    def kernel(order_ref, spot_ref, qs, ks, vs, g_ref, o_ref, lse_ref, sum_ref, *refs):
        d_refs = refs[:steps]
        gs, ps, kt, dqt, drow, dk, dv, dsort = refs[steps:]
        g_masks = head_masks(1.0)

        def sort_in(s, carry):
            here, there = span(s, blk), span(order_ref[s], blk)
            g_block = g_ref[here, :].astype(F32)
            for head in range(2):
                gs[head, there, :] = (g_block * g_masks[head]).astype(BF16)
            ps[there, :] = g_block * o_ref[here, :].astype(F32)
            return carry

        lax.fori_loop(0, seq // blk, sort_in, 0)

        def turn(t, carry):
            kt[t] = flipped(ks[span(t, tile), :]).astype(BF16)
            products = ps[span(t, tile), :].T
            for head in range(2):
                drow[t, head : head + 1, :] = jnp.sum(
                    products[head * HEAD_DIM : (head + 1) * HEAD_DIM], axis=0, keepdims=True
                )
            dqt[t] = jnp.zeros((SLOT, tile), F32)
            return carry

        lax.fori_loop(0, tiles, turn, 0)
        visible = causal(tile)
        sum_ref[...] = jnp.zeros(sum_ref.shape, F32)

        def key_tile(j, carry):
            dk[...] = jnp.zeros(dk.shape, F32)
            dv[...] = jnp.zeros(dv.shape, F32)

            def query_tile(i, diagonal):
                key_add, value_add = [], []
                for head in range(2):
                    scores = dot_nt(ks[span(j, tile), :], qs[head, span(i, tile), :])
                    terms = jnp.exp(scores - lse_ref[i, head : head + 1, :])
                    if diagonal:
                        terms = jnp.where(visible, terms, 0.0)
                    slopes = dot_nt(vs[span(j, tile), :], gs[head, span(i, tile), :])
                    slopes = (terms * (slopes - drow[i, head : head + 1, :])).astype(BF16)
                    value_add.append(dot_nn(terms.astype(BF16), gs[head, span(i, tile), :]))
                    key_add.append(dot_nn(slopes, qs[head, span(i, tile), :]))
                    rows = slice(head * HEAD_DIM, (head + 1) * HEAD_DIM)
                    dqt[i, rows, :] += dot_nn(kt[j, rows, :], slopes)
                dk[...] += key_add[0] + key_add[1]
                dv[...] += value_add[0] + value_add[1]

            query_tile(j, True)

            def later(i, carry):
                query_tile(i, False)
                return carry

            lax.fori_loop(j + 1, tiles, later, 0)
            dsort[1, span(j, tile), :] = dk[...].astype(BF16)
            dsort[2, span(j, tile), :] = dv[...].astype(BF16)
            sum_ref[1:2, :] += jnp.sum(dv[...], axis=0, keepdims=True)
            return carry

        lax.fori_loop(0, tiles, key_tile, 0)

        def finish(t, carry):
            query_grad = dqt[t].T * SCALE
            dsort[0, span(t, tile), :] = query_grad.astype(BF16)
            sum_ref[0:1, :] += jnp.sum(query_grad, axis=0, keepdims=True)
            return carry

        lax.fori_loop(0, tiles, finish, 0)

        for step, entries in enumerate(layout):
            base = 0
            for offset, other in entries:
                device = device_at(chips, spot_ref, offset, other)
                for part in range(4 if other is None else 2):
                    there = span(order_ref[2 * device + part], blk)
                    for kind in range(3):
                        d_refs[step][base : base + blk, kind * SLOT : (kind + 1) * SLOT] = dsort[kind, there, :]
                    base += blk

    outs = [shape_of(8, SLOT, F32)]
    for entries in layout:
        rows = sum(4 * blk if other is None else 2 * blk for _, other in entries)
        outs.append(shape_of(rows, 3 * SLOT, BF16))
    scratch = [
        pltpu.VMEM((2, seq, SLOT), BF16),
        pltpu.VMEM((seq, SLOT), F32),
        pltpu.VMEM((tiles, SLOT, tile), BF16),
        pltpu.VMEM((tiles, SLOT, tile), F32),
        pltpu.VMEM((tiles, 8, tile), F32),
        pltpu.VMEM((tile, SLOT), F32),
        pltpu.VMEM((tile, SLOT), F32),
        pltpu.VMEM((3, seq, SLOT), BF16),
    ]
    args = [order, spot, queries, keys, values, grads, mixed, lse]
    ins = [SMEM_SPEC] * 2 + [VMEM_SPEC] * 6
    result = local_call(
        kernel, "attend_backward", outs, ins, args, 10 * seq * seq * SLOT, scratch, seq * seq
    )
    return list(result[1:]), result[0]


def body(
    tokens,
    cotangent,
    block_order,
    ln1_gain,
    ln1_bias,
    w_qkv,
    qv_bias,
    w_out,
    out_bias,
    ln2_gain,
    ln2_bias,
    w_fc,
    fc_bias,
    w_proj,
    proj_bias,
):
    width = HEADS * HEAD_DIM
    half = width // 2
    count = lax.axis_size("context")
    rows = tokens.shape[1]
    seq = count * rows
    blk = rows // 2
    hidden = fc_bias.shape[0] * 2
    share = hidden // count
    own_rows = w_qkv.shape[0]
    padded = count * SLOT
    grad_scale = 1.0 / math.sqrt(lax.axis_size("fsdp") * seq)
    side = lax.axis_index("fsdp")
    ring = Ring(count)
    mine, layout, far = ring.mine, ring.layout(), ring.far
    upper = mine // (count // 2)
    order = block_order.astype(jnp.int32)
    spot = ring.spot
    sizes = [[2 * rows if other is None else rows for _, other in entries] for entries in layout]

    vectors = jnp.concatenate(
        [
            jnp.stack(
                [ln1_gain, ln1_bias, qv_bias[:, 0], qv_bias[:, 1], out_bias, ln2_gain, ln2_bias, proj_bias]
            ),
            fc_bias.reshape(-1, half),
        ],
        axis=0,
    )
    low, high = pair_halves(vectors, side)
    rows_of = jnp.concatenate([low[:8], high[:8]], axis=1).astype(F32)
    gain_one, shift_one, q_bias, v_bias, out_b, gain_two, shift_two, proj_b = [rows_of[i : i + 1] for i in range(8)]
    fc_b = jnp.concatenate([low[8:].reshape(-1), high[8:].reshape(-1)])
    fc_b = lax.dynamic_slice(fc_b, (mine * share,), (share,)).astype(F32)[None]
    slot_bias = jnp.concatenate([q_bias, jnp.zeros_like(q_bias), v_bias], axis=0)
    slot_bias = jnp.pad(slot_bias, ((0, 0), (0, padded - width)))
    slot_bias = lax.dynamic_slice(slot_bias, (0, mine * SLOT), (3, SLOT)).reshape(1, 3 * SLOT)

    xs16 = tokens[0]
    xs = xs16.astype(F32)
    head_blocks = start_heads(w_qkv, side, count)
    landed_heads = spread(head_blocks)
    w_heads = wide(finish_heads(landed_heads, side, own_rows, width), 0)
    x_steps, h_one, n_one = [], [], []

    def visit_tokens(step, blocks):
        h_blocks, n_blocks = norm_blocks(blocks, wide(gain_one), wide(shift_one), width)
        x_steps.append(blocks)
        h_one.append(h_blocks)
        n_one.append(n_blocks)
        return h_blocks[0]

    def hold_tokens(step, value):
        if step == 2:
            return after(value, head_blocks)
        return after(value, landed_heads) if step == far else value

    ring.gather(wide(xs16), visit_tokens, hold_tokens)

    low, high = pair_halves(w_out, side)
    w_out_rows = after(jnp.concatenate([low, high], axis=1), x_steps[far - 1][0])
    w_out_all = lax.all_gather(w_out_rows, "context", axis=0, tiled=True)
    fc_blocks = start_fc(after(w_fc, landed_heads), side, count, share)
    landed_fc = spread(fc_blocks)
    w_fc_part = wide(finish_fc(landed_fc, side, upper, own_rows), 0)
    cot16 = cotangent[0]
    cot_all = lax.all_gather(after(wide(cot16), x_steps[far][0]), "context", axis=0, tiled=True)
    low, high = pair_halves(after(w_proj, w_heads), side)
    w_proj_part = wide(jnp.concatenate([low, high], axis=1))

    mixed, lse, *saved = attend_forward(order, spot, h_one, after(w_heads, fc_blocks), slot_bias, layout, blk)
    mixed = after(mixed, landed_fc)
    attn_out = lax.all_to_all(mixed, "context", 0, 1, tiled=True)[:, :width]

    resid_one = xs + dot_nn(attn_out, w_out_all) + out_b
    normed_two, inv_two = norm_stats(resid_one)
    h_two = (normed_two * gain_two + shift_two).astype(BF16)

    h_steps, acts, slopes, bias_sums, h2_terms = [], [], [], [], []

    def visit_feed(step, blocks):
        act, slope, bias_sum, terms = feed_blocks(
            spot, blocks, cot_all, w_fc_part, w_proj_part, fc_b, ring.size, layout[step]
        )
        h_steps.append(blocks)
        acts.append(act)
        slopes.append(slope)
        bias_sums.append(bias_sum)
        h2_terms.append(terms)
        return bias_sum

    ring.gather(wide(h_two), visit_feed)
    h_two_all, acts_all, slopes_all = pack(spot, [h_steps, acts, slopes], layout, ring.size, seq)

    g_fc = (dot_tn(h_two_all, slopes_all)[:width] * grad_scale).astype(BF16)
    g_proj = dot_tn(acts_all, cot_all)[:, :width] * grad_scale
    fillers = {far - 1: g_fc, far - 2: g_proj}

    def hold_feed(step, value):
        return after(value, fillers[step]) if step in fillers else value

    grad_h2 = ring.scatter(lambda step, event: h2_terms[step], hold_feed)[:, :width]
    g_w_proj = pair_sum(g_proj[:, :half], g_proj[:, half:], side)

    grad_y = cot16.astype(F32)
    normed_one, inv_one = norm_stats(xs)
    grad_r1 = grad_y + norm_back(grad_h2, normed_two, inv_two, gain_two)
    grad_r16 = grad_r1.astype(BF16)
    grad_o16 = dot_nt(grad_r16, w_out_all).astype(BF16)
    grad_heads = lax.all_to_all(
        jnp.pad(grad_o16, ((0, 0), (0, padded - width))), "context", 1, 0, tiled=True
    )
    g_out = dot_tn(attn_out, grad_r16) * grad_scale
    g_out = pair_sum(g_out[:, :half], g_out[:, half:], side).astype(BF16).reshape(count, own_rows, half)

    def give_out(step, event):
        act = after(acts[step], grad_o16 if event is None else event)
        return project_blocks(act, w_proj_part, sizes[step])

    out_events = []

    def hold_out(step, value):
        out_events.append(value)
        return value

    result = (resid_one + ring.scatter(give_out, hold_out)[:, :width] + proj_b).astype(BF16)
    g_w_fc = return_fc(after(g_fc, grad_o16), side, upper, count, share, own_rows)

    grad_heads = after(grad_heads, out_events[0])
    d_steps, head_sums = attend_backward(order, spot, saved, grad_heads, mixed, lse, layout, blk)
    norm_sums = []

    def give_input(step, event):
        grad = d_steps[step] if event is None else after(d_steps[step], event)
        sums, terms = input_blocks(grad, w_heads, n_one[step])
        norm_sums.append(sums)
        return terms

    h_one_all, d_all = pack(spot, [h_one, d_steps], layout, ring.size, seq)
    g_qkv = (dot_tn(h_one_all, d_all)[:width] * grad_scale).astype(BF16)
    grad_h1 = ring.scatter(give_input, lambda step, value: after(value, g_qkv) if step == far - 2 else value)
    grad_h1 = grad_h1[:, :width]
    grad_x = (grad_r1 + norm_back(grad_h1, normed_one, inv_one, gain_one)).astype(BF16)
    g_w_qkv = return_heads(g_qkv, side, count, own_rows, width)

    even = even_rows(g_out, 1).reshape(ring.size, -1, half)
    g_w_out = ring.scatter(lambda step, event, blocks=ring.pick(even): blocks[step])[:own_rows]

    fc_place = lax.dynamic_update_slice(jnp.zeros((hidden,), F32), total(bias_sums)[0], (mine * share,))
    head_place = lax.dynamic_update_slice(
        jnp.zeros((2, padded), F32), head_sums[:2], (jnp.int32(0), mine * SLOT)
    )[:, :width]
    local = jnp.concatenate(
        [
            jnp.sum(grad_h2 * normed_two, axis=0),
            jnp.sum(grad_h2, axis=0),
            jnp.sum(grad_r1, axis=0),
            jnp.sum(grad_y, axis=0),
            fc_place,
            total(norm_sums)[:, :width].reshape(-1),
            head_place.reshape(-1),
        ]
    )
    sums = sum_everywhere(local.reshape(-1, SLOT) * grad_scale, count).reshape(-1)

    def own_half(vector):
        return lax.dynamic_slice(vector, (side * (vector.shape[0] // 2),), (vector.shape[0] // 2,))

    g_ln2_gain, g_ln2_bias, g_out_bias, g_proj_bias = [
        own_half(sums[i * width : (i + 1) * width]) for i in range(4)
    ]
    g_fc_bias = own_half(sums[4 * width : 4 * width + hidden])
    late = sums[4 * width + hidden :]
    g_ln1_gain, g_ln1_bias, g_q, g_v = [own_half(late[i * width : (i + 1) * width]) for i in range(4)]
    return (
        result[None],
        grad_x[None],
        g_ln1_gain,
        g_ln1_bias,
        g_w_qkv,
        jnp.stack([g_q, g_v], axis=1),
        g_w_out,
        g_out_bias,
        g_ln2_gain,
        g_ln2_bias,
        g_w_fc,
        g_fc_bias,
        g_w_proj,
        g_proj_bias,
    )


def solution(mesh):
    rows = P("fsdp", "context", None)
    weight = P("context", "fsdp")
    vector = P("fsdp")
    pair = P("fsdp", None)
    return jax.shard_map(
        body,
        mesh=mesh,
        in_specs=(
            rows, rows, P(), vector, vector, weight, pair, weight,
            vector, vector, vector, weight, vector, weight, vector,
        ),
        out_specs=(
            rows, rows, vector, vector, weight, pair, weight,
            vector, vector, vector, weight, vector, weight, vector,
        ),
        check_vma=False,
    )
```

time: 835 us -> 666 us (0.80)
  waiting for transfers between devices: 303 us -> 188 us
  Pallas kernels: 36.2 us -> 148 us
  local copies, waits for them, and re-layouts: 149 us -> 91.4 us
  matrix products: 71.6 us -> 27.6 us
  other arithmetic: 99.7 us -> 66.1 us
  starting transfers between devices: 150 us -> 118 us
    pallas_call x2 -> x24, Pallas kernels: 36.2 us -> 148 us  [the longest x22 131 us: local_call(): pl.pallas_call(kernel, out_shape=tuple(outs), in_specs=list(ins), out_spe...]
    ppermute x98 -> x54, waiting for transfers between devices: 197 us -> 86.8 us  [the longest x24 81.6 us: send(): return lax.ppermute(value, 'context', self.links)]
    all_to_all x4, waiting for transfers between devices: 69.8 us -> 16.7 us  [spread(): return lax.all_to_all(value, 'context', 0, 0, tiled=True)]
    ppermute x11 -> x14, waiting for transfers between devices: 18.9 us -> 57.8 us  [cross(): return lax.ppermute(value, 'fsdp', [(0, 1), (1, 0)])]
    convert_element_type x5 -> x4, local copies, waits for them, and re-layouts: 30.4 us -> 0.97 us  [scatter(): self.own(value, 1).astype(BF16)]
    ppermute x98 -> x54, starting transfers between devices: 83.8 us -> 56.9 us  [the longest x24 52.1 us: send(): return lax.ppermute(value, 'context', self.links)]
    dot_general x8 -> x5, matrix products: 50.8 us -> 26.1 us  [the longest x4 22.3 us: dot_tn(): lax.dot_general(first, second, (((0,), (0,)), ((), ())), preferred_elemen...]
    dot_general x4 -> x1, matrix products: 20.8 us -> 1.55 us  [dot_nt(): lax.dot_general(first, second, (((1,), (1,)), ((), ())), preferred_elemen...]
  transfers between devices with their start and end apart: 125 -> 80, of which waited for: 50 -> 32; matrix products, arithmetic and copies ran while one was open for 33% -> 24% of each run, Pallas kernels for 4% -> 21%
where the time goes in v2:
time: 666 us; the launch traced here: 655 us
  waiting for transfers between devices  188 us (28%)
  Pallas kernels  148 us (22%)
  starting transfers between devices  118 us (18%)
  local copies, waits for them, and re-layouts  91.4 us (14%)
  other arithmetic  66.1 us (10%)
  matrix products  27.6 us (4%)
  between operations  16.1 us (2%)
    pallas_call x22, Pallas kernels, local_call(): pl.pallas_call(kernel, out_shape=tuple(outs), in_specs=list(ins), out_spe...  131 us
    ppermute x24, waiting for transfers between devices, send(): return lax.ppermute(value, 'context', self.links)  81.6 us
    ppermute x14, waiting for transfers between devices, cross(): return lax.ppermute(value, 'fsdp', [(0, 1), (1, 0)])  57.8 us
    ppermute x24, starting transfers between devices, send(): return lax.ppermute(value, 'context', self.links)  52.1 us
    all_to_all x4, starting transfers between devices, spread(): return lax.all_to_all(value, 'context', 0, 0, tiled=True)  32.2 us
    unnamed x158, local copies, waits for them, and re-layouts  29.2 us
    dot_general x4, matrix products, dot_tn(): lax.dot_general(first, second, (((0,), (0,)), ((), ())), preferred_elemen...  22.3 us
    convert_element_type x16, other arithmetic, scatter(): sent = value.astype(BF16)  21.3 us
  transfers between devices with their start and end apart: 80, of which 32 were waited for; matrix products, arithmetic and copies ran while one was open for 24% of the time, Pallas kernels for 21%

profile of v2, /device:TPU:0, one launch (start us, length us, event | category | flops | bytes accessed | tf_op | source)
XLA Modules:
  0.0 654.9 jit_solution(7395599947980723186)
XLA Ops:
  23.3 8.9 %collective-permute-done.2.refs_0_ = bf16[256,1664]{1,0:T(8,128)(2,1)S(1)} collective-permute-done((bf16[256,1664]{1,0:T(8,128)(2,1)S(1)}, bf16[256,1664]{1,0:T(8,128)(2,1)S(1)}, u32[]{:S(2)}, u32[]{:S(2)}) %collective-permute-start.2) | collective-permute-done | bytes 852000 | tf_op jit(solution)/shard_map/ppermute | solution.py:78
  38.1 4.4 norm_blocks.6
  42.5 5.8 collective-permute-done.5.refs_0_
  50.7 4.8 collective-permute-done.13
  56.4 4.7 collective-permute-done.7.refs_0_
  62.1 5.9 all-to-all-start
  70.7 4.4 norm_blocks.7
  76.2 16.7 %all-to-all-done = bf16[16,150,128]{2,1,0:T(8,128)(2,1)S(1)} async-done(((bf16[16,150,128]{2,1,0:T(8,128)(2,1)}), bf16[16,150,128]{2,1,0:T(8,128)(2,1)S(1)}, u32[]{:S(2)}, u32[]{:S(2)}) %all-to-all-start) | async-done | bytes 614432 | tf_op jit(solution)/shard_map/all_to_all | solution.py:190
  97.6 5.4 collective-permute-done.9.refs_0_
  106.9 7.7 %collective-permute-done.12 = bf16[50,3200]{1,0:T(8,128)(2,1)} collective-permute-done((bf16[50,3200]{1,0:T(8,128)(2,1)S(1)}, bf16[50,3200]{1,0:T(8,128)(2,1)}, u32[]{:S(2)}, u32[]{:S(2)}) %collective-permute-start.12) | collective-permute-done | bytes 320032 | tf_op jit(solution)/shard_map/ppermute | solution.py:161
  118.8 12.1 %all-to-all-start.1 = ((bf16[16,50,400]{2,1,0:T(8,128)(2,1)}), bf16[16,50,400]{2,1,0:T(8,128)(2,1)S(1)}, u32[]{:S(2)}, u32[]{:S(2)}) async-start(bf16[16,50,400]{2,1,0:T(8,128)(2,1)} %copy.126), calls=%async_computation.1 | async-start | bytes 1835008 | tf_op jit(solution)/shard_map/all_to_all | solution.py:190
  139.4 4.4 norm_blocks.8
  143.9 21.0 %attend_forward.1 = (bf16[2048,128]{1,0:T(8,128)(2,1)}, f32[4,8,512]{2,1,0:T(8,128)}, bf16[2,2048,128]{2,1,0:T(8,128)(2,1)}, bf16[2048,128]{1,0:T(8,128)(2,1)}, bf16[2048,128]{1,0:T(8,128)(2,1)}) custom-call(s32[32]{0:T(128)} %order_ref.1, s32[2]{0:T(128)} %pad_add_fusion.refs_1_.refs_0_.spot_ref, bf16[256,1664]{1,0:T(8,128)(2,1)} %get-tuple-element.122.refs_2_.refs_1_, ...), custom_call_target="tpu_custom_call" | custom-call | flops 4764729344 | bytes 10782344 | tf_op jit(solution)/shard_map/attend_forward/pallas_call | solution.py:282
  166.9 6.7 %all-to-all-start.2 = ((bf16[16,128,128]{1,2,0:T(8,128)(2,1)}), bf16[16,128,128]{1,2,0:T(8,128)(2,1)S(1)}, u32[]{:S(2)}, u32[]{:S(2)}) async-start(bf16[16,128,128]{1,2,0:T(8,128)(2,1)} %copy.127), calls=%async_computation.2 | async-start | bytes 1048576 | tf_op jit(solution)/shard_map/all_to_all | solution.py:785
  173.7 8.0 %reshape.163 = bf16[1600,1600]{1,0:T(8,128)(2,1)} reshape(bf16[16,100,1600]{2,1,0:T(8,128)(2,1)} %all-gather.6.cloned.1.call-done) | data formatting | bytes 10240000
  181.7 15.1 %all-to-all-done.2 = bf16[16,128,128]{1,2,0:T(8,128)(2,1)S(1)} async-done(((bf16[16,128,128]{1,2,0:T(8,128)(2,1)}), bf16[16,128,128]{1,2,0:T(8,128)(2,1)S(1)}, u32[]{:S(2)}, u32[]{:S(2)}) %all-to-all-start.2) | async-done | bytes 524320 | tf_op jit(solution)/shard_map/all_to_all | solution.py:785
  205.2 6.0 collective-permute-start.17
  211.1 10.5 %collective-permute-done.16 = bf16[400,800]{1,0:T(8,128)(2,1)S(1)} collective-permute-done((bf16[400,800]{1,0:T(8,128)(2,1)}, bf16[400,800]{1,0:T(8,128)(2,1)S(1)}, u32[]{:S(2)}, u32[]{:S(2)}) %collective-permute-start.16) | collective-permute-done | bytes 640032 | tf_op jit(solution)/shard_map/ppermute | solution.py:161
  224.3 14.4 %collective-permute-done.15 = bf16[16,50,400]{2,0,1:T(8,128)(2,1)S(1)} collective-permute-done((bf16[16,50,400]{2,0,1:T(8,128)(2,1)S(1)}, bf16[16,50,400]{2,0,1:T(8,128)(2,1)S(1)}, u32[]{:S(2)}, u32[]{:S(2)}) %collective-permute-start.15) | collective-permute-done | bytes 640032 | tf_op jit(solution)/shard_map/ppermute | solution.py:161
  244.3 5.6 feed_blocks.5
  249.9 5.1 collective-permute-start.19
  255.0 7.4 %feed_blocks.6 = (bf16[512,400]{1,0:T(8,128)(2,1)}, bf16[512,400]{1,0:T(8,128)(2,1)}, f32[1,400]{1,0:T(1,128)}, bf16[256,1664]{1,0:T(8,128)(2,1)}, bf16[256,1664]{1,0:T(8,128)(2,1)}) custom-call(s32[2]{0:T(128)} %pad_add_fusion.refs_1_.refs_0_.spot_ref, bf16[2048,1664]{1,0:T(8,128)(2,1)} %all-gather.4.cloned.1.call-done.refs_1_, ...), custom_call_target="tpu_custom_call" | custom-call | flops 2044723200 | bytes 13708424 | tf_op jit(solution)/shard_map/feed_blocks/pallas_call | solution.py:282
  269.3 10.8 %collective-permute-done.21.refs_2_.refs_6_ = bf16[256,1664]{1,0:T(8,128)(2,1)S(1)} collective-permute-done((bf16[256,1664]{1,0:T(8,128)(2,1)S(1)}, bf16[256,1664]{1,0:T(8,128)(2,1)S(1)}, u32[]{:S(2)}, u32[]{:S(2)}) %collective-permute-start.21) | collective-permute-done | bytes 852000 | tf_op jit(solution)/shard_map/ppermute | solution.py:78
  281.2 7.4 %feed_blocks.7 = (bf16[512,400]{1,0:T(8,128)(2,1)}, bf16[512,400]{1,0:T(8,128)(2,1)}, f32[1,400]{1,0:T(1,128)}, bf16[256,1664]{1,0:T(8,128)(2,1)}, bf16[256,1664]{1,0:T(8,128)(2,1)}) custom-call(s32[2]{0:T(128)} %pad_add_fusion.refs_1_.refs_0_.spot_ref, bf16[2048,1664]{1,0:T(8,128)(2,1)} %all-gather.4.cloned.1.call-done.refs_1_, ...), custom_call_target="tpu_custom_call" | custom-call | flops 2044723200 | bytes 13708424 | tf_op jit(solution)/shard_map/feed_blocks/pallas_call | solution.py:282
  290.7 6.3 collective-permute-done.23.refs_2_.refs_8_
  299.5 5.5 feed_blocks.9
  306.5 7.4 %feed_blocks.8 = (bf16[512,400]{1,0:T(8,128)(2,1)}, bf16[512,400]{1,0:T(8,128)(2,1)}, f32[1,400]{1,0:T(1,128)}, bf16[256,1664]{1,0:T(8,128)(2,1)}, bf16[256,1664]{1,0:T(8,128)(2,1)}) custom-call(s32[2]{0:T(128)} %pad_add_fusion.refs_1_.refs_0_.spot_ref, bf16[2048,1664]{1,0:T(8,128)(2,1)} %all-gather.4.cloned.1.call-done.refs_1_, ...), custom_call_target="tpu_custom_call" | custom-call | flops 2044723200 | bytes 13708424 | tf_op jit(solution)/shard_map/feed_blocks/pallas_call | solution.py:282
  314.1 9.2 %pack.2 = (bf16[2048,1664]{1,0:T(8,128)(2,1)}, bf16[2048,400]{1,0:T(8,128)(2,1)}, bf16[2048,400]{1,0:T(8,128)(2,1)}) custom-call(s32[2]{0:T(128)} %pad_add_fusion.refs_1_.refs_0_.spot_ref, bf16[256,1664]{1,0:T(8,128)(2,1)} %copy-done.4, bf16[256,1664]{1,0:T(8,128)(2,1)} %collective-permute-done.17.refs_2_, ...), custom_call_target="tpu_custom_call" | custom-call | bytes 20185088 | tf_op jit(solution)/shard_map/pack/pallas_call | solution.py:442
  325.3 7.9 %fusion.15 = bf16[1600,400]{0,1:T(8,128)(2,1)} fusion(bf16[2048,400]{1,0:T(8,128)(2,1)} %get-tuple-element.169, bf16[2048,1664]{1,0:T(8,128)(2,1)} %get-tuple-element.168), kind=kOutput, calls=%fused_computation.12 | convolution fusion | flops 2622720000 | bytes 9734144 | tf_op jit(solution)/shard_map/dot_general | solution.py:272
  337.4 4.8 fusion.9
  342.2 5.5 collective-permute-done.30
  351.4 10.5 %collective-permute-done.31 = bf16[256,1664]{1,0:T(8,128)(2,1)} collective-permute-done((bf16[256,1664]{1,0:T(8,128)(2,1)}, bf16[256,1664]{1,0:T(8,128)(2,1)}, u32[]{:S(2)}, u32[]{:S(2)}) %collective-permute-start.31) | collective-permute-done | bytes 852000 | tf_op jit(solution)/shard_map/ppermute | solution.py:78
  367.7 8.6 %collective-permute-done.32 = bf16[256,1664]{1,0:T(8,128)(2,1)S(1)} collective-permute-done((bf16[256,1664]{1,0:T(8,128)(2,1)S(1)}, bf16[256,1664]{1,0:T(8,128)(2,1)S(1)}, u32[]{:S(2)}, u32[]{:S(2)}) %collective-permute-start.32) | collective-permute-done | bytes 852000 | tf_op jit(solution)/shard_map/ppermute | solution.py:78
  395.8 4.8 all-to-all-start.3
  400.6 4.6 reshape.150
  427.7 7.6 %collective-permute-done.69 = bf16[16,50,400]{2,0,1:T(8,128)(2,1)S(1)} collective-permute-done((bf16[16,50,400]{2,0,1:T(8,128)(2,1)S(1)}, bf16[16,50,400]{2,0,1:T(8,128)(2,1)S(1)}, u32[]{:S(2)}, u32[]{:S(2)}) %collective-permute-start.69) | collective-permute-done | bytes 640032 | tf_op jit(solution)/shard_map/ppermute | solution.py:161
  438.2 7.7 %all-to-all-start.5 = ((bf16[16,50,400]{2,1,0:T(8,128)(2,1)}), bf16[16,50,400]{2,1,0:T(8,128)(2,1)}, u32[]{:S(2)}, u32[]{:S(2)}) async-start(bf16[16,50,400]{2,1,0:T(8,128)(2,1)} %add_convert_fusion.1), calls=%async_computation.5 | async-start | bytes 1835008 | tf_op jit(solution)/shard_map/all_to_all | solution.py:190
  445.9 21.0 %attend_backward.1 = (f32[8,128]{1,0:T(8,128)}, bf16[256,384]{1,0:T(8,128)(2,1)}, bf16[512,384]{1,0:T(8,128)(2,1)}, bf16[512,384]{1,0:T(8,128)(2,1)}, bf16[512,3...) custom-call(s32[32]{0:T(128)} %order_ref.1, s32[2]{0:T(128)} %pad_add_fusion.refs_1_.refs_0_.spot_ref, ...), custom_call_target="tpu_custom_call" | custom-call | flops 5368709120 | bytes 4788360 | tf_op jit(solution)/shard_map/attend_backward/pallas_call | solution.py:282
  470.5 7.5 %pack.3 = (bf16[2048,1664]{1,0:T(8,128)(2,1)}, bf16[2048,384]{1,0:T(8,128)(2,1)}) custom-call(s32[2]{0:T(128)} %pad_add_fusion.refs_1_.refs_0_.spot_ref, bf16[256,1664]{1,0:T(8,128)(2,1)} %get-tuple-element.122.refs_2_.refs_1_, bf16[256,1664]{1,0:T(8,128)(2,1)} %get-tuple-element.123.refs_3_.refs_2_, bf16[256,1664]{1,0:T(8,128)(2,1)} %get-tuple-element.124.refs_4_.refs_3_, ...), custom_call_target="tpu_custom_call" | custom-call | bytes 16777216 | tf_op jit(solution)/shard_map/pack/pallas_call | solution.py:442
  478.0 8.0 %fusion.18 = bf16[1600,384]{1,0:T(8,128)(2,1)} fusion(bf16[2048,384]{1,0:T(8,128)(2,1)} %get-tuple-element.211, bf16[2048,1664]{1,0:T(8,128)(2,1)} %get-tuple-element.210), kind=kOutput, calls=%fused_computation.13 | convolution fusion | flops 2517811200 | bytes 9617408 | tf_op jit(solution)/shard_map/dot_general | solution.py:272
  501.6 4.4 input_blocks.6
  509.1 6.5 all-to-all-start.4
  538.9 4.3 input_blocks.7
  543.2 7.0 %add_convert_fusion = bf16[1600,800]{0,1:T(8,128)(2,1)} fusion(bf16[1600,800]{0,1:T(8,128)(2,1)} %collective-permute-done.59, f32[1600,1600]{0,1:T(8,128)} %copy-done, pred[]{:T(512)S(6)} %eq.13), kind=kLoop, calls=%fused_computation.7 | loop fusion | flops 5120000 | bytes 15360001 | tf_op jit(solution)/shard_map/convert_element_type | solution.py:826
  550.2 5.2 copy.139
  586.2 4.4 input_blocks.8
  590.6 5.6 collective-permute-done.66
  625.7 6.8 %collective-permute-done.55 = f32[150,128]{1,0:T(8,128)S(1)} collective-permute-done((f32[150,128]{1,0:T(8,128)S(1)}, f32[150,128]{1,0:T(8,128)S(1)}, u32[]{:S(2)}, u32[]{:S(2)}) %collective-permute-start.55) | collective-permute-done | bytes 76832 | tf_op jit(solution)/shard_map/ppermute | solution.py:177
  (475 shorter events, 264.5 us)
Async XLA Ops:
  7.2 166.5 %all-gather.6.cloned.1.call-start = ((), (), s32[]{:S(2)}) async-start(), calls=%async_computation.7 | async-start | bytes 5883904 | tf_op jit(solution)/shard_map/all_gather | solution.py:774
  48.3 12.8 %collective-permute-start.7 = (bf16[256,1664]{1,0:T(8,128)(2,1)S(1)}, bf16[256,1664]{1,0:T(8,128)(2,1)}, u32[]{:S(2)}, u32[]{:S(2)}) collective-permute-start(bf16[256,1664]{1,0:T(8,128)(2,1)S(1)} %collective-permute-done.5.refs_0_), channel_id=1, source_target_pairs={{0,4},{1,3},{4,8},{5,1},{8,12},{9,5},{12,14},{13,9},{14,10},{15,13... | collective-permute-start | bytes 2555912 | tf_op jit(solution)/shard_map/ppermute | solution.py:78
  62.1 30.8 %all-to-all-start = ((bf16[16,150,128]{2,1,0:T(8,128)(2,1)}), bf16[16,150,128]{2,1,0:T(8,128)(2,1)S(1)}, u32[]{:S(2)}, u32[]{:S(2)}) async-start(bf16[16,150,128]{2,1,0:T(8,128)(2,1)} %copy.122), calls=%async_computation | async-start | bytes 1245184 | tf_op jit(solution)/shard_map/all_to_all | solution.py:190
  68.0 176.3 %all-gather.4.cloned.1.call-start = ((), (), s32[]{:S(2)}) async-start(), calls=%async_computation.6 | async-start | bytes 7241728 | tf_op jit(solution)/shard_map/all_gather | solution.py:779
  105.0 27.3 %collective-permute-start.11 = (bf16[16,150,128]{2,0,1:T(8,128)(2,1)}, bf16[16,150,128]{2,0,1:T(8,128)(2,1)S(1)}, u32[]{:S(2)}, u32[]{:S(2)}) collective-permute-start(bf16[16,150,128]{2,0,1:T(8,128)(2,1)} %copy.123), channel_id=1, source_target_pairs={{0,16},{16,0},{1,17},{17,1},{2,18},{18,2},{3,19},{19,3},{4,20},{20... | collective-permute-start | bytes 1843208 | tf_op jit(solution)/shard_map/ppermute | solution.py:161
  118.8 46.1 %all-to-all-start.1 = ((bf16[16,50,400]{2,1,0:T(8,128)(2,1)}), bf16[16,50,400]{2,1,0:T(8,128)(2,1)S(1)}, u32[]{:S(2)}, u32[]{:S(2)}) async-start(bf16[16,50,400]{2,1,0:T(8,128)(2,1)} %copy.126), calls=%async_computation.1 | async-start | bytes 1835008 | tf_op jit(solution)/shard_map/all_to_all | solution.py:190
  166.9 29.8 %all-to-all-start.2 = ((bf16[16,128,128]{1,2,0:T(8,128)(2,1)}), bf16[16,128,128]{1,2,0:T(8,128)(2,1)S(1)}, u32[]{:S(2)}, u32[]{:S(2)}) async-start(bf16[16,128,128]{1,2,0:T(8,128)(2,1)} %copy.127), calls=%async_computation.2 | async-start | bytes 1048576 | tf_op jit(solution)/shard_map/all_to_all | solution.py:785
  202.6 19.1 %collective-permute-start.16 = (bf16[400,800]{1,0:T(8,128)(2,1)}, bf16[400,800]{1,0:T(8,128)(2,1)S(1)}, u32[]{:S(2)}, u32[]{:S(2)}) collective-permute-start(bf16[400,800]{1,0:T(8,128)(2,1)} %param.28), channel_id=1, source_target_pairs={{0,16},{16,0},{1,17},{17,1},{2,18},{18,2},{3,19},{19,3},{4,20},{20... | collective-permute-start | bytes 1920008 | tf_op jit(solution)/shard_map/ppermute | solution.py:161
  202.8 35.9 %collective-permute-start.15 = (bf16[16,50,400]{2,0,1:T(8,128)(2,1)S(1)}, bf16[16,50,400]{2,0,1:T(8,128)(2,1)S(1)}, u32[]{:S(2)}, u32[]{:S(2)}) collective-permute-start(bf16[16,50,400]{2,0,1:T(8,128)(2,1)S(1)} %copy.130), channel_id=1, source_target_pairs={{0,16},{16,0},{1,17},{17,1},{2,18},{18,2},{3,19},{19,3},{4,20},{20... | collective-permute-start | bytes 1920008 | tf_op jit(solution)/shard_map/ppermute | solution.py:161
  205.2 34.1 %collective-permute-start.17 = (bf16[256,1664]{1,0:T(8,128)(2,1)S(1)}, bf16[256,1664]{1,0:T(8,128)(2,1)}, u32[]{:S(2)}, u32[]{:S(2)}) collective-permute-start(bf16[256,1664]{1,0:T(8,128)(2,1)S(1)} %pad_maximum_fusion.3.refs_2_.refs_1_), channel_id=1, source_target_pairs={{0,4},{1,3},{4,8},{5,1},{8,12},{9,5},{12,14},{13,9},{14,10},{15,13... | collective-permute-start | bytes 2555912 | tf_op jit(solution)/shard_map/ppermute | solution.py:78
  239.3 15.7 %collective-permute-start.18 = (bf16[256,1664]{1,0:T(8,128)(2,1)}, bf16[256,1664]{1,0:T(8,128)(2,1)}, u32[]{:S(2)}, u32[]{:S(2)}) collective-permute-start(bf16[256,1664]{1,0:T(8,128)(2,1)} %collective-permute-done.17.refs_2_), channel_id=1, source_target_pairs={{0,1},{1,0},{2,3},{3,2},{4,5},{5,4},{6,7},{7,6},{8,9},{9,8},{10,11... | collective-permute-start | bytes 2555912 | tf_op jit(solution)/shard_map/ppermute | solution.py:75
  249.9 15.7 %collective-permute-start.19 = (bf16[256,1664]{1,0:T(8,128)(2,1)}, bf16[256,1664]{1,0:T(8,128)(2,1)S(1)}, u32[]{:S(2)}, u32[]{:S(2)}) collective-permute-start(bf16[256,1664]{1,0:T(8,128)(2,1)} %collective-permute-done.17.refs_2_), channel_id=1, source_target_pairs={{0,4},{1,3},{4,8},{5,1},{8,12},{9,5},{12,14},{13,9},{14,10},{15,13... | collective-permute-start | bytes 2555912 | tf_op jit(solution)/shard_map/ppermute | solution.py:78
  265.5 14.6 %collective-permute-start.21 = (bf16[256,1664]{1,0:T(8,128)(2,1)S(1)}, bf16[256,1664]{1,0:T(8,128)(2,1)S(1)}, u32[]{:S(2)}, u32[]{:S(2)}) collective-permute-start(bf16[256,1664]{1,0:T(8,128)(2,1)S(1)} %collective-permute-done.19.refs_2_.refs_4_), channel_id=1, source_target_pairs={{0,4},{1,3},{4,8},{5,1},{8,12},{9,5},{12,14},{13,9},{14,10},{15,13... | collective-permute-start | bytes 2555912 | tf_op jit(solution)/shard_map/ppermute | solution.py:78
  290.7 14.9 %collective-permute-start.22 = (bf16[256,1664]{1,0:T(8,128)(2,1)S(1)}, bf16[256,1664]{1,0:T(8,128)(2,1)S(1)}, u32[]{:S(2)}, u32[]{:S(2)}) collective-permute-start(bf16[256,1664]{1,0:T(8,128)(2,1)S(1)} %collective-permute-done.21.refs_2_.refs_6_), channel_id=1, source_target_pairs={{0,1},{1,0},{2,3},{3,2},{4,5},{5,4},{6,7},{7,6},{8,9},{9,8},{10,11... | collective-permute-start | bytes 2555912 | tf_op jit(solution)/shard_map/ppermute | solution.py:75
  305.0 18.3 %collective-permute-start.28 = (bf16[128,1664]{1,0:T(8,128)(2,1)}, bf16[128,1664]{1,0:T(8,128)(2,1)S(1)}, u32[]{:S(2)}, u32[]{:S(2)}) collective-permute-start(bf16[128,1664]{1,0:T(8,128)(2,1)} %get-tuple-element.162), channel_id=1, source_target_pairs={{0,1},{1,0},{2,3},{3,2},{4,5},{5,4},{6,7},{7,6},{8,9},{9,8},{10,11... | collective-permute-start | bytes 1277960 | tf_op jit(solution)/shard_map/ppermute | solution.py:75
  305.2 37.0 %collective-permute-start.26 = (bf16[256,1664]{1,0:T(8,128)(2,1)}, bf16[256,1664]{1,0:T(8,128)(2,1)S(1)}, u32[]{:S(2)}, u32[]{:S(2)}) collective-permute-start(bf16[256,1664]{1,0:T(8,128)(2,1)} %get-tuple-element.158), channel_id=1, source_target_pairs={{0,1},{1,0},{2,3},{3,2},{4,5},{5,4},{6,7},{7,6},{8,9},{9,8},{10,11... | collective-permute-start | bytes 2555912 | tf_op jit(solution)/shard_map/ppermute | solution.py:75
  313.9 19.5 %collective-permute-start.27 = (bf16[256,1664]{1,0:T(8,128)(2,1)}, bf16[256,1664]{1,0:T(8,128)(2,1)S(1)}, u32[]{:S(2)}, u32[]{:S(2)}) collective-permute-start(bf16[256,1664]{1,0:T(8,128)(2,1)} %get-tuple-element.160), channel_id=1, source_target_pairs={{0,1},{1,0},{2,3},{3,2},{4,5},{5,4},{6,7},{7,6},{8,9},{9,8},{10,11... | collective-permute-start | bytes 2555912 | tf_op jit(solution)/shard_map/ppermute | solution.py:75
  334.7 13.0 %collective-permute-start.30 = (bf16[256,1664]{1,0:T(8,128)(2,1)S(1)}, bf16[256,1664]{1,0:T(8,128)(2,1)S(1)}, u32[]{:S(2)}, u32[]{:S(2)}) collective-permute-start(bf16[256,1664]{1,0:T(8,128)(2,1)S(1)} %fusion.24), channel_id=1, source_target_pairs={{0,4},{1,3},{4,8},{5,1},{8,12},{9,5},{12,14},{13,9},{14,10},{15,13... | collective-permute-start | bytes 2555912 | tf_op jit(solution)/shard_map/ppermute | solution.py:78
  337.4 14.1 %collective-permute-start.25 = (bf16[256,1664]{1,0:T(8,128)(2,1)}, bf16[256,1664]{1,0:T(8,128)(2,1)S(1)}, u32[]{:S(2)}, u32[]{:S(2)}) collective-permute-start(bf16[256,1664]{1,0:T(8,128)(2,1)} %get-tuple-element.156), channel_id=1, source_target_pairs={{0,1},{1,0},{2,3},{3,2},{4,5},{5,4},{6,7},{7,6},{8,9},{9,8},{10,11... | collective-permute-start | bytes 2555912 | tf_op jit(solution)/shard_map/ppermute | solution.py:75
  348.9 13.0 %collective-permute-start.31 = (bf16[256,1664]{1,0:T(8,128)(2,1)}, bf16[256,1664]{1,0:T(8,128)(2,1)}, u32[]{:S(2)}, u32[]{:S(2)}) collective-permute-start(bf16[256,1664]{1,0:T(8,128)(2,1)} %add_convert_fusion.7), channel_id=1, source_target_pairs={{0,4},{1,3},{4,8},{5,1},{8,12},{9,5},{12,14},{13,9},{14,10},{15,13... | collective-permute-start | bytes 2555912 | tf_op jit(solution)/shard_map/ppermute | solution.py:78
  363.5 12.7 %collective-permute-start.32 = (bf16[256,1664]{1,0:T(8,128)(2,1)S(1)}, bf16[256,1664]{1,0:T(8,128)(2,1)S(1)}, u32[]{:S(2)}, u32[]{:S(2)}) collective-permute-start(bf16[256,1664]{1,0:T(8,128)(2,1)S(1)} %add_convert_fusion.6), channel_id=1, source_target_pairs={{0,4},{1,3},{4,8},{5,1},{8,12},{9,5},{12,14},{13,9},{14,10},{15,13... | collective-permute-start | bytes 2555912 | tf_op jit(solution)/shard_map/ppermute | solution.py:78
  367.3 15.8 %collective-permute-start.71 = (bf16[400,800]{1,0:T(8,128)(2,1)S(1)}, bf16[400,800]{1,0:T(8,128)(2,1)}, u32[]{:S(2)}, u32[]{:S(2)}) collective-permute-start(bf16[400,800]{1,0:T(8,128)(2,1)S(1)} %select_convert_fusion.1), channel_id=1, source_target_pairs={{0,16},{16,0},{1,17},{17,1},{2,18},{18,2},{3,19},{19,3},{4,20},{20... | collective-permute-start | bytes 1920008 | tf_op jit(solution)/shard_map/ppermute | solution.py:161
  394.7 22.7 %collective-permute-start.34 = (bf16[128,1664]{1,0:T(8,128)(2,1)}, bf16[128,1664]{1,0:T(8,128)(2,1)S(1)}, u32[]{:S(2)}, u32[]{:S(2)}) collective-permute-start(bf16[128,1664]{1,0:T(8,128)(2,1)} %get-tuple-element.175), channel_id=1, source_target_pairs={{0,1},{1,0},{2,3},{3,2},{4,5},{5,4},{6,7},{7,6},{8,9},{9,8},{10,11... | collective-permute-start | bytes 1277960 | tf_op jit(solution)/shard_map/ppermute | solution.py:75
  395.8 42.4 %all-to-all-start.3 = ((bf16[128,16,128]{2,0,1:T(8,128)(2,1)}), bf16[128,16,128]{2,0,1:T(8,128)(2,1)}, u32[]{:S(2)}, u32[]{:S(2)}) async-start(bf16[128,16,128]{2,0,1:T(8,128)(2,1)} %copy.135), calls=%async_computation.3 | async-start | bytes 1048576 | tf_op jit(solution)/shard_map/all_to_all | solution.py:822
  414.2 21.1 %collective-permute-start.69 = (bf16[16,50,400]{2,0,1:T(8,128)(2,1)S(1)}, bf16[16,50,400]{2,0,1:T(8,128)(2,1)S(1)}, u32[]{:S(2)}, u32[]{:S(2)}) collective-permute-start(bf16[16,50,400]{2,0,1:T(8,128)(2,1)S(1)} %copy.142), channel_id=1, source_target_pairs={{0,16},{16,0},{1,17},{17,1},{2,18},{18,2},{3,19},{19,3},{4,20},{20... | collective-permute-start | bytes 1920008 | tf_op jit(solution)/shard_map/ppermute | solution.py:161
  417.6 19.3 %collective-permute-start.36 = (bf16[128,1664]{1,0:T(8,128)(2,1)S(1)}, bf16[128,1664]{1,0:T(8,128)(2,1)S(1)}, u32[]{:S(2)}, u32[]{:S(2)}) collective-permute-start(bf16[128,1664]{1,0:T(8,128)(2,1)S(1)} %add_convert_fusion.10), channel_id=1, source_target_pairs={{0,4},{1,3},{4,8},{5,1},{8,12},{9,5},{12,14},{13,9},{14,10},{15,13... | collective-permute-start | bytes 1277960 | tf_op jit(solution)/shard_map/ppermute | solution.py:78
  423.5 119.7 %collective-permute-start.59 = (bf16[1600,800]{0,1:T(8,128)(2,1)}, bf16[1600,800]{0,1:T(8,128)(2,1)}, u32[]{:S(2)}, u32[]{:S(2)}) collective-permute-start(bf16[1600,800]{0,1:T(8,128)(2,1)} %select_convert_fusion), channel_id=1, source_target_pairs={{0,16},{16,0},{1,17},{17,1},{2,18},{18,2},{3,19},{19,3},{4,20},{20... | collective-permute-start | bytes 7680008 | tf_op jit(solution)/shard_map/ppermute | solution.py:161
  427.6 66.4 %collective-permute-start.35 = (bf16[256,1664]{1,0:T(8,128)(2,1)}, bf16[256,1664]{1,0:T(8,128)(2,1)}, u32[]{:S(2)}, u32[]{:S(2)}) collective-permute-start(bf16[256,1664]{1,0:T(8,128)(2,1)} %get-tuple-element.178), channel_id=1, source_target_pairs={{0,1},{1,0},{2,3},{3,2},{4,5},{5,4},{6,7},{7,6},{8,9},{9,8},{10,11... | collective-permute-start | bytes 2555912 | tf_op jit(solution)/shard_map/ppermute | solution.py:75
  438.2 70.9 %all-to-all-start.5 = ((bf16[16,50,400]{2,1,0:T(8,128)(2,1)}), bf16[16,50,400]{2,1,0:T(8,128)(2,1)}, u32[]{:S(2)}, u32[]{:S(2)}) async-start(bf16[16,50,400]{2,1,0:T(8,128)(2,1)} %add_convert_fusion.1), calls=%async_computation.5 | async-start | bytes 1835008 | tf_op jit(solution)/shard_map/all_to_all | solution.py:190
  470.0 21.0 %collective-permute-start.43 = (bf16[128,1664]{1,0:T(8,128)(2,1)}, bf16[128,1664]{1,0:T(8,128)(2,1)}, u32[]{:S(2)}, u32[]{:S(2)}) collective-permute-start(bf16[128,1664]{1,0:T(8,128)(2,1)} %get-tuple-element.199), channel_id=1, source_target_pairs={{0,1},{1,0},{2,3},{3,2},{4,5},{5,4},{6,7},{7,6},{8,9},{9,8},{10,11... | collective-permute-start | bytes 1277960 | tf_op jit(solution)/shard_map/ppermute | solution.py:75
  491.0 15.8 %collective-permute-start.57 = (bf16[16,150,128]{2,0,1:T(8,128)(2,1)S(1)}, bf16[16,150,128]{2,0,1:T(8,128)(2,1)S(1)}, u32[]{:S(2)}, u32[]{:S(2)}) collective-permute-start(bf16[16,150,128]{2,0,1:T(8,128)(2,1)S(1)} %copy.136), channel_id=1, source_target_pairs={{0,16},{16,0},{1,17},{17,1},{2,18},{18,2},{3,19},{19,3},{4,20},{20... | collective-permute-start | bytes 1843208 | tf_op jit(solution)/shard_map/ppermute | solution.py:161
  492.3 15.7 %collective-permute-start.45 = (bf16[128,1664]{1,0:T(8,128)(2,1)S(1)}, bf16[128,1664]{1,0:T(8,128)(2,1)S(1)}, u32[]{:S(2)}, u32[]{:S(2)}) collective-permute-start(bf16[128,1664]{1,0:T(8,128)(2,1)S(1)} %add_convert_fusion.9), channel_id=1, source_target_pairs={{0,4},{1,3},{4,8},{5,1},{8,12},{9,5},{12,14},{13,9},{14,10},{15,13... | collective-permute-start | bytes 1277960 | tf_op jit(solution)/shard_map/ppermute | solution.py:78
  496.4 20.9 %collective-permute-start.38 = (bf16[256,1664]{1,0:T(8,128)(2,1)}, bf16[256,1664]{1,0:T(8,128)(2,1)}, u32[]{:S(2)}, u32[]{:S(2)}) collective-permute-start(bf16[256,1664]{1,0:T(8,128)(2,1)} %fusion.25), channel_id=1, source_target_pairs={{0,4},{1,3},{4,8},{5,1},{8,12},{9,5},{12,14},{13,9},{14,10},{15,13... | collective-permute-start | bytes 2555912 | tf_op jit(solution)/shard_map/ppermute | solution.py:78
  501.6 15.7 %collective-permute-start.37 = (bf16[256,1664]{1,0:T(8,128)(2,1)}, bf16[256,1664]{1,0:T(8,128)(2,1)}, u32[]{:S(2)}, u32[]{:S(2)}) collective-permute-start(bf16[256,1664]{1,0:T(8,128)(2,1)} %get-tuple-element.181), channel_id=1, source_target_pairs={{0,1},{1,0},{2,3},{3,2},{4,5},{5,4},{6,7},{7,6},{8,9},{9,8},{10,11... | collective-permute-start | bytes 2555912 | tf_op jit(solution)/shard_map/ppermute | solution.py:75
  506.8 27.5 %collective-permute-start.44 = (bf16[256,1664]{1,0:T(8,128)(2,1)}, bf16[256,1664]{1,0:T(8,128)(2,1)}, u32[]{:S(2)}, u32[]{:S(2)}) collective-permute-start(bf16[256,1664]{1,0:T(8,128)(2,1)} %get-tuple-element.204), channel_id=1, source_target_pairs={{0,1},{1,0},{2,3},{3,2},{4,5},{5,4},{6,7},{7,6},{8,9},{9,8},{10,11... | collective-permute-start | bytes 2555912 | tf_op jit(solution)/shard_map/ppermute | solution.py:75
  509.1 50.1 %all-to-all-start.4 = ((bf16[16,150,128]{2,1,0:T(8,128)(2,1)}), bf16[16,150,128]{2,1,0:T(8,128)(2,1)}, u32[]{:S(2)}, u32[]{:S(2)}) async-start(bf16[16,150,128]{2,1,0:T(8,128)(2,1)} %add_convert_fusion.8), calls=%async_computation.4 | async-start | bytes 1245184 | tf_op jit(solution)/shard_map/all_to_all | solution.py:190
  520.0 53.1 %collective-permute-start.40 = (bf16[256,1664]{1,0:T(8,128)(2,1)}, bf16[256,1664]{1,0:T(8,128)(2,1)}, u32[]{:S(2)}, u32[]{:S(2)}) collective-permute-start(bf16[256,1664]{1,0:T(8,128)(2,1)} %add_convert_fusion.5), channel_id=1, source_target_pairs={{0,4},{1,3},{4,8},{5,1},{8,12},{9,5},{12,14},{13,9},{14,10},{15,13... | collective-permute-start | bytes 2555912 | tf_op jit(solution)/shard_map/ppermute | solution.py:78
  525.7 47.5 %collective-permute-start.39 = (bf16[256,1664]{1,0:T(8,128)(2,1)}, bf16[256,1664]{1,0:T(8,128)(2,1)}, u32[]{:S(2)}, u32[]{:S(2)}) collective-permute-start(bf16[256,1664]{1,0:T(8,128)(2,1)} %get-tuple-element.184), channel_id=1, source_target_pairs={{0,1},{1,0},{2,3},{3,2},{4,5},{5,4},{6,7},{7,6},{8,9},{9,8},{10,11... | collective-permute-start | bytes 2555912 | tf_op jit(solution)/shard_map/ppermute | solution.py:75
  537.3 47.3 %collective-permute-start.47 = (bf16[256,1664]{1,0:T(8,128)(2,1)}, bf16[256,1664]{1,0:T(8,128)(2,1)S(1)}, u32[]{:S(2)}, u32[]{:S(2)}) collective-permute-start(bf16[256,1664]{1,0:T(8,128)(2,1)} %fusion.26), channel_id=1, source_target_pairs={{0,4},{1,3},{4,8},{5,1},{8,12},{9,5},{12,14},{13,9},{14,10},{15,13... | collective-permute-start | bytes 2555912 | tf_op jit(solution)/shard_map/ppermute | solution.py:78
  571.2 13.3 %collective-permute-start.46 = (bf16[256,1664]{1,0:T(8,128)(2,1)}, bf16[256,1664]{1,0:T(8,128)(2,1)S(1)}, u32[]{:S(2)}, u32[]{:S(2)}) collective-permute-start(bf16[256,1664]{1,0:T(8,128)(2,1)} %get-tuple-element.209), channel_id=1, source_target_pairs={{0,1},{1,0},{2,3},{3,2},{4,5},{5,4},{6,7},{7,6},{8,9},{9,8},{10,11... | collective-permute-start | bytes 2555912 | tf_op jit(solution)/shard_map/ppermute | solution.py:75
  573.1 17.5 %collective-permute-start.60 = (bf16[200,800]{1,0:T(8,128)(2,1)S(1)}, bf16[200,800]{1,0:T(8,128)(2,1)}, u32[]{:S(2)}, u32[]{:S(2)}) collective-permute-start(bf16[200,800]{1,0:T(8,128)(2,1)S(1)} %copy-done.44), channel_id=1, source_target_pairs={{0,1},{1,0},{2,3},{3,2},{4,5},{5,4},{6,7},{7,6},{8,9},{9,8},{10,11... | collective-permute-start | bytes 960008 | tf_op jit(solution)/shard_map/ppermute | solution.py:75
  579.5 20.4 %collective-permute-start.41 = (bf16[256,1664]{1,0:T(8,128)(2,1)S(1)}, bf16[256,1664]{1,0:T(8,128)(2,1)S(1)}, u32[]{:S(2)}, u32[]{:S(2)}) collective-permute-start(bf16[256,1664]{1,0:T(8,128)(2,1)S(1)} %add_convert_fusion.4), channel_id=1, source_target_pairs={{0,4},{1,3},{4,8},{5,1},{8,12},{9,5},{12,14},{13,9},{14,10},{15,13... | collective-permute-start | bytes 2555912 | tf_op jit(solution)/shard_map/ppermute | solution.py:78
  583.1 13.1 %collective-permute-start.66 = (bf16[200,800]{1,0:T(8,128)(2,1)}, bf16[200,800]{1,0:T(8,128)(2,1)}, u32[]{:S(2)}, u32[]{:S(2)}) collective-permute-start(bf16[200,800]{1,0:T(8,128)(2,1)} %fusion.47), channel_id=1, source_target_pairs={{0,4},{1,3},{4,8},{5,1},{8,12},{9,5},{12,14},{13,9},{14,10},{15,13... | collective-permute-start | bytes 960008 | tf_op jit(solution)/shard_map/ppermute | solution.py:78
  584.9 20.3 %collective-permute-start.49 = (bf16[256,1664]{1,0:T(8,128)(2,1)S(1)}, bf16[256,1664]{1,0:T(8,128)(2,1)S(1)}, u32[]{:S(2)}, u32[]{:S(2)}) collective-permute-start(bf16[256,1664]{1,0:T(8,128)(2,1)S(1)} %add_convert_fusion.3), channel_id=1, source_target_pairs={{0,4},{1,3},{4,8},{5,1},{8,12},{9,5},{12,14},{13,9},{14,10},{15,13... | collective-permute-start | bytes 2555912 | tf_op jit(solution)/shard_map/ppermute | solution.py:78
  590.6 14.6 %collective-permute-start.48 = (bf16[256,1664]{1,0:T(8,128)(2,1)}, bf16[256,1664]{1,0:T(8,128)(2,1)S(1)}, u32[]{:S(2)}, u32[]{:S(2)}) collective-permute-start(bf16[256,1664]{1,0:T(8,128)(2,1)} %get-tuple-element.217), channel_id=1, source_target_pairs={{0,1},{1,0},{2,3},{3,2},{4,5},{5,4},{6,7},{7,6},{8,9},{9,8},{10,11... | collective-permute-start | bytes 2555912 | tf_op jit(solution)/shard_map/ppermute | solution.py:75
  598.2 13.1 %collective-permute-start.67 = (bf16[200,800]{1,0:T(8,128)(2,1)}, bf16[200,800]{1,0:T(8,128)(2,1)}, u32[]{:S(2)}, u32[]{:S(2)}) collective-permute-start(bf16[200,800]{1,0:T(8,128)(2,1)} %fusion.49), channel_id=1, source_target_pairs={{0,4},{1,3},{4,8},{5,1},{8,12},{9,5},{12,14},{13,9},{14,10},{15,13... | collective-permute-start | bytes 960008 | tf_op jit(solution)/shard_map/ppermute | solution.py:78
  602.2 30.8 %collective-permute-start.42 = (bf16[128,1664]{1,0:T(8,128)(2,1)}, bf16[128,1664]{1,0:T(8,128)(2,1)}, u32[]{:S(2)}, u32[]{:S(2)}) collective-permute-start(bf16[128,1664]{1,0:T(8,128)(2,1)} %dynamic-slice_convert_fusion.1), channel_id=1, source_target_pairs={{0,1},{1,0},{2,3},{3,2},{4,5},{5,4},{6,7},{7,6},{8,9},{9,8},{10,11... | collective-permute-start | bytes 1277960 | tf_op jit(solution)/shard_map/ppermute | solution.py:75
  620.1 17.9 %collective-permute-start.50 = (bf16[256,1664]{1,0:T(8,128)(2,1)S(1)}, bf16[256,1664]{1,0:T(8,128)(2,1)}, u32[]{:S(2)}, u32[]{:S(2)}) collective-permute-start(bf16[256,1664]{1,0:T(8,128)(2,1)S(1)} %add_convert_fusion.2), channel_id=1, source_target_pairs={{0,4},{1,3},{4,8},{5,1},{8,12},{9,5},{12,14},{13,9},{14,10},{15,13... | collective-permute-start | bytes 2555912 | tf_op jit(solution)/shard_map/ppermute | solution.py:78
  (105 other events, 917.5 us)
Sparse Core Ops, SparseCore 0:
  61.2 68.2 all-gather.5
  132.4 83.2 all-gather.3

commit v3 on v2

--- a/solution.py
+++ b/solution.py
@@ -86,16 +86,18 @@
         current = jnp.concatenate(
             [jnp.where(self.core == 0, block, other), jnp.where(self.core == 0, other, block)], axis=0
         )
-        events = [visit(0, [current])]
+        blocks = [current]
         for step in range(1, self.far + 1):
             if step == self.far:
                 current = self.own(current)
-            if step >= 2:
-                current = after(current, events[step - 2])
             if hold is not None:
                 current = hold(step, current)
+            event = visit(step - 1, blocks)
             current = self.send(current)
-            events.append(visit(step, [current, self.swap(current)]))
+            if event is not None:
+                current = after(current, event)
+            blocks = [current, self.swap(current)]
+        visit(self.far, blocks)
 
     def pick(self, array):
         cut = array.shape[1] // 2
@@ -109,7 +111,7 @@
             steps.append(blocks)
         return steps
 
-    def scatter(self, give, hold=None):
+    def scatter(self, give, fill=None):
         sent = None
         for step in range(self.far, 0, -1):
             first, second = give(step, sent)
@@ -126,9 +128,10 @@
             elif step < self.far - 1:
                 value = value + got.astype(F32)
             sent = value.astype(BF16)
-            if hold is not None:
-                sent = hold(step, sent)
             got = self.send(sent)
+            events = fill(step, sent) if fill is not None else ()
+            if events:
+                got = after(got, *events)
         value = total([give(0, sent)[0], got])
         return self.own(value) + self.swap(self.own(value, 1).astype(BF16)).astype(F32)
 
@@ -207,17 +210,11 @@
     return both[:, :rows].reshape(landed.shape[0] * rows, landed.shape[2])
 
 
-def return_fc(grad, side, upper, count, share, rows):
-    grad = even_rows(grad.reshape(count, rows, share), 1)
-    cut = grad.shape[1] // 2
-    first, second = grad[:, :cut], grad[:, cut:]
-    is_first = upper == side
-    got = cross(jnp.where(is_first, second, first))
-    landed = spread(total([jnp.where(is_first, first, second), got]).astype(BF16))
+def return_fc(landed, side, count, rows):
     low, high = landed[: count // 2], landed[count // 2 :]
     mine, got = jnp.where(side == 0, low, high), cross(jnp.where(side == 0, high, low))
     both = jnp.concatenate([mine, got], axis=1).astype(F32).transpose(1, 0, 2)
-    return both.reshape(2 * cut, count // 2 * share)[:rows]
+    return both.reshape(both.shape[0], -1)[:rows]
 
 
 def start_heads(w_qkv, side, count):
@@ -233,24 +230,16 @@
     return blocks.reshape(rows + cut, count, SLOT).transpose(1, 0, 2)
 
 
-def finish_heads(landed, side, rows, width):
-    other = cross(landed)
+def finish_heads(landed, other, side, rows, width):
     one, two = jnp.where(side == 0, landed, other), jnp.where(side == 0, other, landed)
     keys = jnp.concatenate([one[:, rows:], two[:, rows:]], axis=1)[:, :rows]
     heads = jnp.concatenate([one[:, :rows], keys, two[:, :rows]], axis=2)
     return heads.reshape(width, 3 * SLOT)
 
 
-def return_heads(grad, side, count, rows, width):
+def return_heads(landed, side, count, rows, width):
     half = width // 2
-    grad = grad.reshape(count, rows, 3 * SLOT)
-    keys = even_rows(grad[:, :, SLOT : 2 * SLOT], 1)
-    cut = keys.shape[1] // 2
-    one = jnp.concatenate([grad[:, :, :SLOT], keys[:, :cut]], axis=1)
-    two = jnp.concatenate([grad[:, :, 2 * SLOT :], keys[:, cut:]], axis=1)
-    got = cross(jnp.where(side == 0, two, one))
-    landed = spread(total([jnp.where(side == 0, one, two), got]).astype(BF16))
-    landed = landed.transpose(1, 0, 2).reshape(rows + cut, count * SLOT)[:, :width]
+    landed = landed.transpose(1, 0, 2).reshape(-1, count * SLOT)[:, :width]
     main, keys = landed[:rows], landed[rows:]
     low, high = keys[:, :half], keys[:, half:]
     got, own = cross(jnp.where(side == 0, high, low)), jnp.where(side == 0, low, high)
@@ -317,65 +306,38 @@
     return list(result[:count]), list(result[count:])
 
 
-def feed_blocks(spot, blocks, cot_all, w_fc, w_proj, bias, size, entries):
+def feed_blocks(blocks, cots, w_fc, w_proj, bias):
     count, (width, share) = len(blocks), w_fc.shape
     sizes = [x.shape[0] for x in blocks]
     rows = sum(sizes)
-    unit = sizes[0] // 2 if entries[0][1] is None else sizes[0]
 
     def kernel(*refs):
-        spot_ref, cot_ref, h_refs = refs[0], refs[1], refs[2 : 2 + count]
-        fc_ref, proj_ref, bias_ref, act_ref, du_ref, sum_ref = refs[2 + count : 8 + count]
-        outs, cots, sems = refs[8 + count : -2], refs[-2], refs[-1]
-        copies, at = [], 0
-        for i, (offset, other) in enumerate(entries):
-            device = device_at(size, spot_ref, offset, other)
-            rows_there = pl.ds(pl.multiple_of(device * unit, unit), sizes[i])
-            copy = pltpu.make_async_copy(cot_ref.at[rows_there, :], cots.at[pl.ds(at, sizes[i]), :], sems.at[i])
-            copy.start()
-            copies.append(copy)
-            at += sizes[i]
-        rows_in = jnp.concatenate([h_refs[i][...] for i in range(count)], axis=0)
+        h_refs, c_refs = refs[:count], refs[count : 2 * count]
+        fc_ref, proj_ref, bias_ref, act_ref, du_ref, sum_ref = refs[2 * count : 2 * count + 6]
+        outs, results = refs[2 * count + 6 : 3 * count + 6], refs[3 * count + 6 :]
+        rows_in = jnp.concatenate([ref[...] for ref in h_refs], axis=0)
+        cot_in = jnp.concatenate([ref[...] for ref in c_refs], axis=0)
         act, slope = gelu_pair(dot_nn(rows_in, fc_ref[...]) + bias_ref[...])
         act_ref[...] = act.astype(BF16)
-        for copy in copies:
-            copy.wait()
-        grad = dot_nt(cots[...], proj_ref[...]) * slope
+        grad = dot_nt(cot_in, proj_ref[...]) * slope
         sum_ref[...] = jnp.sum(grad, axis=0, keepdims=True)
         grad = grad.astype(BF16)
         du_ref[...] = grad
         terms = dot_nt(grad, fc_ref[...]).astype(BF16)
+        output = dot_nn(act_ref[...], proj_ref[...]).astype(BF16)
         at = 0
         for i in range(count):
             outs[i][...] = terms[at : at + sizes[i]]
+            results[i][...] = output[at : at + sizes[i]]
             at += sizes[i]
 
     outs = [shape_of(rows, share, BF16), shape_of(rows, share, BF16), shape_of(1, share, F32)]
-    outs += [shape_of(size, width, BF16) for size in sizes]
-    args = [spot, cot_all] + list(blocks) + [w_fc, w_proj, bias]
-    ins = [SMEM_SPEC, ANY_SPEC] + [VMEM_SPEC] * (count + 3)
-    scratch = [pltpu.VMEM((rows, width), BF16), pltpu.SemaphoreType.DMA((count,))]
+    outs += [shape_of(size, width, BF16) for size in sizes] * 2
+    args = list(blocks) + list(cots) + [w_fc, w_proj, bias]
     result = local_call(
-        kernel, "feed_blocks", outs, ins, args, 6 * rows * width * share, scratch, rows * share
-    )
-    return result[0], result[1], result[2], list(result[3:])
-
-
-def project_blocks(act, w_proj, sizes):
-    width = w_proj.shape[1]
-
-    def kernel(act_ref, proj_ref, *outs):
-        terms = dot_nn(act_ref[...], proj_ref[...]).astype(BF16)
-        at = 0
-        for i, size in enumerate(sizes):
-            outs[i][...] = terms[at : at + size]
-            at += size
-
-    outs = [shape_of(size, width, BF16) for size in sizes]
-    result = local_call(
-        kernel, "project_blocks", outs, [VMEM_SPEC] * 2, [act, w_proj], 2 * act.size * width
-    )
-    return list(result)
+        kernel, "feed_blocks", outs, [VMEM_SPEC] * len(args), args, 8 * rows * width * share, exps=rows * share
+    )
+    return result[0], result[1], result[2], list(result[3 : 3 + count]), list(result[3 + count :])
 
 
 def input_blocks(grad, w_heads, normed):
@@ -403,52 +365,109 @@
     return result[0], list(result[1:])
 
 
-def pack(spot, groups, layout, size, seq):
-    flat, plan = [], []
-    for index, steps in enumerate(groups):
-        for blocks, entries in zip(steps, layout):
-            blocks = blocks if isinstance(blocks, list) else [blocks]
+def weight_terms(flags, steps, grads, scale, count, rows, heads):
+    flat = [block for blocks in steps for block in blocks]
+    width, cols = flat[0].shape[1], grads[0].shape[1]
+    cut = (rows + 1) // 2
+    shape = (count, rows + cut, SLOT) if heads else (count, cut, cols)
+
+    def kernel(*refs):
+        flag_ref, h_refs = refs[0], refs[1 : 1 + len(flat)]
+        g_refs, (keep_ref, send_ref, held, part) = refs[1 + len(flat) : -4], refs[-4:]
+        product, index = None, 0
+        for step, blocks in enumerate(steps):
             at = 0
-            for i, (offset, other) in enumerate(entries):
-                rows = 2 * seq // (2 * size) if other is None else seq // (2 * size)
-                if len(blocks) == len(entries):
-                    plan.append((index, len(flat) + i, 0, rows, offset, other))
+            for block in blocks:
+                size = block.shape[0]
+                add = dot_tn(g_refs[step][at : at + size, :], h_refs[index][...])
+                product = add if product is None else product + add
+                at += size
+                index += 1
+        held[...] = product.T * scale
+
+        def give(out_ref, second):
+            for d in range(count):
+                if heads:
+                    lanes = slice(2 * SLOT, 3 * SLOT) if second else slice(0, SLOT)
+                    part[0:rows, :] = held[d * rows : (d + 1) * rows, lanes]
+                    first = d * rows + (cut if second else 0)
+                    part[rows : rows + cut, :] = held[first : first + cut, SLOT : 2 * SLOT]
+                    out_ref[d] = part[0 : rows + cut, :].astype(BF16)
                 else:
-                    plan.append((index, len(flat), at, rows, offset, other))
-                at += rows
-            flat += blocks
-    unit = seq // (2 * size)
+                    first = d * rows + (cut if second else 0)
+                    out_ref[d] = held[first : first + cut, :].astype(BF16)
+
+        @pl.when(flag_ref[0] == 0)
+        def _():
+            give(keep_ref, False)
+            give(send_ref, True)
+
+        @pl.when(flag_ref[0] != 0)
+        def _():
+            give(keep_ref, True)
+            give(send_ref, False)
+
+    outs = [jax.ShapeDtypeStruct(shape, BF16)] * 2
+    args = [flags] + flat + list(grads)
+    ins = [SMEM_SPEC] + [VMEM_SPEC] * (len(args) - 1)
+    scratch = [pltpu.VMEM((width, cols), F32), pltpu.VMEM((rows + cut + 8, SLOT), F32)]
+    total_rows = sum(x.shape[0] for x in flat)
+    return local_call(kernel, "weight_terms", outs, ins, args, 2 * total_rows * width * cols, scratch)
+
+
+def proj_terms(acts, steps, scale):
+    flat = [block for blocks in steps for block in blocks]
+    width, share = flat[0].shape[1], acts[0].shape[1]
 
     def kernel(*refs):
-        spot_ref, ins = refs[0], refs[1 : 1 + len(flat)]
-        outs, sems = refs[1 + len(flat) : -1], refs[-1]
-        copies = []
-        for i, (index, source, first, rows, offset, other) in enumerate(plan):
+        c_refs, a_refs, out_ref = refs[: len(flat)], refs[len(flat) : -1], refs[-1]
+        product, index = None, 0
+        for step, blocks in enumerate(steps):
+            at = 0
+            for block in blocks:
+                size = block.shape[0]
+                add = dot_tn(a_refs[step][at : at + size, :], c_refs[index][...])
+                product = add if product is None else product + add
+                at += size
+                index += 1
+        out_ref[...] = product * scale
+
+    outs = [shape_of(share, width, F32)]
+    args = flat + list(acts)
+    total_rows = sum(x.shape[0] for x in flat)
+    flops = 2 * total_rows * width * share
+    return local_call(kernel, "proj_terms", outs, [VMEM_SPEC] * len(args), args, flops)[0]
+
+
+def out_blocks(spot, mixed, grad, layout, size, scale):
+    (rows, height), cols = mixed.shape, grad.shape[1]
+    unit = height // (2 * size)
+    plan = [entry for entries in layout for entry in entries]
+
+    def kernel(spot_ref, o_ref, grad_ref, *refs):
+        outs, held = refs[:-1], refs[-1]
+        turned = o_ref[...].astype(F32).T.astype(BF16)
+        held[...] = dot_nn(turned, grad_ref[...]) * scale
+        for i, (offset, other) in enumerate(plan):
             device = device_at(size, spot_ref, offset, other)
-            there = pl.ds(pl.multiple_of(device * unit, unit), rows)
-            copy = pltpu.make_async_copy(
-                ins[source].at[pl.ds(first, rows), :], outs[index].at[there, :], sems.at[i]
-            )
-            copy.start()
-            copies.append(copy)
-        for copy in copies:
-            copy.wait()
-
-    outs = []
-    for steps in groups:
-        sample = steps[0][0] if isinstance(steps[0], list) else steps[0]
-        outs.append(shape_of(seq, sample.shape[1], sample.dtype))
-    moved = sum(2 * math.prod(x.shape) * x.dtype.itemsize for x in outs)
-    return pl.pallas_call(
+            block = held[pl.ds(pl.multiple_of(device * unit, 8), outs[i].shape[0]), :]
+            outs[i][...] = block.astype(BF16)
+
+    outs = [shape_of(2 * unit if other is None else unit, cols, BF16) for _, other in plan]
+    result = local_call(
         kernel,
-        out_shape=tuple(outs),
-        in_specs=[SMEM_SPEC] + [ANY_SPEC] * len(flat),
-        out_specs=tuple(VMEM_SPEC for _ in outs),
-        scratch_shapes=[pltpu.SemaphoreType.DMA((len(plan),))],
-        compiler_params=pltpu.CompilerParams(vmem_limit_bytes=VMEM_LIMIT),
-        cost_estimate=pl.CostEstimate(flops=0, bytes_accessed=moved, transcendentals=0),
-        name="pack",
-    )(spot, *flat)
+        "out_blocks",
+        outs,
+        [SMEM_SPEC] + [VMEM_SPEC] * 2,
+        [spot, mixed, grad],
+        2 * rows * height * cols,
+        [pltpu.VMEM((height, cols), F32)],
+    )
+    steps, at = [], 0
+    for entries in layout:
+        steps.append(list(result[at : at + len(entries)]))
+        at += len(entries)
+    return steps
 
 
 def head_masks(scale):
@@ -752,7 +771,8 @@
     xs = xs16.astype(F32)
     head_blocks = start_heads(w_qkv, side, count)
     landed_heads = spread(head_blocks)
-    w_heads = wide(finish_heads(landed_heads, side, own_rows, width), 0)
+    other_heads = cross(landed_heads)
+    w_heads = wide(finish_heads(landed_heads, other_heads, side, own_rows, width), 0)
     x_steps, h_one, n_one = [], [], []
 
     def visit_tokens(step, blocks):
@@ -762,101 +782,151 @@
         n_one.append(n_blocks)
         return h_blocks[0]
 
+    cot16 = cotangent[0]
+    cot_wide = wide(cot16)
+
+    low, high = pair_halves(w_out, side)
+    w_out_rows = jnp.concatenate([low, high], axis=1)
+    w_out_rows = jnp.pad(w_out_rows, ((0, -own_rows % 8), (0, 0)))
+    out_rows = w_out_rows.shape[0]
+    fc_blocks = start_fc(w_fc, side, count, share)
+    made = {}
+
     def hold_tokens(step, value):
+        if step == 1:
+            value = after(value, w_out_rows)
         if step == 2:
-            return after(value, head_blocks)
-        return after(value, landed_heads) if step == far else value
+            value = after(value, head_blocks)
+        if step == 3:
+            value = after(value, landed_heads)
+        if step == far:
+            value = after(value, fc_blocks, other_heads)
+        made["tokens"] = value
+        return value
 
     ring.gather(wide(xs16), visit_tokens, hold_tokens)
 
-    low, high = pair_halves(w_out, side)
-    w_out_rows = after(jnp.concatenate([low, high], axis=1), x_steps[far - 1][0])
-    w_out_all = lax.all_gather(w_out_rows, "context", axis=0, tiled=True)
-    fc_blocks = start_fc(after(w_fc, landed_heads), side, count, share)
-    landed_fc = spread(fc_blocks)
-    w_fc_part = wide(finish_fc(landed_fc, side, upper, own_rows), 0)
-    cot16 = cotangent[0]
-    cot_all = lax.all_gather(after(wide(cot16), x_steps[far][0]), "context", axis=0, tiled=True)
+    w_out_all = lax.all_gather(after(w_out_rows, made["tokens"]), "context", axis=0, tiled=True)
+    landed_fc = spread(after(fc_blocks, x_steps[far - 1][0]))
     low, high = pair_halves(after(w_proj, w_heads), side)
     w_proj_part = wide(jnp.concatenate([low, high], axis=1))
 
-    mixed, lse, *saved = attend_forward(order, spot, h_one, after(w_heads, fc_blocks), slot_bias, layout, blk)
-    mixed = after(mixed, landed_fc)
+    mixed, lse, *saved = attend_forward(order, spot, h_one, w_heads, slot_bias, layout, blk)
+
+    cot_steps = []
+    ring.gather(
+        cot_wide,
+        lambda step, blocks: cot_steps.append(blocks),
+        lambda step, value: after(value, made["tokens"] if step == 1 else mixed) if step <= 2 else value,
+    )
+
+    w_fc_part = wide(finish_fc(after(landed_fc, mixed), side, upper, own_rows), 0)
+    mixed = after(mixed, landed_fc, w_proj_part, cot_steps[max(1, far // 4)][0])
     attn_out = lax.all_to_all(mixed, "context", 0, 1, tiled=True)[:, :width]
+    attn_out = after(attn_out, w_fc_part, cot_steps[max(2, 3 * far // 4)][0]).reshape(rows, count, own_rows)
+    attn_out = jnp.pad(attn_out, ((0, 0), (0, 0), (0, out_rows - own_rows))).reshape(rows, -1)
 
     resid_one = xs + dot_nn(attn_out, w_out_all) + out_b
     normed_two, inv_two = norm_stats(resid_one)
     h_two = (normed_two * gain_two + shift_two).astype(BF16)
 
-    h_steps, acts, slopes, bias_sums, h2_terms = [], [], [], [], []
+    h_steps, acts, slopes, bias_sums, h2_terms, out_terms = [], [], [], [], [], []
 
     def visit_feed(step, blocks):
-        act, slope, bias_sum, terms = feed_blocks(
-            spot, blocks, cot_all, w_fc_part, w_proj_part, fc_b, ring.size, layout[step]
+        act, slope, bias_sum, terms, outputs = feed_blocks(
+            blocks, cot_steps[step], w_fc_part, w_proj_part, fc_b
         )
         h_steps.append(blocks)
         acts.append(act)
         slopes.append(slope)
         bias_sums.append(bias_sum)
         h2_terms.append(terms)
+        out_terms.append(outputs)
         return bias_sum
 
     ring.gather(wide(h_two), visit_feed)
-    h_two_all, acts_all, slopes_all = pack(spot, [h_steps, acts, slopes], layout, ring.size, seq)
-
-    g_fc = (dot_tn(h_two_all, slopes_all)[:width] * grad_scale).astype(BF16)
-    g_proj = dot_tn(acts_all, cot_all)[:, :width] * grad_scale
-    fillers = {far - 1: g_fc, far - 2: g_proj}
-
-    def hold_feed(step, value):
-        return after(value, fillers[step]) if step in fillers else value
-
-    grad_h2 = ring.scatter(lambda step, event: h2_terms[step], hold_feed)[:, :width]
-    g_w_proj = pair_sum(g_proj[:, :half], g_proj[:, half:], side)
+
+    is_first = (upper == side).astype(jnp.int32)
+
+    def fill_feed(step, event):
+        if step == far:
+            flags = after(1 - is_first, event).reshape(1)
+            made["fc"] = weight_terms(flags, h_steps, slopes, grad_scale, count, own_rows, False)
+            made["fc_got"] = cross(made["fc"][1])
+            return (made["fc"][1],)
+        if step == far - 1:
+            made["proj"] = proj_terms([after(acts[0], event)] + acts[1:], cot_steps, grad_scale)
+            return (made["proj"],)
+        if step == far - 2:
+            g_proj = after(made["proj"], event)[:, :width]
+            left, right = g_proj[:, :half], g_proj[:, half:]
+            made["proj_keep"] = jnp.where(side == 0, left, right)
+            send = jnp.where(side == 0, right, left).astype(BF16)
+            made["proj_got"] = cross(send)
+            made["fc_sum"] = total([after(made["fc"][0], event), made["fc_got"]]).astype(BF16)
+            return (send, made["fc_sum"])
+        return ()
+
+    grad_h2 = ring.scatter(lambda step, event: h2_terms[step], fill_feed)[:, :width]
 
     grad_y = cot16.astype(F32)
     normed_one, inv_one = norm_stats(xs)
     grad_r1 = grad_y + norm_back(grad_h2, normed_two, inv_two, gain_two)
     grad_r16 = grad_r1.astype(BF16)
     grad_o16 = dot_nt(grad_r16, w_out_all).astype(BF16)
-    grad_heads = lax.all_to_all(
-        jnp.pad(grad_o16, ((0, 0), (0, padded - width))), "context", 1, 0, tiled=True
-    )
-    g_out = dot_tn(attn_out, grad_r16) * grad_scale
-    g_out = pair_sum(g_out[:, :half], g_out[:, half:], side).astype(BF16).reshape(count, own_rows, half)
+    grad_o16 = grad_o16.reshape(rows, count, out_rows)[:, :, :own_rows].reshape(rows, width)
+    grad_slots = jnp.pad(grad_o16, ((0, 0), (0, padded - width)))
+    grad_heads = lax.all_to_all(grad_slots, "context", 1, 0, tiled=True)
+
+    g_out_steps = out_blocks(spot, after(attn_out, grad_slots), wide(grad_r16), layout, ring.size, grad_scale)
+    g_out_events = {}
+
+    def fill_out_grad(step, event):
+        g_out_events[step] = event
+        return ()
+
+    g_out = ring.scatter(lambda step, event: g_out_steps[step], fill_out_grad)[:own_rows]
+    g_w_out = pair_sum(g_out[:, :half], g_out[:, half:width], side)
+
+    out_events = {}
 
     def give_out(step, event):
-        act = after(acts[step], grad_o16 if event is None else event)
-        return project_blocks(act, w_proj_part, sizes[step])
-
-    out_events = []
-
-    def hold_out(step, value):
-        out_events.append(value)
-        return value
-
-    result = (resid_one + ring.scatter(give_out, hold_out)[:, :width] + proj_b).astype(BF16)
-    g_w_fc = return_fc(after(g_fc, grad_o16), side, upper, count, share, own_rows)
-
-    grad_heads = after(grad_heads, out_events[0])
+        return [after(term, grad_o16) for term in out_terms[step]] if event is None else out_terms[step]
+
+    def fill_out(step, event):
+        out_events[step] = event
+        return ()
+
+    result = (resid_one + ring.scatter(give_out, fill_out)[:, :width] + proj_b).astype(BF16)
+
+    fc_sum = made["fc_sum"]
+    fc_landed = spread(after(fc_sum, grad_heads))
+    grad_heads = after(grad_heads, out_events[far - 1], g_out_events[far])
     d_steps, head_sums = attend_backward(order, spot, saved, grad_heads, mixed, lse, layout, blk)
     norm_sums = []
 
     def give_input(step, event):
+        event = made[2] if step == 0 else event
         grad = d_steps[step] if event is None else after(d_steps[step], event)
         sums, terms = input_blocks(grad, w_heads, n_one[step])
         norm_sums.append(sums)
         return terms
 
-    h_one_all, d_all = pack(spot, [h_one, d_steps], layout, ring.size, seq)
-    g_qkv = (dot_tn(h_one_all, d_all)[:width] * grad_scale).astype(BF16)
-    grad_h1 = ring.scatter(give_input, lambda step, value: after(value, g_qkv) if step == far - 2 else value)
-    grad_h1 = grad_h1[:, :width]
+    def fill_input(step, event):
+        made[step] = event
+        if step == far:
+            flags = after(side, event).astype(jnp.int32).reshape(1)
+            made["qkv"] = weight_terms(flags, h_one, d_steps, grad_scale, count, own_rows, True)
+            return (made["qkv"][1], fc_landed)
+        return ()
+
+    grad_h1 = ring.scatter(give_input, fill_input)[:, :width]
     grad_x = (grad_r1 + norm_back(grad_h1, normed_one, inv_one, gain_one)).astype(BF16)
-    g_w_qkv = return_heads(g_qkv, side, count, own_rows, width)
-
-    even = even_rows(g_out, 1).reshape(ring.size, -1, half)
-    g_w_out = ring.scatter(lambda step, event, blocks=ring.pick(even): blocks[step])[:own_rows]
+    keep, send = made["qkv"]
+    qkv_sum = total([after(keep, made[far - 1]), cross(send)]).astype(BF16)
+    g_w_qkv = return_heads(spread(qkv_sum), side, count, own_rows, width)
+    g_w_proj = total([after(made["proj_keep"], made[2]), made["proj_got"]])
+    g_w_fc = return_fc(after(fc_landed, made[2]), side, count, own_rows)
 
     fc_place = lax.dynamic_update_slice(jnp.zeros((hidden,), F32), total(bias_sums)[0], (mine * share,))
     head_place = lax.dynamic_update_slice(

time: 666 us -> 562 us (0.84)
  waiting for transfers between devices: 188 us -> 114 us
  local copies, waits for them, and re-layouts: 91.4 us -> 63.5 us
  matrix products: 27.6 us -> 7.95 us
  starting transfers between devices: 118 us -> 129 us
  other arithmetic: 66.1 us -> 73.8 us
    ppermute x24 -> x28, waiting for transfers between devices: 81.6 us -> 54.3 us  [send(): return lax.ppermute(value, 'context', self.links)]
    ppermute x14, waiting for transfers between devices: 57.8 us -> 34.3 us  [cross(): return lax.ppermute(value, 'fsdp', [(0, 1), (1, 0)])]
    dot_general x4 -> x0, matrix products: 22.3 us -> none  [dot_tn(): lax.dot_general(first, second, (((0,), (0,)), ((), ())), preferred_elemen...]
    pallas_call x2 -> x0, Pallas kernels: 16.7 us -> none  [pack(): pl.pallas_call(kernel, out_shape=tuple(outs), in_specs=[SMEM_SPEC] + [ANY...]
    pallas_call x22 -> x21, Pallas kernels: 131 us -> 147 us  [local_call(): pl.pallas_call(kernel, out_shape=tuple(outs), in_specs=list(ins), out_spe...]
    all_to_all x4, starting transfers between devices: 32.2 us -> 18.6 us  [spread(): return lax.all_to_all(value, 'context', 0, 0, tiled=True)]
    unnamed x158 -> x161, local copies, waits for them, and re-layouts: 29.2 us -> 18.5 us
    all_to_all x1, waiting for transfers between devices: 15.1 us -> 5.91 us  [body(): attn_out = lax.all_to_all(mixed, 'context', 0, 1, tiled=True)[:, :width]]
  transfers between devices with their start and end apart: 80 -> 88, of which waited for: 32 -> 30; matrix products, arithmetic and copies ran while one was open for 24% -> 21% of each run, Pallas kernels for 21% -> 26%
where the time goes in v3:
time: 562 us; the launch traced here: 552 us
  Pallas kernels  147 us (26%)
  starting transfers between devices  129 us (23%)
  waiting for transfers between devices  114 us (20%)
  other arithmetic  73.8 us (13%)
  local copies, waits for them, and re-layouts  63.5 us (11%)
  between operations  15.9 us (3%)
  matrix products  7.95 us (1%)
    pallas_call x21, Pallas kernels, local_call(): pl.pallas_call(kernel, out_shape=tuple(outs), in_specs=list(ins), out_spe...  147 us
    ppermute x28, starting transfers between devices, send(): return lax.ppermute(value, 'context', self.links)  60.6 us
    ppermute x28, waiting for transfers between devices, send(): return lax.ppermute(value, 'context', self.links)  54.3 us
    ppermute x14, waiting for transfers between devices, cross(): return lax.ppermute(value, 'fsdp', [(0, 1), (1, 0)])  34.3 us
    convert_element_type x16, other arithmetic, scatter(): sent = value.astype(BF16)  24.7 us
    all_to_all x4, starting transfers between devices, spread(): return lax.all_to_all(value, 'context', 0, 0, tiled=True)  18.6 us
    unnamed x161, local copies, waits for them, and re-layouts  18.5 us
    ppermute x14, starting transfers between devices, cross(): return lax.ppermute(value, 'fsdp', [(0, 1), (1, 0)])  16.3 us
  transfers between devices with their start and end apart: 88, of which 30 were waited for; matrix products, arithmetic and copies ran while one was open for 21% of the time, Pallas kernels for 26%

profile of v3, /device:TPU:0, one launch (start us, length us, event | category | flops | bytes accessed | tf_op | source)
XLA Modules:
  0.0 551.5 jit_solution(4649967082633905801)
XLA Ops:
  28.8 4.9 all-to-all-start
  35.7 3.1 norm_blocks.5
  40.4 3.3 collective-permute-start.6
  46.6 4.5 norm_blocks.6
  51.1 5.8 %collective-permute-done.6.refs_0_ = bf16[256,1664]{1,0:T(8,128)(2,1)} collective-permute-done((bf16[256,1664]{1,0:T(8,128)(2,1)}, bf16[256,1664]{1,0:T(8,128)(2,1)}, u32[]{:S(2)}, u32[]{:S(2)}) %collective-permute-start.6) | collective-permute-done | bytes 852000 | tf_op jit(solution)/shard_map/ppermute | solution.py:78
  56.9 4.8 collective-permute-start.8
  66.7 4.4 norm_blocks.7
  74.1 4.0 collective-permute-done.11
  86.4 4.2 all-to-all-start.1
  90.6 4.4 norm_blocks.8
  107.7 21.0 %attend_forward.1 = (bf16[2048,128]{1,0:T(8,128)(2,1)}, f32[4,8,512]{2,1,0:T(8,128)}, bf16[2,2048,128]{2,1,0:T(8,128)(2,1)}, bf16[2048,128]{1,0:T(8,128)(2,1)}, bf16[2048,128]{1,0:T(8,128)(2,1)}) custom-call(s32[32]{0:T(128)} %order_ref.1, s32[2]{0:T(128)} %pad_add_fusion.refs_1_.spot_ref, bf16[256,1664]{1,0:T(8,128)(2,1)} %get-tuple-element.144.refs_2_.refs_1_, ...), custom_call_target="tpu_custom_call" | custom-call | flops 4764729344 | bytes 10782344 | tf_op jit(solution)/shard_map/attend_forward/pallas_call | solution.py:271
  128.8 4.2 collective-permute-start.18
  133.1 9.6 %all-to-all-done.1 = bf16[16,50,400]{2,1,0:T(8,128)(2,1)S(1)} async-done(((bf16[16,50,400]{2,1,0:T(8,128)(2,1)}), bf16[16,50,400]{2,1,0:T(8,128)(2,1)S(1)}, u32[]{:S(2)}, u32[]{:S(2)}) %all-to-all-start.1) | async-done | bytes 640032 | tf_op jit(solution)/shard_map/all_to_all | solution.py:193
  147.9 13.8 %all-to-all-start.2 = ((bf16[16,128,128]{1,2,0:T(8,128)(2,1)}), bf16[16,128,128]{1,2,0:T(8,128)(2,1)}, u32[]{:S(2)}, u32[]{:S(2)}) async-start(bf16[16,128,128]{1,2,0:T(8,128)(2,1)} %copy.124), calls=%async_computation.2 | async-start | bytes 1048576 | tf_op jit(solution)/shard_map/all_to_all | solution.py:825
  170.5 5.9 %all-to-all-done.2 = bf16[16,128,128]{1,2,0:T(8,128)(2,1)} async-done(((bf16[16,128,128]{1,2,0:T(8,128)(2,1)}), bf16[16,128,128]{1,2,0:T(8,128)(2,1)}, u32[]{:S(2)}, u32[]{:S(2)}) %all-to-all-start.2) | async-done | bytes 524320 | tf_op jit(solution)/shard_map/all_to_all | solution.py:825
  177.4 3.1 collective-permute-done.19.refs_2_.refs_5_
  181.4 3.7 fusion.41
  189.1 4.3 collective-permute-start.21
  195.0 5.4 feed_blocks.5
  200.4 3.2 collective-permute-done.21.refs_0_.refs_2_
  208.3 8.0 %feed_blocks.6 = (bf16[512,400]{1,0:T(8,128)(2,1)}, bf16[512,400]{1,0:T(8,128)(2,1)}, f32[1,400]{1,0:T(1,128)}, bf16[256,1664]{1,0:T(8,128)(2,1)}, bf16[256,1664...) custom-call(bf16[256,1664]{1,0:T(8,128)(2,1)} %collective-permute-done.21.refs_0_.refs_2_, ...), custom_call_target="tpu_custom_call" | custom-call | flops 2726297600 | bytes 10300544 | tf_op jit(solution)/shard_map/feed_blocks/pallas_call | solution.py:271
  221.3 8.0 %feed_blocks.7 = (bf16[512,400]{1,0:T(8,128)(2,1)}, bf16[512,400]{1,0:T(8,128)(2,1)}, f32[1,400]{1,0:T(1,128)}, bf16[256,1664]{1,0:T(8,128)(2,1)}, bf16[256,1664...) custom-call(bf16[256,1664]{1,0:T(8,128)(2,1)} %copy-done.71, bf16[256,1664]{1,0:T(8,128)(2,1)} %copy-done.72, ...), custom_call_target="tpu_custom_call" | custom-call | flops 2726297600 | bytes 10300544 | tf_op jit(solution)/shard_map/feed_blocks/pallas_call | solution.py:271
  233.4 4.8 collective-permute-done.35.refs_2_.refs_7_
  240.1 8.0 %feed_blocks.8 = (bf16[512,400]{1,0:T(8,128)(2,1)}, bf16[512,400]{1,0:T(8,128)(2,1)}, f32[1,400]{1,0:T(1,128)}, bf16[256,1664]{1,0:T(8,128)(2,1)}, bf16[256,1664...) custom-call(bf16[256,1664]{1,0:T(8,128)(2,1)} %copy-done.46, bf16[256,1664]{1,0:T(8,128)(2,1)} %copy-done.73, ...), custom_call_target="tpu_custom_call" | custom-call | flops 2726297600 | bytes 10300544 | tf_op jit(solution)/shard_map/feed_blocks/pallas_call | solution.py:271
  250.8 5.4 feed_blocks.9
  261.9 9.1 %weight_terms.2 = (bf16[16,50,400]{2,1,0:T(8,128)(2,1)}, bf16[16,50,400]{2,1,0:T(8,128)(2,1)}) custom-call(s32[1]{0:T(128)} %bitcast.13.refs_0_, bf16[256,1664]{1,0:T(8,128)(2,1)} %copy-done.23, bf16[256,1664]{1,0:T(8,128)(2,1)} %collective-permute-done.21.refs_0_.refs_2_, bf16[256,1664]{1,0:T(8,128)(2,1)} %copy-done.70, bf16[256,1664]{1,0:T(8,128)(2,1)} %copy-done.71, ...), custom_call_target="tpu_custom_call" | custom-call | flops 2726297600 | bytes 9734148 | tf_op jit(solution)/shard_map/weight_terms/pallas_call | solution.py:271
  275.4 8.7 %proj_terms.1 = f32[400,1664]{1,0:T(8,128)} custom-call(bf16[256,1664]{1,0:T(8,128)(2,1)} %copy-done.9, bf16[256,1664]{1,0:T(8,128)(2,1)} %collective-permute-done.16.refs_2_.refs_1_, bf16[256,1664]{1,0:T(8,128)(2,1)} %copy-done.18, bf16[256,1664]{1,0:T(8,128)(2,1)} %collective-permute-done.18.refs_2_.refs_3_, bf16[256,1664]{1,0:T(8,128)(2,1)} %copy-done.19, ...), custom_call_target="tpu_custom_call" | custom-call | flops 2726297600 | bytes 11116544 | tf_op jit(solution)/shard_map/proj_terms/pallas_call | solution.py:271
  288.1 6.6 %collective-permute-done.44 = bf16[16,50,400]{2,0,1:T(8,128)(2,1)S(1)} collective-permute-done((bf16[16,50,400]{2,0,1:T(8,128)(2,1)S(1)}, bf16[16,50,400]{2,0,1:T(8,128)(2,1)S(1)}, u32[]{:S(2)}, u32[]{:S(2)}) %collective-permute-start.44) | collective-permute-done | bytes 640032 | tf_op jit(solution)/shard_map/ppermute | solution.py:164
  300.0 11.5 %collective-permute-done.45 = bf16[256,1664]{1,0:T(8,128)(2,1)S(1)} collective-permute-done((bf16[256,1664]{1,0:T(8,128)(2,1)S(1)}, bf16[256,1664]{1,0:T(8,128)(2,1)S(1)}, u32[]{:S(2)}, u32[]{:S(2)}) %collective-permute-start.45) | collective-permute-done | bytes 852000 | tf_op jit(solution)/shard_map/ppermute | solution.py:78
  320.7 4.3 convolution_convert_fusion
  327.2 5.3 out_blocks.1
  335.7 4.2 all-to-all-start.3
  344.6 8.6 %collective-permute-done.73 = bf16[104,1664]{1,0:T(8,128)(2,1)S(1)} collective-permute-done((bf16[104,1664]{1,0:T(8,128)(2,1)S(1)}, bf16[104,1664]{1,0:T(8,128)(2,1)S(1)}, u32[]{:S(2)}, u32[]{:S(2)}) %collective-permute-start.73) | collective-permute-done | bytes 346144 | tf_op jit(solution)/shard_map/ppermute | solution.py:78
  355.1 4.3 collective-permute-start.48
  360.6 4.5 collective-permute-done.48
  371.2 4.5 all-to-all-start.4
  375.7 21.0 %attend_backward.1 = (f32[8,128]{1,0:T(8,128)}, bf16[256,384]{1,0:T(8,128)(2,1)}, bf16[512,384]{1,0:T(8,128)(2,1)}, bf16[512,384]{1,0:T(8,128)(2,1)}, bf16[512,3...) custom-call(s32[32]{0:T(128)} %order_ref.1, s32[2]{0:T(128)} %pad_add_fusion.refs_1_.spot_ref, ...), custom_call_target="tpu_custom_call" | custom-call | flops 5368709120 | bytes 4788360 | tf_op jit(solution)/shard_map/attend_backward/pallas_call | solution.py:271
  397.6 3.2 input_blocks.5
  407.1 8.4 %weight_terms.3 = (bf16[16,150,128]{2,1,0:T(8,128)(2,1)}, bf16[16,150,128]{2,1,0:T(8,128)(2,1)}) custom-call(s32[1]{0:T(128)} %bitcast.19.refs_0_, bf16[256,1664]{1,0:T(8,128)(2,1)} %get-tuple-element.144.refs_2_.refs_1_, bf16[256,1664]{1,0:T(8,128)(2,1)} %get-tuple-element.147.refs_3_.refs_2_, bf16[256,1664]{1,0:T(8,128)(2,1)} %get-tuple-element.148.refs_4_.refs_3_, ...), custom_call_target="tpu_custom_call" | custom-call | flops 2617245696 | bytes 9617412 | tf_op jit(solution)/shard_map/weight_terms/pallas_call | solution.py:271
  417.6 4.3 input_blocks.6
  438.0 14.8 %collective-permute-done.68 = bf16[16,150,128]{2,0,1:T(8,128)(2,1)S(1)} collective-permute-done((bf16[16,150,128]{2,0,1:T(8,128)(2,1)}, bf16[16,150,128]{2,0,1:T(8,128)(2,1)S(1)}, u32[]{:S(2)}, u32[]{:S(2)}) %collective-permute-start.68) | collective-permute-done | bytes 614432 | tf_op jit(solution)/shard_map/ppermute | solution.py:164
  454.7 5.0 all-to-all-start.5
  459.7 4.3 input_blocks.7
  479.3 3.2 input_blocks.8
  482.5 4.4 input_blocks.9
  492.5 3.8 collective-permute-done.64
  497.4 4.4 collective-permute-done.78
  532.3 4.4 collective-permute-done.61
  (484 shorter events, 230.8 us)
Async XLA Ops:
  25.8 14.7 %collective-permute-start.3 = (bf16[256,1664]{1,0:T(8,128)(2,1)S(1)}, bf16[256,1664]{1,0:T(8,128)(2,1)}, u32[]{:S(2)}, u32[]{:S(2)}) collective-permute-start(bf16[256,1664]{1,0:T(8,128)(2,1)S(1)} %pad_maximum_fusion.2.refs_0_), channel_id=1, source_target_pairs={{0,4},{1,3},{4,8},{5,1},{8,12},{9,5},{12,14},{13,9},{14,10},{15,13... | collective-permute-start | bytes 2555912 | tf_op jit(solution)/shard_map/ppermute | solution.py:78
  28.8 28.2 %all-to-all-start = ((bf16[16,150,128]{2,1,0:T(8,128)(2,1)}), bf16[16,150,128]{2,1,0:T(8,128)(2,1)S(1)}, u32[]{:S(2)}, u32[]{:S(2)}) async-start(bf16[16,150,128]{2,1,0:T(8,128)(2,1)} %copy.118), calls=%async_computation | async-start | bytes 1245184 | tf_op jit(solution)/shard_map/all_to_all | solution.py:193
  33.7 146.9 %all-gather.2.cloned.1.call-start = ((), (), s32[]{:S(2)}) async-start(), calls=%async_computation.6 | async-start | bytes 5883904 | tf_op jit(solution)/shard_map/all_gather | solution.py:809
  40.4 16.5 %collective-permute-start.6 = (bf16[256,1664]{1,0:T(8,128)(2,1)}, bf16[256,1664]{1,0:T(8,128)(2,1)}, u32[]{:S(2)}, u32[]{:S(2)}) collective-permute-start(bf16[256,1664]{1,0:T(8,128)(2,1)} %collective-permute-done.3.refs_0_), channel_id=1, source_target_pairs={{0,4},{1,3},{4,8},{5,1},{8,12},{9,5},{12,14},{13,9},{14,10},{15,13... | collective-permute-start | bytes 2555912 | tf_op jit(solution)/shard_map/ppermute | solution.py:78
  44.6 17.2 %collective-permute-start.10 = (bf16[50,3200]{1,0:T(8,128)(2,1)}, bf16[50,3200]{1,0:T(8,128)(2,1)}, u32[]{:S(2)}, u32[]{:S(2)}) collective-permute-start(bf16[50,3200]{1,0:T(8,128)(2,1)} %slice.190), channel_id=1, source_target_pairs={{0,16},{16,0},{1,17},{17,1},{2,18},{18,2},{3,19},{19,3},{4,20},{20... | collective-permute-start | bytes 960008 | tf_op jit(solution)/shard_map/ppermute | solution.py:164
  56.9 15.3 %collective-permute-start.8 = (bf16[256,1664]{1,0:T(8,128)(2,1)}, bf16[256,1664]{1,0:T(8,128)(2,1)}, u32[]{:S(2)}, u32[]{:S(2)}) collective-permute-start(bf16[256,1664]{1,0:T(8,128)(2,1)} %collective-permute-done.6.refs_0_), channel_id=1, source_target_pairs={{0,4},{1,3},{4,8},{5,1},{8,12},{9,5},{12,14},{13,9},{14,10},{15,13... | collective-permute-start | bytes 2555912 | tf_op jit(solution)/shard_map/ppermute | solution.py:78
  63.7 14.4 %collective-permute-start.11 = (bf16[16,150,128]{2,0,1:T(8,128)(2,1)}, bf16[16,150,128]{2,0,1:T(8,128)(2,1)}, u32[]{:S(2)}, u32[]{:S(2)}) collective-permute-start(bf16[16,150,128]{2,0,1:T(8,128)(2,1)} %copy.119), channel_id=1, source_target_pairs={{0,16},{16,0},{1,17},{17,1},{2,18},{18,2},{3,19},{19,3},{4,20},{20... | collective-permute-start | bytes 1843208 | tf_op jit(solution)/shard_map/ppermute | solution.py:164
  78.9 16.0 %collective-permute-start.12 = (bf16[128,1664]{1,0:T(8,128)(2,1)}, bf16[128,1664]{1,0:T(8,128)(2,1)}, u32[]{:S(2)}, u32[]{:S(2)}) collective-permute-start(bf16[128,1664]{1,0:T(8,128)(2,1)} %constant_dynamic-slice_fusion.2), channel_id=1, source_target_pairs={{0,4},{1,3},{4,8},{5,1},{8,12},{9,5},{12,14},{13,9},{14,10},{15,13... | collective-permute-start | bytes 1277960 | tf_op jit(solution)/shard_map/ppermute | solution.py:78
  82.4 46.3 %collective-permute-start.16 = (bf16[256,1664]{1,0:T(8,128)(2,1)S(1)}, bf16[256,1664]{1,0:T(8,128)(2,1)}, u32[]{:S(2)}, u32[]{:S(2)}) collective-permute-start(bf16[256,1664]{1,0:T(8,128)(2,1)S(1)} %pad_maximum_fusion.3.refs_1_.refs_0_), channel_id=1, source_target_pairs={{0,4},{1,3},{4,8},{5,1},{8,12},{9,5},{12,14},{13,9},{14,10},{15,13... | collective-permute-start | bytes 2555912 | tf_op jit(solution)/shard_map/ppermute | solution.py:78
  86.4 56.3 %all-to-all-start.1 = ((bf16[16,50,400]{2,1,0:T(8,128)(2,1)}), bf16[16,50,400]{2,1,0:T(8,128)(2,1)S(1)}, u32[]{:S(2)}, u32[]{:S(2)}) async-start(bf16[16,50,400]{2,1,0:T(8,128)(2,1)} %copy.122), calls=%async_computation.1 | async-start | bytes 1835008 | tf_op jit(solution)/shard_map/all_to_all | solution.py:193
  103.0 29.9 %collective-permute-start.14 = (bf16[400,800]{1,0:T(8,128)(2,1)S(1)}, bf16[400,800]{1,0:T(8,128)(2,1)S(1)}, u32[]{:S(2)}, u32[]{:S(2)}) collective-permute-start(bf16[400,800]{1,0:T(8,128)(2,1)S(1)} %copy-done.36), channel_id=1, source_target_pairs={{0,16},{16,0},{1,17},{17,1},{2,18},{18,2},{3,19},{19,3},{4,20},{20... | collective-permute-start | bytes 1920008 | tf_op jit(solution)/shard_map/ppermute | solution.py:164
  128.8 33.0 %collective-permute-start.18 = (bf16[256,1664]{1,0:T(8,128)(2,1)}, bf16[256,1664]{1,0:T(8,128)(2,1)}, u32[]{:S(2)}, u32[]{:S(2)}) collective-permute-start(bf16[256,1664]{1,0:T(8,128)(2,1)} %collective-permute-done.16.refs_2_.refs_1_), channel_id=1, source_target_pairs={{0,4},{1,3},{4,8},{5,1},{8,12},{9,5},{12,14},{13,9},{14,10},{15,13... | collective-permute-start | bytes 2555912 | tf_op jit(solution)/shard_map/ppermute | solution.py:78
  143.8 20.0 %collective-permute-start.17 = (bf16[16,50,400]{2,0,1:T(8,128)(2,1)}, bf16[16,50,400]{2,0,1:T(8,128)(2,1)}, u32[]{:S(2)}, u32[]{:S(2)}) collective-permute-start(bf16[16,50,400]{2,0,1:T(8,128)(2,1)} %copy.125), channel_id=1, source_target_pairs={{0,16},{16,0},{1,17},{17,1},{2,18},{18,2},{3,19},{19,3},{4,20},{20... | collective-permute-start | bytes 1920008 | tf_op jit(solution)/shard_map/ppermute | solution.py:164
  147.9 28.4 %all-to-all-start.2 = ((bf16[16,128,128]{1,2,0:T(8,128)(2,1)}), bf16[16,128,128]{1,2,0:T(8,128)(2,1)}, u32[]{:S(2)}, u32[]{:S(2)}) async-start(bf16[16,128,128]{1,2,0:T(8,128)(2,1)} %copy.124), calls=%async_computation.2 | async-start | bytes 1048576 | tf_op jit(solution)/shard_map/all_to_all | solution.py:825
  161.8 18.7 %collective-permute-start.19 = (bf16[256,1664]{1,0:T(8,128)(2,1)}, bf16[256,1664]{1,0:T(8,128)(2,1)S(1)}, u32[]{:S(2)}, u32[]{:S(2)}) collective-permute-start(bf16[256,1664]{1,0:T(8,128)(2,1)} %collective-permute-done.18.refs_2_.refs_3_), channel_id=1, source_target_pairs={{0,4},{1,3},{4,8},{5,1},{8,12},{9,5},{12,14},{13,9},{14,10},{15,13... | collective-permute-start | bytes 2555912 | tf_op jit(solution)/shard_map/ppermute | solution.py:78
  189.1 14.6 %collective-permute-start.21 = (bf16[256,1664]{1,0:T(8,128)(2,1)S(1)}, bf16[256,1664]{1,0:T(8,128)(2,1)}, u32[]{:S(2)}, u32[]{:S(2)}) collective-permute-start(bf16[256,1664]{1,0:T(8,128)(2,1)S(1)} %pad_maximum_fusion.4.refs_0_.refs_1_), channel_id=1, source_target_pairs={{0,4},{1,3},{4,8},{5,1},{8,12},{9,5},{12,14},{13,9},{14,10},{15,13... | collective-permute-start | bytes 2555912 | tf_op jit(solution)/shard_map/ppermute | solution.py:78
  203.7 13.4 %collective-permute-start.25 = (bf16[256,1664]{1,0:T(8,128)(2,1)}, bf16[256,1664]{1,0:T(8,128)(2,1)S(1)}, u32[]{:S(2)}, u32[]{:S(2)}) collective-permute-start(bf16[256,1664]{1,0:T(8,128)(2,1)} %collective-permute-done.21.refs_0_.refs_2_), channel_id=1, source_target_pairs={{0,4},{1,3},{4,8},{5,1},{8,12},{9,5},{12,14},{13,9},{14,10},{15,13... | collective-permute-start | bytes 2555912 | tf_op jit(solution)/shard_map/ppermute | solution.py:78
  206.2 13.3 %collective-permute-start.27 = (bf16[256,1664]{1,0:T(8,128)(2,1)}, bf16[256,1664]{1,0:T(8,128)(2,1)S(1)}, u32[]{:S(2)}, u32[]{:S(2)}) collective-permute-start(bf16[256,1664]{1,0:T(8,128)(2,1)} %collective-permute-done.18.refs_2_.refs_3_), channel_id=1, source_target_pairs={{0,1},{1,0},{2,3},{3,2},{4,5},{5,4},{6,7},{7,6},{8,9},{9,8},{10,11... | collective-permute-start | bytes 2555912 | tf_op jit(solution)/shard_map/ppermute | solution.py:75
  217.1 12.9 %collective-permute-start.29 = (bf16[256,1664]{1,0:T(8,128)(2,1)S(1)}, bf16[256,1664]{1,0:T(8,128)(2,1)S(1)}, u32[]{:S(2)}, u32[]{:S(2)}) collective-permute-start(bf16[256,1664]{1,0:T(8,128)(2,1)S(1)} %collective-permute-done.25.refs_0_.refs_4_), channel_id=1, source_target_pairs={{0,4},{1,3},{4,8},{5,1},{8,12},{9,5},{12,14},{13,9},{14,10},{15,13... | collective-permute-start | bytes 2555912 | tf_op jit(solution)/shard_map/ppermute | solution.py:78
  219.3 18.9 %collective-permute-start.31 = (bf16[256,1664]{1,0:T(8,128)(2,1)S(1)}, bf16[256,1664]{1,0:T(8,128)(2,1)S(1)}, u32[]{:S(2)}, u32[]{:S(2)}) collective-permute-start(bf16[256,1664]{1,0:T(8,128)(2,1)S(1)} %copy-done.13), channel_id=1, source_target_pairs={{0,1},{1,0},{2,3},{3,2},{4,5},{5,4},{6,7},{7,6},{8,9},{9,8},{10,11... | collective-permute-start | bytes 2555912 | tf_op jit(solution)/shard_map/ppermute | solution.py:75
  232.1 16.0 %collective-permute-start.33 = (bf16[128,1664]{1,0:T(8,128)(2,1)S(1)}, bf16[128,1664]{1,0:T(8,128)(2,1)S(1)}, u32[]{:S(2)}, u32[]{:S(2)}) collective-permute-start(bf16[128,1664]{1,0:T(8,128)(2,1)S(1)} %constant_dynamic-slice_fusion.1), channel_id=1, source_target_pairs={{0,4},{1,3},{4,8},{5,1},{8,12},{9,5},{12,14},{13,9},{14,10},{15,13... | collective-permute-start | bytes 1277960 | tf_op jit(solution)/shard_map/ppermute | solution.py:78
  272.4 12.7 %collective-permute-start.42 = (bf16[256,1664]{1,0:T(8,128)(2,1)S(1)}, bf16[256,1664]{1,0:T(8,128)(2,1)S(1)}, u32[]{:S(2)}, u32[]{:S(2)}) collective-permute-start(bf16[256,1664]{1,0:T(8,128)(2,1)S(1)} %fusion.3), channel_id=1, source_target_pairs={{0,4},{1,3},{4,8},{5,1},{8,12},{9,5},{12,14},{13,9},{14,10},{15,13... | collective-permute-start | bytes 2555912 | tf_op jit(solution)/shard_map/ppermute | solution.py:78
  274.5 20.2 %collective-permute-start.44 = (bf16[16,50,400]{2,0,1:T(8,128)(2,1)S(1)}, bf16[16,50,400]{2,0,1:T(8,128)(2,1)S(1)}, u32[]{:S(2)}, u32[]{:S(2)}) collective-permute-start(bf16[16,50,400]{2,0,1:T(8,128)(2,1)S(1)} %copy.131), channel_id=1, source_target_pairs={{0,16},{16,0},{1,17},{17,1},{2,18},{18,2},{3,19},{19,3},{4,20},{20... | collective-permute-start | bytes 1920008 | tf_op jit(solution)/shard_map/ppermute | solution.py:164
  285.5 12.7 %collective-permute-start.43 = (bf16[256,1664]{1,0:T(8,128)(2,1)S(1)}, bf16[256,1664]{1,0:T(8,128)(2,1)S(1)}, u32[]{:S(2)}, u32[]{:S(2)}) collective-permute-start(bf16[256,1664]{1,0:T(8,128)(2,1)S(1)} %add_convert_fusion.6), channel_id=1, source_target_pairs={{0,4},{1,3},{4,8},{5,1},{8,12},{9,5},{12,14},{13,9},{14,10},{15,13... | collective-permute-start | bytes 2555912 | tf_op jit(solution)/shard_map/ppermute | solution.py:78
  298.6 12.9 %collective-permute-start.45 = (bf16[256,1664]{1,0:T(8,128)(2,1)S(1)}, bf16[256,1664]{1,0:T(8,128)(2,1)S(1)}, u32[]{:S(2)}, u32[]{:S(2)}) collective-permute-start(bf16[256,1664]{1,0:T(8,128)(2,1)S(1)} %add_convert_fusion.5), channel_id=1, source_target_pairs={{0,4},{1,3},{4,8},{5,1},{8,12},{9,5},{12,14},{13,9},{14,10},{15,13... | collective-permute-start | bytes 2555912 | tf_op jit(solution)/shard_map/ppermute | solution.py:78
  315.7 148.3 %collective-permute-start.24 = (bf16[256,1664]{1,0:T(8,128)(2,1)}, bf16[256,1664]{1,0:T(8,128)(2,1)}, u32[]{:S(2)}, u32[]{:S(2)}) collective-permute-start(bf16[256,1664]{1,0:T(8,128)(2,1)} %get-tuple-element.174), channel_id=1, source_target_pairs={{0,1},{1,0},{2,3},{3,2},{4,5},{5,4},{6,7},{7,6},{8,9},{9,8},{10,11... | collective-permute-start | bytes 2555912 | tf_op jit(solution)/shard_map/ppermute | solution.py:75
  316.2 105.7 %collective-permute-start.28 = (bf16[256,1664]{1,0:T(8,128)(2,1)}, bf16[256,1664]{1,0:T(8,128)(2,1)}, u32[]{:S(2)}, u32[]{:S(2)}) collective-permute-start(bf16[256,1664]{1,0:T(8,128)(2,1)} %get-tuple-element.178), channel_id=1, source_target_pairs={{0,1},{1,0},{2,3},{3,2},{4,5},{5,4},{6,7},{7,6},{8,9},{9,8},{10,11... | collective-permute-start | bytes 2555912 | tf_op jit(solution)/shard_map/ppermute | solution.py:75
  316.2 49.1 %collective-permute-start.32 = (bf16[256,1664]{1,0:T(8,128)(2,1)}, bf16[256,1664]{1,0:T(8,128)(2,1)}, u32[]{:S(2)}, u32[]{:S(2)}) collective-permute-start(bf16[256,1664]{1,0:T(8,128)(2,1)} %get-tuple-element.182), channel_id=1, source_target_pairs={{0,1},{1,0},{2,3},{3,2},{4,5},{5,4},{6,7},{7,6},{8,9},{9,8},{10,11... | collective-permute-start | bytes 2555912 | tf_op jit(solution)/shard_map/ppermute | solution.py:75
  335.7 34.4 %all-to-all-start.3 = ((bf16[128,16,128]{0,2,1:T(8,128)(2,1)}), bf16[128,16,128]{0,2,1:T(8,128)(2,1)S(1)}, u32[]{:S(2)}, u32[]{:S(2)}) async-start(bf16[128,16,128]{0,2,1:T(8,128)(2,1)} %bitcast.16), calls=%async_computation.3 | async-start | bytes 1048576 | tf_op jit(solution)/shard_map/all_to_all | solution.py:879
  339.9 15.2 %collective-permute-start.72 = (bf16[208,1664]{1,0:T(8,128)(2,1)}, bf16[208,1664]{1,0:T(8,128)(2,1)S(1)}, u32[]{:S(2)}, u32[]{:S(2)}) collective-permute-start(bf16[208,1664]{1,0:T(8,128)(2,1)} %get-tuple-element.271), channel_id=1, source_target_pairs={{0,1},{1,0},{2,3},{3,2},{4,5},{5,4},{6,7},{7,6},{8,9},{9,8},{10,11... | collective-permute-start | bytes 2076680 | tf_op jit(solution)/shard_map/ppermute | solution.py:75
  353.2 47.7 %collective-permute-start.71 = (bf16[208,1664]{1,0:T(8,128)(2,1)}, bf16[208,1664]{1,0:T(8,128)(2,1)}, u32[]{:S(2)}, u32[]{:S(2)}) collective-permute-start(bf16[208,1664]{1,0:T(8,128)(2,1)} %get-tuple-element.269), channel_id=1, source_target_pairs={{0,1},{1,0},{2,3},{3,2},{4,5},{5,4},{6,7},{7,6},{8,9},{9,8},{10,11... | collective-permute-start | bytes 2076680 | tf_op jit(solution)/shard_map/ppermute | solution.py:75
  365.1 61.6 %collective-permute-start.70 = (bf16[208,1664]{1,0:T(8,128)(2,1)}, bf16[208,1664]{1,0:T(8,128)(2,1)}, u32[]{:S(2)}, u32[]{:S(2)}) collective-permute-start(bf16[208,1664]{1,0:T(8,128)(2,1)} %get-tuple-element.267), channel_id=1, source_target_pairs={{0,1},{1,0},{2,3},{3,2},{4,5},{5,4},{6,7},{7,6},{8,9},{9,8},{10,11... | collective-permute-start | bytes 2076680 | tf_op jit(solution)/shard_map/ppermute | solution.py:75
  365.2 37.6 %collective-permute-start.74 = (bf16[208,1664]{1,0:T(8,128)(2,1)}, bf16[208,1664]{1,0:T(8,128)(2,1)}, u32[]{:S(2)}, u32[]{:S(2)}) collective-permute-start(bf16[208,1664]{1,0:T(8,128)(2,1)} %fusion.6), channel_id=1, source_target_pairs={{0,4},{1,3},{4,8},{5,1},{8,12},{9,5},{12,14},{13,9},{14,10},{15,13... | collective-permute-start | bytes 2076680 | tf_op jit(solution)/shard_map/ppermute | solution.py:78
  371.2 61.6 %all-to-all-start.4 = ((bf16[16,50,400]{2,1,0:T(8,128)(2,1)}), bf16[16,50,400]{2,1,0:T(8,128)(2,1)}, u32[]{:S(2)}, u32[]{:S(2)}) async-start(bf16[16,50,400]{2,1,0:T(8,128)(2,1)} %add_convert_fusion), calls=%async_computation.4 | async-start | bytes 1835008 | tf_op jit(solution)/shard_map/all_to_all | solution.py:193
  400.8 22.0 %collective-permute-start.49 = (bf16[256,1664]{1,0:T(8,128)(2,1)S(1)}, bf16[256,1664]{1,0:T(8,128)(2,1)S(1)}, u32[]{:S(2)}, u32[]{:S(2)}) collective-permute-start(bf16[256,1664]{1,0:T(8,128)(2,1)S(1)} %copy-done.24), channel_id=1, source_target_pairs={{0,4},{1,3},{4,8},{5,1},{8,12},{9,5},{12,14},{13,9},{14,10},{15,13... | collective-permute-start | bytes 2555912 | tf_op jit(solution)/shard_map/ppermute | solution.py:78
  404.8 21.9 %collective-permute-start.75 = (bf16[208,1664]{1,0:T(8,128)(2,1)S(1)}, bf16[208,1664]{1,0:T(8,128)(2,1)S(1)}, u32[]{:S(2)}, u32[]{:S(2)}) collective-permute-start(bf16[208,1664]{1,0:T(8,128)(2,1)S(1)} %add_convert_fusion.8), channel_id=1, source_target_pairs={{0,4},{1,3},{4,8},{5,1},{8,12},{9,5},{12,14},{13,9},{14,10},{15,13... | collective-permute-start | bytes 2076680 | tf_op jit(solution)/shard_map/ppermute | solution.py:78
  421.9 65.9 %collective-permute-start.80 = (bf16[400,800]{1,0:T(8,128)(2,1)}, bf16[400,800]{1,0:T(8,128)(2,1)}, u32[]{:S(2)}, u32[]{:S(2)}) collective-permute-start(bf16[400,800]{1,0:T(8,128)(2,1)} %select_convert_fusion), channel_id=1, source_target_pairs={{0,16},{16,0},{1,17},{17,1},{2,18},{18,2},{3,19},{19,3},{4,20},{20... | collective-permute-start | bytes 1920008 | tf_op jit(solution)/shard_map/ppermute | solution.py:164
  426.7 26.1 %collective-permute-start.68 = (bf16[16,150,128]{2,0,1:T(8,128)(2,1)}, bf16[16,150,128]{2,0,1:T(8,128)(2,1)S(1)}, u32[]{:S(2)}, u32[]{:S(2)}) collective-permute-start(bf16[16,150,128]{2,0,1:T(8,128)(2,1)} %copy.136), channel_id=1, source_target_pairs={{0,16},{16,0},{1,17},{17,1},{2,18},{18,2},{3,19},{19,3},{4,20},{20... | collective-permute-start | bytes 1843208 | tf_op jit(solution)/shard_map/ppermute | solution.py:164
  431.2 33.2 %collective-permute-start.50 = (bf16[256,1664]{1,0:T(8,128)(2,1)}, bf16[256,1664]{1,0:T(8,128)(2,1)}, u32[]{:S(2)}, u32[]{:S(2)}) collective-permute-start(bf16[256,1664]{1,0:T(8,128)(2,1)} %add_convert_fusion.4), channel_id=1, source_target_pairs={{0,4},{1,3},{4,8},{5,1},{8,12},{9,5},{12,14},{13,9},{14,10},{15,13... | collective-permute-start | bytes 2555912 | tf_op jit(solution)/shard_map/ppermute | solution.py:78
  433.9 34.9 %collective-permute-start.76 = (bf16[208,1664]{1,0:T(8,128)(2,1)}, bf16[208,1664]{1,0:T(8,128)(2,1)}, u32[]{:S(2)}, u32[]{:S(2)}) collective-permute-start(bf16[208,1664]{1,0:T(8,128)(2,1)} %add_convert_fusion.7), channel_id=1, source_target_pairs={{0,4},{1,3},{4,8},{5,1},{8,12},{9,5},{12,14},{13,9},{14,10},{15,13... | collective-permute-start | bytes 2076680 | tf_op jit(solution)/shard_map/ppermute | solution.py:78
  452.8 19.3 %collective-permute-start.58 = (bf16[256,1664]{1,0:T(8,128)(2,1)}, bf16[256,1664]{1,0:T(8,128)(2,1)}, u32[]{:S(2)}, u32[]{:S(2)}) collective-permute-start(bf16[256,1664]{1,0:T(8,128)(2,1)} %fusion.5), channel_id=1, source_target_pairs={{0,4},{1,3},{4,8},{5,1},{8,12},{9,5},{12,14},{13,9},{14,10},{15,13... | collective-permute-start | bytes 2555912 | tf_op jit(solution)/shard_map/ppermute | solution.py:78
  454.7 57.4 %all-to-all-start.5 = ((bf16[16,150,128]{2,1,0:T(8,128)(2,1)}), bf16[16,150,128]{2,1,0:T(8,128)(2,1)S(1)}, u32[]{:S(2)}, u32[]{:S(2)}) async-start(bf16[16,150,128]{2,1,0:T(8,128)(2,1)} %add_convert_fusion.9), calls=%async_computation.5 | async-start | bytes 1245184 | tf_op jit(solution)/shard_map/all_to_all | solution.py:193
  467.2 41.6 %collective-permute-start.51 = (bf16[256,1664]{1,0:T(8,128)(2,1)}, bf16[256,1664]{1,0:T(8,128)(2,1)}, u32[]{:S(2)}, u32[]{:S(2)}) collective-permute-start(bf16[256,1664]{1,0:T(8,128)(2,1)} %add_convert_fusion.3), channel_id=1, source_target_pairs={{0,4},{1,3},{4,8},{5,1},{8,12},{9,5},{12,14},{13,9},{14,10},{15,13... | collective-permute-start | bytes 2555912 | tf_op jit(solution)/shard_map/ppermute | solution.py:78
  472.0 18.3 %collective-permute-start.77 = (bf16[104,1664]{1,0:T(8,128)(2,1)}, bf16[104,1664]{1,0:T(8,128)(2,1)}, u32[]{:S(2)}, u32[]{:S(2)}) collective-permute-start(bf16[104,1664]{1,0:T(8,128)(2,1)} %dynamic-slice_convert_fusion.3), channel_id=1, source_target_pairs={{0,1},{1,0},{2,3},{3,2},{4,5},{5,4},{6,7},{7,6},{8,9},{9,8},{10,11... | collective-permute-start | bytes 1038344 | tf_op jit(solution)/shard_map/ppermute | solution.py:75
  474.6 47.4 %collective-permute-start.60 = (bf16[256,1664]{1,0:T(8,128)(2,1)}, bf16[256,1664]{1,0:T(8,128)(2,1)}, u32[]{:S(2)}, u32[]{:S(2)}) collective-permute-start(bf16[256,1664]{1,0:T(8,128)(2,1)} %add_convert_fusion.2), channel_id=1, source_target_pairs={{0,4},{1,3},{4,8},{5,1},{8,12},{9,5},{12,14},{13,9},{14,10},{15,13... | collective-permute-start | bytes 2555912 | tf_op jit(solution)/shard_map/ppermute | solution.py:78
  478.4 37.4 %collective-permute-start.79 = (bf16[8,50,400]{2,1,0:T(8,128)(2,1)}, bf16[8,50,400]{2,1,0:T(8,128)(2,1)}, u32[]{:S(2)}, u32[]{:S(2)}) collective-permute-start(bf16[8,50,400]{2,1,0:T(8,128)(2,1)} %get-tuple-element.381), channel_id=1, source_target_pairs={{0,16},{16,0},{1,17},{17,1},{2,18},{18,2},{3,19},{19,3},{4,20},{20... | collective-permute-start | bytes 960008 | tf_op jit(solution)/shard_map/ppermute | solution.py:164
  490.3 31.6 %collective-permute-start.59 = (bf16[256,1664]{1,0:T(8,128)(2,1)}, bf16[256,1664]{1,0:T(8,128)(2,1)}, u32[]{:S(2)}, u32[]{:S(2)}) collective-permute-start(bf16[256,1664]{1,0:T(8,128)(2,1)} %get-tuple-element.255), channel_id=1, source_target_pairs={{0,1},{1,0},{2,3},{3,2},{4,5},{5,4},{6,7},{7,6},{8,9},{9,8},{10,11... | collective-permute-start | bytes 2555912 | tf_op jit(solution)/shard_map/ppermute | solution.py:75
  512.1 25.6 %collective-permute-start.52 = (bf16[128,1664]{1,0:T(8,128)(2,1)}, bf16[128,1664]{1,0:T(8,128)(2,1)}, u32[]{:S(2)}, u32[]{:S(2)}) collective-permute-start(bf16[128,1664]{1,0:T(8,128)(2,1)} %dynamic-slice_convert_fusion.1), channel_id=1, source_target_pairs={{0,1},{1,0},{2,3},{3,2},{4,5},{5,4},{6,7},{7,6},{8,9},{9,8},{10,11... | collective-permute-start | bytes 1277960 | tf_op jit(solution)/shard_map/ppermute | solution.py:75
  (116 other events, 679.5 us)
Sparse Core Ops, SparseCore 0:
  78.2 74.2 all-gather.1

commit v4 on v3

--- a/solution.py
+++ b/solution.py
@@ -112,28 +112,50 @@
         return steps
 
     def scatter(self, give, fill=None):
-        sent = None
+        going = Scatter(self, give)
         for step in range(self.far, 0, -1):
-            first, second = give(step, sent)
-            if step == self.far:
-                value = total([first, self.swap(second)])
-            else:
-                value = total([second, self.swap(first)])
-            if step == self.far - 1:
-                got = got.astype(F32)
-                blank = jnp.zeros_like(got)
-                value = value + jnp.concatenate(
-                    [jnp.where(self.core == 0, got, blank), jnp.where(self.core == 0, blank, got)], axis=0
-                )
-            elif step < self.far - 1:
-                value = value + got.astype(F32)
-            sent = value.astype(BF16)
-            got = self.send(sent)
-            events = fill(step, sent) if fill is not None else ()
-            if events:
-                got = after(got, *events)
-        value = total([give(0, sent)[0], got])
-        return self.own(value) + self.swap(self.own(value, 1).astype(BF16)).astype(F32)
+            going.hop()
+            events = fill(step, going.sent) if fill is not None else ()
+            going.hold(*events)
+        return going.finish()
+
+
+class Scatter:
+    def __init__(self, ring, give):
+        self.ring, self.give, self.step = ring, give, ring.far
+        self.sent = self.got = None
+
+    def hop(self, *events):
+        ring, step = self.ring, self.step
+        first, second = self.give(step, self.sent)
+        if events:
+            first, second = after(first, *events), after(second, *events)
+        if step == ring.far:
+            value = total([first, ring.swap(second)])
+        else:
+            value = total([second, ring.swap(first)])
+        if step == ring.far - 1:
+            got = self.got.astype(F32)
+            blank = jnp.zeros_like(got)
+            value = value + jnp.concatenate(
+                [jnp.where(ring.core == 0, got, blank), jnp.where(ring.core == 0, blank, got)], axis=0
+            )
+        elif step < ring.far - 1:
+            value = value + self.got.astype(F32)
+        self.sent = value.astype(BF16)
+        self.got = ring.send(self.sent)
+        self.step -= 1
+
+    def hold(self, *events):
+        if events:
+            self.got = after(self.got, *events)
+
+    def finish(self):
+        ring = self.ring
+        while self.step:
+            self.hop()
+        value = total([self.give(0, self.sent)[0], self.got])
+        return ring.own(value) + ring.swap(ring.own(value, 1).astype(BF16)).astype(F32)
 
 
 def device_at(size, spot, offset, other):
@@ -602,17 +624,31 @@
     return local_call(kernel, "attend_forward", outs, ins, args, flops, scratch, seq * seq)
 
 
-def attend_backward(order, spot, saved, grads, mixed, lse, layout, blk):
+def attend_backward(order, spot, saved, grads, mixed, lse, layout, blk, w_heads=None, normed=None):
     queries, keys, values = saved
     seq = keys.shape[0]
     chips = 2 * (len(layout) - 1)
     tile = tile_of(seq)
     tiles = seq // tile
     steps = len(layout)
-
-    def kernel(order_ref, spot_ref, qs, ks, vs, g_ref, o_ref, lse_ref, sum_ref, *refs):
-        d_refs = refs[:steps]
-        gs, ps, kt, dqt, drow, dk, dv, dsort = refs[steps:]
+    flat = [block for blocks in normed for block in blocks] if normed else []
+    pieces = len(flat)
+
+    def kernel(order_ref, spot_ref, qs, ks, vs, g_ref, o_ref, lse_ref, *refs):
+        if pieces:
+            w_ref, n_refs, refs = refs[0], refs[1 : 1 + pieces], refs[1 + pieces :]
+            norm_ref, t_refs = refs[1 + steps], refs[2 + steps : 2 + steps + pieces]
+            held, sems = refs[-2:]
+            copies, at = [], 0
+            for i in range(pieces):
+                rows = flat[i].shape[0]
+                copy = pltpu.make_async_copy(n_refs[i], held.at[pl.ds(at, rows), :], sems.at[i])
+                copy.start()
+                copies.append(copy)
+                at += rows
+            refs = refs[: 1 + steps] + refs[2 + steps + pieces : -2]
+        sum_ref, d_refs = refs[0], refs[1 : 1 + steps]
+        gs, ps, kt, dqt, drow, dk, dv, dsort = refs[1 + steps :]
         g_masks = head_masks(1.0)
 
         def sort_in(s, carry):
@@ -690,6 +726,24 @@
                     for kind in range(3):
                         d_refs[step][base : base + blk, kind * SLOT : (kind + 1) * SLOT] = dsort[kind, there, :]
                     base += blk
+
+        if pieces:
+            for copy in copies:
+                copy.wait()
+            gains, shifts, at, index = 0.0, 0.0, 0, 0
+            for step, blocks in enumerate(normed):
+                terms = dot_nt(d_refs[step][...], w_ref[...])
+                shifts = shifts + jnp.sum(terms, axis=0, keepdims=True)
+                first = 0
+                for block in blocks:
+                    rows = block.shape[0]
+                    term = terms[first : first + rows]
+                    t_refs[index][...] = term.astype(BF16)
+                    values = held[at : at + rows, :].astype(F32)
+                    gains = gains + jnp.sum(term * values, axis=0, keepdims=True)
+                    first, at, index = first + rows, at + rows, index + 1
+            norm_ref[0:1, :] = gains
+            norm_ref[1:2, :] = shifts
 
     outs = [shape_of(8, SLOT, F32)]
     for entries in layout:
@@ -707,10 +761,20 @@
     ]
     args = [order, spot, queries, keys, values, grads, mixed, lse]
     ins = [SMEM_SPEC] * 2 + [VMEM_SPEC] * 6
-    result = local_call(
-        kernel, "attend_backward", outs, ins, args, 10 * seq * seq * SLOT, scratch, seq * seq
-    )
-    return list(result[1:]), result[0]
+    flops = 10 * seq * seq * SLOT
+    if pieces:
+        width = w_heads.shape[0]
+        args += [w_heads] + flat
+        ins += [VMEM_SPEC] + [ANY_SPEC] * pieces
+        outs += [shape_of(2, width, F32)] + [shape_of(block.shape[0], width, BF16) for block in flat]
+        scratch += [pltpu.VMEM((seq, width), BF16), pltpu.SemaphoreType.DMA((pieces,))]
+        flops += 6 * seq * width * SLOT
+    result = local_call(kernel, "attend_backward", outs, ins, args, flops, scratch, seq * seq)
+    terms, at = [], 2 + steps
+    for blocks in normed or []:
+        terms.append(list(result[at : at + len(blocks)]))
+        at += len(blocks)
+    return list(result[1 : 1 + steps]), result[0], terms, result[1 + steps] if pieces else None
 
 
 def body(
@@ -879,54 +943,61 @@
     grad_heads = lax.all_to_all(grad_slots, "context", 1, 0, tiled=True)
 
     g_out_steps = out_blocks(spot, after(attn_out, grad_slots), wide(grad_r16), layout, ring.size, grad_scale)
-    g_out_events = {}
-
-    def fill_out_grad(step, event):
-        g_out_events[step] = event
-        return ()
-
-    g_out = ring.scatter(lambda step, event: g_out_steps[step], fill_out_grad)[:own_rows]
-    g_w_out = pair_sum(g_out[:, :half], g_out[:, half:width], side)
-
-    out_events = {}
-
-    def give_out(step, event):
-        return [after(term, grad_o16) for term in out_terms[step]] if event is None else out_terms[step]
-
-    def fill_out(step, event):
-        out_events[step] = event
-        return ()
-
-    result = (resid_one + ring.scatter(give_out, fill_out)[:, :width] + proj_b).astype(BF16)
+    out_grad_ring = Scatter(ring, lambda step, event: g_out_steps[step])
+    out_grad_ring.hop()
+
+    out_ring = Scatter(ring, lambda step, event: out_terms[step])
+    out_ring.hop(grad_o16)
+    out_ring.hop()
 
     fc_sum = made["fc_sum"]
     fc_landed = spread(after(fc_sum, grad_heads))
-    grad_heads = after(grad_heads, out_events[far - 1], g_out_events[far])
-    d_steps, head_sums = attend_backward(order, spot, saved, grad_heads, mixed, lse, layout, blk)
-    norm_sums = []
+    grad_heads = after(grad_heads, out_ring.sent, out_grad_ring.sent, made["proj_got"])
+    fused = seq * width <= 4 * 1024 * 1024
+    d_steps, head_sums, h1_terms, h1_sums = attend_backward(
+        order, spot, saved, grad_heads, mixed, lse, layout, blk, *((w_heads, n_one) if fused else ())
+    )
+    norm_sums = [h1_sums] if fused else []
 
     def give_input(step, event):
+        if fused:
+            return h1_terms[step]
         event = made[2] if step == 0 else event
         grad = d_steps[step] if event is None else after(d_steps[step], event)
         sums, terms = input_blocks(grad, w_heads, n_one[step])
         norm_sums.append(sums)
         return terms
 
-    def fill_input(step, event):
-        made[step] = event
-        if step == far:
+    input_ring = Scatter(ring, give_input)
+    input_ring.hop(out_ring.got, out_grad_ring.got, fc_landed)
+    made[far] = input_ring.sent
+    out_ring.hop(input_ring.sent)
+    out_grad_ring.hop(input_ring.sent)
+    input_ring.hold(out_ring.sent, out_grad_ring.sent)
+    for step in range(far - 1, 1, -1):
+        input_ring.hop()
+        made[step] = event = input_ring.sent
+        if step == far - 1:
             flags = after(side, event).astype(jnp.int32).reshape(1)
-            made["qkv"] = weight_terms(flags, h_one, d_steps, grad_scale, count, own_rows, True)
-            return (made["qkv"][1], fc_landed)
-        return ()
-
-    grad_h1 = ring.scatter(give_input, fill_input)[:, :width]
+            keep, send = weight_terms(flags, h_one, d_steps, grad_scale, count, own_rows, True)
+            got = cross(send)
+            out_ring.hop(event)
+            input_ring.hold(send, out_ring.sent)
+        if step == far - 2:
+            out_grad_ring.hop(event)
+            input_ring.hold(out_grad_ring.sent)
+    input_ring.hop()
+    made[1] = input_ring.sent
+    qkv_sum = total([after(keep, made[1]), got]).astype(BF16)
+    out_grad_ring.hop(made[1])
+    grad_h1 = input_ring.finish()[:, :width]
     grad_x = (grad_r1 + norm_back(grad_h1, normed_one, inv_one, gain_one)).astype(BF16)
-    keep, send = made["qkv"]
-    qkv_sum = total([after(keep, made[far - 1]), cross(send)]).astype(BF16)
+    result = (resid_one + out_ring.finish()[:, :width] + proj_b).astype(BF16)
+    g_out = out_grad_ring.finish()[:own_rows]
+    g_w_out = pair_sum(g_out[:, :half], g_out[:, half:width], side)
     g_w_qkv = return_heads(spread(qkv_sum), side, count, own_rows, width)
-    g_w_proj = total([after(made["proj_keep"], made[2]), made["proj_got"]])
-    g_w_fc = return_fc(after(fc_landed, made[2]), side, count, own_rows)
+    g_w_proj = total([after(made["proj_keep"], made[1]), made["proj_got"]])
+    g_w_fc = return_fc(after(fc_landed, qkv_sum), side, count, own_rows)
 
     fc_place = lax.dynamic_update_slice(jnp.zeros((hidden,), F32), total(bias_sums)[0], (mine * share,))
     head_place = lax.dynamic_update_slice(
@@ -943,7 +1014,7 @@
             head_place.reshape(-1),
         ]
     )
-    sums = sum_everywhere(local.reshape(-1, SLOT) * grad_scale, count).reshape(-1)
+    sums = sum_everywhere(after(local, out_grad_ring.sent).reshape(-1, SLOT) * grad_scale, count).reshape(-1)
 
     def own_half(vector):
         return lax.dynamic_slice(vector, (side * (vector.shape[0] // 2),), (vector.shape[0] // 2,))

time: 562 us -> 538 us (0.957)
  the two profiles are of different devices: /device:TPU:0 before, /device:TPU:4 now
where the time goes in v4:
time: 538 us; the launch traced here: 528 us
  waiting for transfers between devices  133 us (25%)
  Pallas kernels  132 us (25%)
  starting transfers between devices  100 us (19%)
  other arithmetic  73.7 us (14%)
  local copies, waits for them, and re-layouts  65 us (12%)
  between operations  15.7 us (3%)
  matrix products  7.96 us (1%)
    pallas_call x16, Pallas kernels, local_call(): pl.pallas_call(kernel, out_shape=tuple(outs), in_specs=list(ins), out_spe...  132 us
    ppermute x28, waiting for transfers between devices, send(): return lax.ppermute(value, 'context', self.links)  53.9 us
    ppermute x14, waiting for transfers between devices, cross(): return lax.ppermute(value, 'fsdp', [(0, 1), (1, 0)])  30 us
    convert_element_type x16, other arithmetic, hop(): self.sent = value.astype(BF16)  27.5 us
    all_to_all x4, starting transfers between devices, spread(): return lax.all_to_all(value, 'context', 0, 0, tiled=True)  24.1 us
    ppermute x28, starting transfers between devices, send(): return lax.ppermute(value, 'context', self.links)  20.5 us
    ppermute x35, starting transfers between devices, swap(): return lax.ppermute(value, 'context', self.swaps)  19.2 us
    all_to_all x4, waiting for transfers between devices, spread(): return lax.all_to_all(value, 'context', 0, 0, tiled=True)  17.8 us
  transfers between devices with their start and end apart: 88, of which 38 were waited for; matrix products, arithmetic and copies ran while one was open for 20% of the time, Pallas kernels for 24%

profile of v4, /device:TPU:4, one launch (start us, length us, event | category | flops | bytes accessed | tf_op | source)
XLA Modules:
  0.0 527.9 jit_solution(133893612634259352)
XLA Ops:
  26.4 6.4 %all-to-all-start = ((bf16[16,150,128]{2,1,0:T(8,128)(2,1)}), bf16[16,150,128]{2,1,0:T(8,128)(2,1)S(1)}, u32[]{:S(2)}, u32[]{:S(2)}) async-start(bf16[16,150,128]{2,1,0:T(8,128)(2,1)} %copy.118), calls=%async_computation | async-start | bytes 1245184 | tf_op jit(solution)/shard_map/all_to_all | solution.py:215
  35.4 3.1 norm_blocks.5
  43.1 4.3 norm_blocks.6
  47.5 9.0 %collective-permute-done.6.refs_0_ = bf16[256,1664]{1,0:T(8,128)(2,1)} collective-permute-done((bf16[256,1664]{1,0:T(8,128)(2,1)}, bf16[256,1664]{1,0:T(8,128)(2,1)}, u32[]{:S(2)}, u32[]{:S(2)}) %collective-permute-start.6) | collective-permute-done | bytes 852000 | tf_op jit(solution)/shard_map/ppermute | solution.py:78
  61.5 4.4 norm_blocks.7
  65.9 6.2 %collective-permute-done.8.refs_0_ = bf16[256,1664]{1,0:T(8,128)(2,1)} collective-permute-done((bf16[256,1664]{1,0:T(8,128)(2,1)}, bf16[256,1664]{1,0:T(8,128)(2,1)}, u32[]{:S(2)}, u32[]{:S(2)}) %collective-permute-start.8) | collective-permute-done | bytes 852000 | tf_op jit(solution)/shard_map/ppermute | solution.py:78
  83.1 6.3 %all-to-all-start.1 = ((bf16[16,50,400]{2,1,0:T(8,128)(2,1)}), bf16[16,50,400]{2,1,0:T(8,128)(2,1)S(1)}, u32[]{:S(2)}, u32[]{:S(2)}) async-start(bf16[16,50,400]{2,1,0:T(8,128)(2,1)} %copy.122), calls=%async_computation.1 | async-start | bytes 1835008 | tf_op jit(solution)/shard_map/all_to_all | solution.py:215
  89.4 4.4 norm_blocks.8
  101.9 2.9 norm_blocks.9
  104.8 21.0 %attend_forward.1 = (bf16[2048,128]{1,0:T(8,128)(2,1)}, f32[4,8,512]{2,1,0:T(8,128)}, bf16[2,2048,128]{2,1,0:T(8,128)(2,1)}, bf16[2048,128]{1,0:T(8,128)(2,1)}, bf16[2048,128]{1,0:T(8,128)(2,1)}) custom-call(s32[32]{0:T(128)} %order_ref.1, s32[2]{0:T(128)} %pad_add_fusion.refs_1_.spot_ref, bf16[256,1664]{1,0:T(8,128)(2,1)} %get-tuple-element.151.refs_2_.refs_1_, ...), custom_call_target="tpu_custom_call" | custom-call | flops 4764729344 | bytes 10782344 | tf_op jit(solution)/shard_map/attend_forward/pallas_call | solution.py:293
  126.4 17.8 %all-to-all-done.1 = bf16[16,50,400]{2,1,0:T(8,128)(2,1)S(1)} async-done(((bf16[16,50,400]{2,1,0:T(8,128)(2,1)}), bf16[16,50,400]{2,1,0:T(8,128)(2,1)S(1)}, u32[]{:S(2)}, u32[]{:S(2)}) %all-to-all-start.1) | async-done | bytes 640032 | tf_op jit(solution)/shard_map/all_to_all | solution.py:215
  150.1 10.4 %all-to-all-start.2 = ((bf16[16,128,128]{1,2,0:T(8,128)(2,1)}), bf16[16,128,128]{1,2,0:T(8,128)(2,1)}, u32[]{:S(2)}, u32[]{:S(2)}) async-start(bf16[16,128,128]{1,2,0:T(8,128)(2,1)} %copy.124), calls=%async_computation.2 | async-start | bytes 1048576 | tf_op jit(solution)/shard_map/all_to_all | solution.py:889
  166.4 3.0 pad.69.refs_2_.refs_4_
  169.3 4.4 all-to-all-done.2
  174.7 6.1 %collective-permute-done.19.refs_2_.refs_5_ = bf16[256,1664]{1,0:T(8,128)(2,1)} collective-permute-done((bf16[256,1664]{1,0:T(8,128)(2,1)}, bf16[256,1664]{1,0:T(8,128)(2,1)}, u32[]{:S(2)}, u32[]{:S(2)}) %collective-permute-start.19) | collective-permute-done | bytes 852000 | tf_op jit(solution)/shard_map/ppermute | solution.py:78
  181.0 3.7 fusion.41
  190.5 4.1 collective-permute-start.23
  194.7 5.5 %feed_blocks.5 = (bf16[256,400]{1,0:T(8,128)(2,1)}, bf16[256,400]{1,0:T(8,128)(2,1)}, f32[1,400]{1,0:T(1,128)}, bf16[256,1664]{1,0:T(8,128)(2,1)}, bf16[256,1664]{1,0:T(8,128)(2,1)}) custom-call(bf16[256,1664]{1,0:T(8,128)(2,1)} %pad_maximum_fusion.4.refs_0_.refs_1_, bf16[256,1664]{1,0:T(8,128)(2,1)} %pad_maximum_fusion.3.refs_1_.refs_0_, ...), custom_call_target="tpu_custom_call" | custom-call | flops 1363148800 | bytes 6483072 | tf_op jit(solution)/shard_map/feed_blocks/pallas_call | solution.py:293
  200.1 3.4 collective-permute-done.21.refs_0_.refs_2_
  207.6 8.0 %feed_blocks.6 = (bf16[512,400]{1,0:T(8,128)(2,1)}, bf16[512,400]{1,0:T(8,128)(2,1)}, f32[1,400]{1,0:T(1,128)}, bf16[256,1664]{1,0:T(8,128)(2,1)}, bf16[256,1664...) custom-call(bf16[256,1664]{1,0:T(8,128)(2,1)} %collective-permute-done.21.refs_0_.refs_2_, ...), custom_call_target="tpu_custom_call" | custom-call | flops 2726297600 | bytes 10300544 | tf_op jit(solution)/shard_map/feed_blocks/pallas_call | solution.py:293
  221.0 8.0 %feed_blocks.7 = (bf16[512,400]{1,0:T(8,128)(2,1)}, bf16[512,400]{1,0:T(8,128)(2,1)}, f32[1,400]{1,0:T(1,128)}, bf16[256,1664]{1,0:T(8,128)(2,1)}, bf16[256,1664...) custom-call(bf16[256,1664]{1,0:T(8,128)(2,1)} %copy-done.68, bf16[256,1664]{1,0:T(8,128)(2,1)} %copy-done.69, ...), custom_call_target="tpu_custom_call" | custom-call | flops 2726297600 | bytes 10300544 | tf_op jit(solution)/shard_map/feed_blocks/pallas_call | solution.py:293
  233.0 6.0 %collective-permute-done.35.refs_2_.refs_7_ = bf16[128,1664]{1,0:T(8,128)(2,1)S(1)} collective-permute-done((bf16[128,1664]{1,0:T(8,128)(2,1)S(1)}, bf16[128,1664]{1,0:T(8,128)(2,1)S(1)}, u32[]{:S(2)}, u32[]{:S(2)}) %collective-permute-start.35) | collective-permute-done | bytes 426016 | tf_op jit(solution)/shard_map/ppermute | solution.py:78
  240.9 8.0 %feed_blocks.8 = (bf16[512,400]{1,0:T(8,128)(2,1)}, bf16[512,400]{1,0:T(8,128)(2,1)}, f32[1,400]{1,0:T(1,128)}, bf16[256,1664]{1,0:T(8,128)(2,1)}, bf16[256,1664...) custom-call(bf16[256,1664]{1,0:T(8,128)(2,1)} %copy-done.42, bf16[256,1664]{1,0:T(8,128)(2,1)} %copy-done.71, ...), custom_call_target="tpu_custom_call" | custom-call | flops 2726297600 | bytes 10300544 | tf_op jit(solution)/shard_map/feed_blocks/pallas_call | solution.py:293
  251.6 5.4 %feed_blocks.9 = (bf16[256,400]{1,0:T(8,128)(2,1)}, bf16[256,400]{1,0:T(8,128)(2,1)}, f32[1,400]{1,0:T(1,128)}, bf16[128,1664]{1,0:T(8,128)(2,1)}, bf16[128,1664...) custom-call(bf16[128,1664]{1,0:T(8,128)(2,1)} %copy-done.73, bf16[128,1664]{1,0:T(8,128)(2,1)} %copy-done.74, ...), custom_call_target="tpu_custom_call" | custom-call | flops 1363148800 | bytes 6483072 | tf_op jit(solution)/shard_map/feed_blocks/pallas_call | solution.py:293
  262.4 9.1 %weight_terms.2 = (bf16[16,50,400]{2,1,0:T(8,128)(2,1)}, bf16[16,50,400]{2,1,0:T(8,128)(2,1)}) custom-call(s32[1]{0:T(128)} %bitcast.13.refs_0_, bf16[256,1664]{1,0:T(8,128)(2,1)} %pad_maximum_fusion.4.refs_0_.refs_1_, bf16[256,1664]{1,0:T(8,128)(2,1)} %collective-permute-done.21.refs_0_.refs_2_, bf16[256,1664]{1,0:T(8,128)(2,1)} %copy-done.67, ...), custom_call_target="tpu_custom_call" | custom-call | flops 2726297600 | bytes 9734148 | tf_op jit(solution)/shard_map/weight_terms/pallas_call | solution.py:293
  277.3 8.7 %proj_terms.1 = f32[400,1664]{1,0:T(8,128)} custom-call(bf16[256,1664]{1,0:T(8,128)(2,1)} %pad_maximum_fusion.3.refs_1_.refs_0_, bf16[256,1664]{1,0:T(8,128)(2,1)} %collective-permute-done.16.refs_2_.refs_1_, bf16[256,1664]{1,0:T(8,128)(2,1)} %copy-done.11, bf16[256,1664]{1,0:T(8,128)(2,1)} %collective-permute-done.18.refs_2_.refs_3_, ...), custom_call_target="tpu_custom_call" | custom-call | flops 2726297600 | bytes 11116544 | tf_op jit(solution)/shard_map/proj_terms/pallas_call | solution.py:293
  290.8 6.5 %collective-permute-done.41 = bf16[16,50,400]{2,0,1:T(8,128)(2,1)} collective-permute-done((bf16[16,50,400]{2,0,1:T(8,128)(2,1)}, bf16[16,50,400]{2,0,1:T(8,128)(2,1)}, u32[]{:S(2)}, u32[]{:S(2)}) %collective-permute-start.41) | collective-permute-done | bytes 640032 | tf_op jit(solution)/shard_map/ppermute | solution.py:186
  302.5 12.8 %collective-permute-done.42 = bf16[256,1664]{1,0:T(8,128)(2,1)} collective-permute-done((bf16[256,1664]{1,0:T(8,128)(2,1)}, bf16[256,1664]{1,0:T(8,128)(2,1)}, u32[]{:S(2)}, u32[]{:S(2)}) %collective-permute-start.42) | collective-permute-done | bytes 852000 | tf_op jit(solution)/shard_map/ppermute | solution.py:78
  319.6 4.3 convolution_convert_fusion
  333.2 5.0 all-to-all-start.3
  339.2 5.3 %out_blocks.1 = (bf16[208,1664]{1,0:T(8,128)(2,1)}, bf16[208,1664]{1,0:T(8,128)(2,1)}, bf16[208,1664]{1,0:T(8,128)(2,1)}, bf16[208,1664]{1,0:T(8,128)(2,1)}, bf1...) custom-call(s32[2]{0:T(128)} %pad_add_fusion.refs_1_.spot_ref, ...), custom_call_target="tpu_custom_call" | custom-call | flops 708837376 | bytes 6389768 | tf_op jit(solution)/shard_map/out_blocks/pallas_call | solution.py:293
  348.5 2.7 all-to-all-done.3
  353.3 5.8 %all-to-all-start.4 = ((bf16[16,50,400]{2,1,0:T(8,128)(2,1)}), bf16[16,50,400]{2,1,0:T(8,128)(2,1)}, u32[]{:S(2)}, u32[]{:S(2)}) async-start(bf16[16,50,400]{2,1,0:T(8,128)(2,1)} %add_convert_fusion), calls=%async_computation.4 | async-start | bytes 1835008 | tf_op jit(solution)/shard_map/all_to_all | solution.py:215
  360.9 25.8 %attend_backward.1 = (f32[8,128]{1,0:T(8,128)}, bf16[256,384]{1,0:T(8,128)(2,1)}, bf16[512,384]{1,0:T(8,128)(2,1)}, bf16[512,384]{1,0:T(8,128)(2,1)}, bf16[512,3...) custom-call(s32[32]{0:T(128)} %order_ref.1, ...), custom_call_target="tpu_custom_call" | custom-call | flops 7985954816 | bytes 19711112 | tf_op jit(solution)/shard_map/attend_backward/pallas_call | solution.py:293
  404.7 8.5 %weight_terms.3 = (bf16[16,150,128]{2,1,0:T(8,128)(2,1)}, bf16[16,150,128]{2,1,0:T(8,128)(2,1)}) custom-call(s32[1]{0:T(128)} %bitcast.19.refs_0_, bf16[256,1664]{1,0:T(8,128)(2,1)} %get-tuple-element.151.refs_2_.refs_1_, bf16[256,1664]{1,0:T(8,128)(2,1)} %get-tuple-element.154.refs_3_.refs_2_, bf16[256,1664]{1,0:T(8,128)(2,1)} %get-tuple-element.155.refs_4_.refs_3_, ...), custom_call_target="tpu_custom_call" | custom-call | flops 2617245696 | bytes 9617412 | tf_op jit(solution)/shard_map/weight_terms/pallas_call | solution.py:293
  413.2 2.7 add_convert_fusion.3
  415.9 2.9 collective-permute-done.62
  418.9 2.7 add_convert_fusion.2
  423.6 3.3 slice_select_fusion
  431.8 2.6 add_convert_fusion.8
  435.9 2.7 add_convert_fusion.1
  440.1 5.0 collective-permute-done.75
  446.1 5.7 %all-to-all-start.5 = ((bf16[16,150,128]{2,1,0:T(8,128)(2,1)}), bf16[16,150,128]{2,1,0:T(8,128)(2,1)}, u32[]{:S(2)}, u32[]{:S(2)}) async-start(bf16[16,150,128]{2,1,0:T(8,128)(2,1)} %add_convert_fusion.9), calls=%async_computation.5 | async-start | bytes 1245184 | tf_op jit(solution)/shard_map/all_to_all | solution.py:215
  462.3 3.5 collective-permute-done.80
  468.2 2.9 reshape.161
  479.6 9.8 %collective-permute-done.73 = f32[150,128]{1,0:T(8,128)S(1)} collective-permute-done((f32[150,128]{1,0:T(8,128)S(1)}, f32[150,128]{1,0:T(8,128)S(1)}, u32[]{:S(2)}, u32[]{:S(2)}) %collective-permute-start.73) | collective-permute-done | bytes 76832 | tf_op jit(solution)/shard_map/ppermute | solution.py:202
  502.3 2.8 collective-permute-done.76
  514.2 4.5 collective-permute-done.79
  (476 shorter events, 204.9 us)
Async XLA Ops:
  24.2 15.5 %collective-permute-start.3 = (bf16[256,1664]{1,0:T(8,128)(2,1)S(1)}, bf16[256,1664]{1,0:T(8,128)(2,1)}, u32[]{:S(2)}, u32[]{:S(2)}) collective-permute-start(bf16[256,1664]{1,0:T(8,128)(2,1)S(1)} %pad_maximum_fusion.2.refs_0_), channel_id=1, source_target_pairs={{0,4},{1,3},{4,8},{5,1},{8,12},{9,5},{12,14},{13,9},{14,10},{15,13... | collective-permute-start | bytes 2555912 | tf_op jit(solution)/shard_map/ppermute | solution.py:78
  26.4 30.0 %all-to-all-start = ((bf16[16,150,128]{2,1,0:T(8,128)(2,1)}), bf16[16,150,128]{2,1,0:T(8,128)(2,1)S(1)}, u32[]{:S(2)}, u32[]{:S(2)}) async-start(bf16[16,150,128]{2,1,0:T(8,128)(2,1)} %copy.118), calls=%async_computation | async-start | bytes 1245184 | tf_op jit(solution)/shard_map/all_to_all | solution.py:215
  32.8 148.2 %all-gather.2.cloned.1.call-start = ((), (), s32[]{:S(2)}) async-start(), calls=%async_computation.6 | async-start | bytes 5883904 | tf_op jit(solution)/shard_map/all_gather | solution.py:873
  39.7 16.8 %collective-permute-start.6 = (bf16[256,1664]{1,0:T(8,128)(2,1)}, bf16[256,1664]{1,0:T(8,128)(2,1)}, u32[]{:S(2)}, u32[]{:S(2)}) collective-permute-start(bf16[256,1664]{1,0:T(8,128)(2,1)} %collective-permute-done.3.refs_0_), channel_id=1, source_target_pairs={{0,4},{1,3},{4,8},{5,1},{8,12},{9,5},{12,14},{13,9},{14,10},{15,13... | collective-permute-start | bytes 2555912 | tf_op jit(solution)/shard_map/ppermute | solution.py:78
  40.5 16.0 %collective-permute-start.10 = (bf16[50,3200]{1,0:T(8,128)(2,1)}, bf16[50,3200]{1,0:T(8,128)(2,1)}, u32[]{:S(2)}, u32[]{:S(2)}) collective-permute-start(bf16[50,3200]{1,0:T(8,128)(2,1)} %slice.190), channel_id=1, source_target_pairs={{0,16},{16,0},{1,17},{17,1},{2,18},{18,2},{3,19},{19,3},{4,20},{20... | collective-permute-start | bytes 960008 | tf_op jit(solution)/shard_map/ppermute | solution.py:186
  56.4 15.6 %collective-permute-start.8 = (bf16[256,1664]{1,0:T(8,128)(2,1)}, bf16[256,1664]{1,0:T(8,128)(2,1)}, u32[]{:S(2)}, u32[]{:S(2)}) collective-permute-start(bf16[256,1664]{1,0:T(8,128)(2,1)} %collective-permute-done.6.refs_0_), channel_id=1, source_target_pairs={{0,4},{1,3},{4,8},{5,1},{8,12},{9,5},{12,14},{13,9},{14,10},{15,13... | collective-permute-start | bytes 2555912 | tf_op jit(solution)/shard_map/ppermute | solution.py:78
  58.4 15.4 %collective-permute-start.11 = (bf16[16,150,128]{2,0,1:T(8,128)(2,1)}, bf16[16,150,128]{2,0,1:T(8,128)(2,1)}, u32[]{:S(2)}, u32[]{:S(2)}) collective-permute-start(bf16[16,150,128]{2,0,1:T(8,128)(2,1)} %copy.119), channel_id=1, source_target_pairs={{0,16},{16,0},{1,17},{17,1},{2,18},{18,2},{3,19},{19,3},{4,20},{20... | collective-permute-start | bytes 1843208 | tf_op jit(solution)/shard_map/ppermute | solution.py:186
  73.9 15.5 %collective-permute-start.9 = (bf16[256,1664]{1,0:T(8,128)(2,1)}, bf16[256,1664]{1,0:T(8,128)(2,1)}, u32[]{:S(2)}, u32[]{:S(2)}) collective-permute-start(bf16[256,1664]{1,0:T(8,128)(2,1)} %collective-permute-done.8.refs_0_), channel_id=1, source_target_pairs={{0,1},{1,0},{2,3},{3,2},{4,5},{5,4},{6,7},{7,6},{8,9},{9,8},{10,11... | collective-permute-start | bytes 2555912 | tf_op jit(solution)/shard_map/ppermute | solution.py:75
  76.0 17.8 %collective-permute-start.12 = (bf16[128,1664]{1,0:T(8,128)(2,1)}, bf16[128,1664]{1,0:T(8,128)(2,1)}, u32[]{:S(2)}, u32[]{:S(2)}) collective-permute-start(bf16[128,1664]{1,0:T(8,128)(2,1)} %constant_dynamic-slice_fusion.2), channel_id=1, source_target_pairs={{0,4},{1,3},{4,8},{5,1},{8,12},{9,5},{12,14},{13,9},{14,10},{15,13... | collective-permute-start | bytes 1277960 | tf_op jit(solution)/shard_map/ppermute | solution.py:78
  79.2 46.6 %collective-permute-start.16 = (bf16[256,1664]{1,0:T(8,128)(2,1)}, bf16[256,1664]{1,0:T(8,128)(2,1)}, u32[]{:S(2)}, u32[]{:S(2)}) collective-permute-start(bf16[256,1664]{1,0:T(8,128)(2,1)} %pad_maximum_fusion.3.refs_1_.refs_0_), channel_id=1, source_target_pairs={{0,4},{1,3},{4,8},{5,1},{8,12},{9,5},{12,14},{13,9},{14,10},{15,13... | collective-permute-start | bytes 2555912 | tf_op jit(solution)/shard_map/ppermute | solution.py:78
  83.1 61.1 %all-to-all-start.1 = ((bf16[16,50,400]{2,1,0:T(8,128)(2,1)}), bf16[16,50,400]{2,1,0:T(8,128)(2,1)S(1)}, u32[]{:S(2)}, u32[]{:S(2)}) async-start(bf16[16,50,400]{2,1,0:T(8,128)(2,1)} %copy.122), calls=%async_computation.1 | async-start | bytes 1835008 | tf_op jit(solution)/shard_map/all_to_all | solution.py:215
  99.4 26.9 %collective-permute-start.14 = (bf16[400,800]{1,0:T(8,128)(2,1)S(1)}, bf16[400,800]{1,0:T(8,128)(2,1)S(1)}, u32[]{:S(2)}, u32[]{:S(2)}) collective-permute-start(bf16[400,800]{1,0:T(8,128)(2,1)S(1)} %copy-done.29), channel_id=1, source_target_pairs={{0,16},{16,0},{1,17},{17,1},{2,18},{18,2},{3,19},{19,3},{4,20},{20... | collective-permute-start | bytes 1920008 | tf_op jit(solution)/shard_map/ppermute | solution.py:186
  125.9 34.7 %collective-permute-start.18 = (bf16[256,1664]{1,0:T(8,128)(2,1)}, bf16[256,1664]{1,0:T(8,128)(2,1)}, u32[]{:S(2)}, u32[]{:S(2)}) collective-permute-start(bf16[256,1664]{1,0:T(8,128)(2,1)} %collective-permute-done.16.refs_2_.refs_1_), channel_id=1, source_target_pairs={{0,4},{1,3},{4,8},{5,1},{8,12},{9,5},{12,14},{13,9},{14,10},{15,13... | collective-permute-start | bytes 2555912 | tf_op jit(solution)/shard_map/ppermute | solution.py:78
  145.3 17.3 %collective-permute-start.17 = (bf16[16,50,400]{2,0,1:T(8,128)(2,1)}, bf16[16,50,400]{2,0,1:T(8,128)(2,1)}, u32[]{:S(2)}, u32[]{:S(2)}) collective-permute-start(bf16[16,50,400]{2,0,1:T(8,128)(2,1)} %copy.125), channel_id=1, source_target_pairs={{0,16},{16,0},{1,17},{17,1},{2,18},{18,2},{3,19},{19,3},{4,20},{20... | collective-permute-start | bytes 1920008 | tf_op jit(solution)/shard_map/ppermute | solution.py:186
  150.1 23.6 %all-to-all-start.2 = ((bf16[16,128,128]{1,2,0:T(8,128)(2,1)}), bf16[16,128,128]{1,2,0:T(8,128)(2,1)}, u32[]{:S(2)}, u32[]{:S(2)}) async-start(bf16[16,128,128]{1,2,0:T(8,128)(2,1)} %copy.124), calls=%async_computation.2 | async-start | bytes 1048576 | tf_op jit(solution)/shard_map/all_to_all | solution.py:889
  160.6 20.3 %collective-permute-start.19 = (bf16[256,1664]{1,0:T(8,128)(2,1)}, bf16[256,1664]{1,0:T(8,128)(2,1)}, u32[]{:S(2)}, u32[]{:S(2)}) collective-permute-start(bf16[256,1664]{1,0:T(8,128)(2,1)} %collective-permute-done.18.refs_2_.refs_3_), channel_id=1, source_target_pairs={{0,4},{1,3},{4,8},{5,1},{8,12},{9,5},{12,14},{13,9},{14,10},{15,13... | collective-permute-start | bytes 2555912 | tf_op jit(solution)/shard_map/ppermute | solution.py:78
  188.2 15.3 %collective-permute-start.21 = (bf16[256,1664]{1,0:T(8,128)(2,1)}, bf16[256,1664]{1,0:T(8,128)(2,1)}, u32[]{:S(2)}, u32[]{:S(2)}) collective-permute-start(bf16[256,1664]{1,0:T(8,128)(2,1)} %pad_maximum_fusion.4.refs_0_.refs_1_), channel_id=1, source_target_pairs={{0,4},{1,3},{4,8},{5,1},{8,12},{9,5},{12,14},{13,9},{14,10},{15,13... | collective-permute-start | bytes 2555912 | tf_op jit(solution)/shard_map/ppermute | solution.py:78
  190.5 15.2 %collective-permute-start.23 = (bf16[256,1664]{1,0:T(8,128)(2,1)}, bf16[256,1664]{1,0:T(8,128)(2,1)S(1)}, u32[]{:S(2)}, u32[]{:S(2)}) collective-permute-start(bf16[256,1664]{1,0:T(8,128)(2,1)} %collective-permute-done.16.refs_2_.refs_1_), channel_id=1, source_target_pairs={{0,1},{1,0},{2,3},{3,2},{4,5},{5,4},{6,7},{7,6},{8,9},{9,8},{10,11... | collective-permute-start | bytes 2555912 | tf_op jit(solution)/shard_map/ppermute | solution.py:75
  203.5 15.5 %collective-permute-start.27 = (bf16[256,1664]{1,0:T(8,128)(2,1)}, bf16[256,1664]{1,0:T(8,128)(2,1)S(1)}, u32[]{:S(2)}, u32[]{:S(2)}) collective-permute-start(bf16[256,1664]{1,0:T(8,128)(2,1)} %collective-permute-done.18.refs_2_.refs_3_), channel_id=1, source_target_pairs={{0,1},{1,0},{2,3},{3,2},{4,5},{5,4},{6,7},{7,6},{8,9},{9,8},{10,11... | collective-permute-start | bytes 2555912 | tf_op jit(solution)/shard_map/ppermute | solution.py:75
  216.4 13.1 %collective-permute-start.29 = (bf16[256,1664]{1,0:T(8,128)(2,1)S(1)}, bf16[256,1664]{1,0:T(8,128)(2,1)S(1)}, u32[]{:S(2)}, u32[]{:S(2)}) collective-permute-start(bf16[256,1664]{1,0:T(8,128)(2,1)S(1)} %collective-permute-done.25.refs_0_.refs_4_), channel_id=1, source_target_pairs={{0,4},{1,3},{4,8},{5,1},{8,12},{9,5},{12,14},{13,9},{14,10},{15,13... | collective-permute-start | bytes 2555912 | tf_op jit(solution)/shard_map/ppermute | solution.py:78
  216.8 22.2 %collective-permute-start.31 = (bf16[256,1664]{1,0:T(8,128)(2,1)}, bf16[256,1664]{1,0:T(8,128)(2,1)S(1)}, u32[]{:S(2)}, u32[]{:S(2)}) collective-permute-start(bf16[256,1664]{1,0:T(8,128)(2,1)} %collective-permute-done.19.refs_2_.refs_5_), channel_id=1, source_target_pairs={{0,1},{1,0},{2,3},{3,2},{4,5},{5,4},{6,7},{7,6},{8,9},{9,8},{10,11... | collective-permute-start | bytes 2555912 | tf_op jit(solution)/shard_map/ppermute | solution.py:75
  231.0 17.9 %collective-permute-start.33 = (bf16[128,1664]{1,0:T(8,128)(2,1)S(1)}, bf16[128,1664]{1,0:T(8,128)(2,1)S(1)}, u32[]{:S(2)}, u32[]{:S(2)}) collective-permute-start(bf16[128,1664]{1,0:T(8,128)(2,1)S(1)} %constant_dynamic-slice_fusion.1), channel_id=1, source_target_pairs={{0,4},{1,3},{4,8},{5,1},{8,12},{9,5},{12,14},{13,9},{14,10},{15,13... | collective-permute-start | bytes 1277960 | tf_op jit(solution)/shard_map/ppermute | solution.py:78
  260.3 13.1 %collective-permute-start.32 = (bf16[256,1664]{1,0:T(8,128)(2,1)}, bf16[256,1664]{1,0:T(8,128)(2,1)}, u32[]{:S(2)}, u32[]{:S(2)}) collective-permute-start(bf16[256,1664]{1,0:T(8,128)(2,1)} %get-tuple-element.194), channel_id=1, source_target_pairs={{0,1},{1,0},{2,3},{3,2},{4,5},{5,4},{6,7},{7,6},{8,9},{9,8},{10,11... | collective-permute-start | bytes 2555912 | tf_op jit(solution)/shard_map/ppermute | solution.py:75
  276.4 20.8 %collective-permute-start.41 = (bf16[16,50,400]{2,0,1:T(8,128)(2,1)}, bf16[16,50,400]{2,0,1:T(8,128)(2,1)}, u32[]{:S(2)}, u32[]{:S(2)}) collective-permute-start(bf16[16,50,400]{2,0,1:T(8,128)(2,1)} %copy.131), channel_id=1, source_target_pairs={{0,16},{16,0},{1,17},{17,1},{2,18},{18,2},{3,19},{19,3},{4,20},{20... | collective-permute-start | bytes 1920008 | tf_op jit(solution)/shard_map/ppermute | solution.py:186
  302.1 13.2 %collective-permute-start.42 = (bf16[256,1664]{1,0:T(8,128)(2,1)}, bf16[256,1664]{1,0:T(8,128)(2,1)}, u32[]{:S(2)}, u32[]{:S(2)}) collective-permute-start(bf16[256,1664]{1,0:T(8,128)(2,1)} %add_convert_fusion.5), channel_id=1, source_target_pairs={{0,4},{1,3},{4,8},{5,1},{8,12},{9,5},{12,14},{13,9},{14,10},{15,13... | collective-permute-start | bytes 2555912 | tf_op jit(solution)/shard_map/ppermute | solution.py:78
  329.9 14.8 %collective-permute-start.46 = (bf16[128,1664]{1,0:T(8,128)(2,1)}, bf16[128,1664]{1,0:T(8,128)(2,1)}, u32[]{:S(2)}, u32[]{:S(2)}) collective-permute-start(bf16[128,1664]{1,0:T(8,128)(2,1)} %add_convert_fusion.11), channel_id=1, source_target_pairs={{0,4},{1,3},{4,8},{5,1},{8,12},{9,5},{12,14},{13,9},{14,10},{15,13... | collective-permute-start | bytes 1277960 | tf_op jit(solution)/shard_map/ppermute | solution.py:78
  330.0 15.8 %collective-permute-start.44 = (bf16[256,1664]{1,0:T(8,128)(2,1)}, bf16[256,1664]{1,0:T(8,128)(2,1)}, u32[]{:S(2)}, u32[]{:S(2)}) collective-permute-start(bf16[256,1664]{1,0:T(8,128)(2,1)} %get-tuple-element.219), channel_id=1, source_target_pairs={{0,1},{1,0},{2,3},{3,2},{4,5},{5,4},{6,7},{7,6},{8,9},{9,8},{10,11... | collective-permute-start | bytes 2555912 | tf_op jit(solution)/shard_map/ppermute | solution.py:75
  330.7 30.2 %collective-permute-start.48 = (bf16[400,800]{1,0:T(8,128)(2,1)}, bf16[400,800]{1,0:T(8,128)(2,1)}, u32[]{:S(2)}, u32[]{:S(2)}) collective-permute-start(bf16[400,800]{1,0:T(8,128)(2,1)} %select_convert_fusion), channel_id=1, source_target_pairs={{0,16},{16,0},{1,17},{17,1},{2,18},{18,2},{3,19},{19,3},{4,20},{20... | collective-permute-start | bytes 1920008 | tf_op jit(solution)/shard_map/ppermute | solution.py:186
  333.2 18.1 %all-to-all-start.3 = ((bf16[128,16,128]{0,2,1:T(8,128)(2,1)}), bf16[128,16,128]{0,2,1:T(8,128)(2,1)}, u32[]{:S(2)}, u32[]{:S(2)}) async-start(bf16[128,16,128]{0,2,1:T(8,128)(2,1)} %bitcast.86), calls=%async_computation.3 | async-start | bytes 1048576 | tf_op jit(solution)/shard_map/all_to_all | solution.py:943
  344.5 14.6 %collective-permute-start.47 = (bf16[104,1664]{1,0:T(8,128)(2,1)}, bf16[104,1664]{1,0:T(8,128)(2,1)}, u32[]{:S(2)}, u32[]{:S(2)}) collective-permute-start(bf16[104,1664]{1,0:T(8,128)(2,1)} %get-tuple-element.226), channel_id=1, source_target_pairs={{0,1},{1,0},{2,3},{3,2},{4,5},{5,4},{6,7},{7,6},{8,9},{9,8},{10,11... | collective-permute-start | bytes 1038344 | tf_op jit(solution)/shard_map/ppermute | solution.py:75
  348.2 38.4 %collective-permute-start.50 = (bf16[256,1664]{1,0:T(8,128)(2,1)}, bf16[256,1664]{1,0:T(8,128)(2,1)S(1)}, u32[]{:S(2)}, u32[]{:S(2)}) collective-permute-start(bf16[256,1664]{1,0:T(8,128)(2,1)} %fusion.4), channel_id=1, source_target_pairs={{0,4},{1,3},{4,8},{5,1},{8,12},{9,5},{12,14},{13,9},{14,10},{15,13... | collective-permute-start | bytes 2555912 | tf_op jit(solution)/shard_map/ppermute | solution.py:78
  353.3 33.4 %all-to-all-start.4 = ((bf16[16,50,400]{2,1,0:T(8,128)(2,1)}), bf16[16,50,400]{2,1,0:T(8,128)(2,1)}, u32[]{:S(2)}, u32[]{:S(2)}) async-start(bf16[16,50,400]{2,1,0:T(8,128)(2,1)} %add_convert_fusion), calls=%async_computation.4 | async-start | bytes 1835008 | tf_op jit(solution)/shard_map/all_to_all | solution.py:215
  360.1 26.5 %collective-permute-start.51 = (bf16[104,1664]{1,0:T(8,128)(2,1)S(1)}, bf16[104,1664]{1,0:T(8,128)(2,1)S(1)}, u32[]{:S(2)}, u32[]{:S(2)}) collective-permute-start(bf16[104,1664]{1,0:T(8,128)(2,1)S(1)} %add_convert_fusion.14), channel_id=1, source_target_pairs={{0,4},{1,3},{4,8},{5,1},{8,12},{9,5},{12,14},{13,9},{14,10},{15,13... | collective-permute-start | bytes 1038344 | tf_op jit(solution)/shard_map/ppermute | solution.py:78
  396.7 16.5 %collective-permute-start.57 = (bf16[256,1664]{1,0:T(8,128)(2,1)}, bf16[256,1664]{1,0:T(8,128)(2,1)}, u32[]{:S(2)}, u32[]{:S(2)}) collective-permute-start(bf16[256,1664]{1,0:T(8,128)(2,1)} %add_convert_fusion.4), channel_id=1, source_target_pairs={{0,4},{1,3},{4,8},{5,1},{8,12},{9,5},{12,14},{13,9},{14,10},{15,13... | collective-permute-start | bytes 2555912 | tf_op jit(solution)/shard_map/ppermute | solution.py:78
  401.6 17.2 %collective-permute-start.61 = (bf16[256,1664]{1,0:T(8,128)(2,1)}, bf16[256,1664]{1,0:T(8,128)(2,1)}, u32[]{:S(2)}, u32[]{:S(2)}) collective-permute-start(bf16[256,1664]{1,0:T(8,128)(2,1)} %get-tuple-element.261), channel_id=1, source_target_pairs={{0,1},{1,0},{2,3},{3,2},{4,5},{5,4},{6,7},{7,6},{8,9},{9,8},{10,11... | collective-permute-start | bytes 2555912 | tf_op jit(solution)/shard_map/ppermute | solution.py:75
  402.2 16.7 %collective-permute-start.62 = (bf16[256,1664]{1,0:T(8,128)(2,1)}, bf16[256,1664]{1,0:T(8,128)(2,1)}, u32[]{:S(2)}, u32[]{:S(2)}) collective-permute-start(bf16[256,1664]{1,0:T(8,128)(2,1)} %fusion.5), channel_id=1, source_target_pairs={{0,4},{1,3},{4,8},{5,1},{8,12},{9,5},{12,14},{13,9},{14,10},{15,13... | collective-permute-start | bytes 2555912 | tf_op jit(solution)/shard_map/ppermute | solution.py:78
  403.0 27.3 %collective-permute-start.65 = (bf16[208,1664]{1,0:T(8,128)(2,1)}, bf16[208,1664]{1,0:T(8,128)(2,1)}, u32[]{:S(2)}, u32[]{:S(2)}) collective-permute-start(bf16[208,1664]{1,0:T(8,128)(2,1)} %fusion.6), channel_id=1, source_target_pairs={{0,4},{1,3},{4,8},{5,1},{8,12},{9,5},{12,14},{13,9},{14,10},{15,13... | collective-permute-start | bytes 2076680 | tf_op jit(solution)/shard_map/ppermute | solution.py:78
  422.0 13.9 %collective-permute-start.60 = (bf16[256,1664]{1,0:T(8,128)(2,1)}, bf16[256,1664]{1,0:T(8,128)(2,1)}, u32[]{:S(2)}, u32[]{:S(2)}) collective-permute-start(bf16[256,1664]{1,0:T(8,128)(2,1)} %get-tuple-element.259), channel_id=1, source_target_pairs={{0,1},{1,0},{2,3},{3,2},{4,5},{5,4},{6,7},{7,6},{8,9},{9,8},{10,11... | collective-permute-start | bytes 2555912 | tf_op jit(solution)/shard_map/ppermute | solution.py:75
  422.5 13.4 %collective-permute-start.63 = (bf16[256,1664]{1,0:T(8,128)(2,1)}, bf16[256,1664]{1,0:T(8,128)(2,1)}, u32[]{:S(2)}, u32[]{:S(2)}) collective-permute-start(bf16[256,1664]{1,0:T(8,128)(2,1)} %add_convert_fusion.2), channel_id=1, source_target_pairs={{0,4},{1,3},{4,8},{5,1},{8,12},{9,5},{12,14},{13,9},{14,10},{15,13... | collective-permute-start | bytes 2555912 | tf_op jit(solution)/shard_map/ppermute | solution.py:78
  429.1 16.0 %collective-permute-start.75 = (bf16[16,150,128]{2,0,1:T(8,128)(2,1)S(1)}, bf16[16,150,128]{2,0,1:T(8,128)(2,1)S(1)}, u32[]{:S(2)}, u32[]{:S(2)}) collective-permute-start(bf16[16,150,128]{2,0,1:T(8,128)(2,1)S(1)} %copy.136), channel_id=1, source_target_pairs={{0,16},{16,0},{1,17},{17,1},{2,18},{18,2},{3,19},{19,3},{4,20},{20... | collective-permute-start | bytes 1843208 | tf_op jit(solution)/shard_map/ppermute | solution.py:186
  430.3 24.1 %collective-permute-start.58 = (bf16[256,1664]{1,0:T(8,128)(2,1)}, bf16[256,1664]{1,0:T(8,128)(2,1)}, u32[]{:S(2)}, u32[]{:S(2)}) collective-permute-start(bf16[256,1664]{1,0:T(8,128)(2,1)} %add_convert_fusion.3), channel_id=1, source_target_pairs={{0,4},{1,3},{4,8},{5,1},{8,12},{9,5},{12,14},{13,9},{14,10},{15,13... | collective-permute-start | bytes 2555912 | tf_op jit(solution)/shard_map/ppermute | solution.py:78
  434.4 22.0 %collective-permute-start.69 = (bf16[208,1664]{1,0:T(8,128)(2,1)}, bf16[208,1664]{1,0:T(8,128)(2,1)}, u32[]{:S(2)}, u32[]{:S(2)}) collective-permute-start(bf16[208,1664]{1,0:T(8,128)(2,1)} %add_convert_fusion.8), channel_id=1, source_target_pairs={{0,4},{1,3},{4,8},{5,1},{8,12},{9,5},{12,14},{13,9},{14,10},{15,13... | collective-permute-start | bytes 2076680 | tf_op jit(solution)/shard_map/ppermute | solution.py:78
  438.7 39.4 %collective-permute-start.66 = (bf16[256,1664]{1,0:T(8,128)(2,1)}, bf16[256,1664]{1,0:T(8,128)(2,1)}, u32[]{:S(2)}, u32[]{:S(2)}) collective-permute-start(bf16[256,1664]{1,0:T(8,128)(2,1)} %add_convert_fusion.1), channel_id=1, source_target_pairs={{0,4},{1,3},{4,8},{5,1},{8,12},{9,5},{12,14},{13,9},{14,10},{15,13... | collective-permute-start | bytes 2555912 | tf_op jit(solution)/shard_map/ppermute | solution.py:78
  446.1 52.7 %all-to-all-start.5 = ((bf16[16,150,128]{2,1,0:T(8,128)(2,1)}), bf16[16,150,128]{2,1,0:T(8,128)(2,1)}, u32[]{:S(2)}, u32[]{:S(2)}) async-start(bf16[16,150,128]{2,1,0:T(8,128)(2,1)} %add_convert_fusion.9), calls=%async_computation.5 | async-start | bytes 1245184 | tf_op jit(solution)/shard_map/all_to_all | solution.py:215
  455.9 16.8 %collective-permute-start.59 = (bf16[128,1664]{1,0:T(8,128)(2,1)S(1)}, bf16[128,1664]{1,0:T(8,128)(2,1)}, u32[]{:S(2)}, u32[]{:S(2)}) collective-permute-start(bf16[128,1664]{1,0:T(8,128)(2,1)S(1)} %dynamic-slice_convert_fusion.1), channel_id=1, source_target_pairs={{0,1},{1,0},{2,3},{3,2},{4,5},{5,4},{6,7},{7,6},{8,9},{9,8},{10,11... | collective-permute-start | bytes 1277960 | tf_op jit(solution)/shard_map/ppermute | solution.py:75
  475.0 31.9 %collective-permute-start.77 = (bf16[208,1664]{1,0:T(8,128)(2,1)}, bf16[208,1664]{1,0:T(8,128)(2,1)}, u32[]{:S(2)}, u32[]{:S(2)}) collective-permute-start(bf16[208,1664]{1,0:T(8,128)(2,1)} %add_convert_fusion.7), channel_id=1, source_target_pairs={{0,4},{1,3},{4,8},{5,1},{8,12},{9,5},{12,14},{13,9},{14,10},{15,13... | collective-permute-start | bytes 2076680 | tf_op jit(solution)/shard_map/ppermute | solution.py:78
  475.8 13.6 %collective-permute-start.73 = (f32[150,128]{1,0:T(8,128)S(1)}, f32[150,128]{1,0:T(8,128)S(1)}, u32[]{:S(2)}, u32[]{:S(2)}) collective-permute-start(f32[150,128]{1,0:T(8,128)S(1)} %add.346), channel_id=1, source_target_pairs={{0,8},{1,9},{2,10},{3,11},{4,12},{5,13},{6,14},{7,15},{8,0},{9,1},... | collective-permute-start | bytes 230408 | tf_op jit(solution)/shard_map/ppermute | solution.py:202
  491.4 15.1 %collective-permute-start.67 = (bf16[128,1664]{1,0:T(8,128)(2,1)}, bf16[128,1664]{1,0:T(8,128)(2,1)S(1)}, u32[]{:S(2)}, u32[]{:S(2)}) collective-permute-start(bf16[128,1664]{1,0:T(8,128)(2,1)} %dynamic-slice_convert_fusion), channel_id=1, source_target_pairs={{0,1},{1,0},{2,3},{3,2},{4,5},{5,4},{6,7},{7,6},{8,9},{9,8},{10,11... | collective-permute-start | bytes 1277960 | tf_op jit(solution)/shard_map/ppermute | solution.py:75
  (115 other events, 606.9 us)
Sparse Core Ops, SparseCore 0:
  74.0 76.6 all-gather.1
